TPU v7x, 32 devices: a whole 2x2x4 slice. The times are simulated.
32 devices in a mesh: member: 16 (over z, y, x), pair: 2 (over core).
Axes of the slice: x: 2, y: 2, z: 4, core: 2. Of those that a mesh axis runs over, the one named last changes fastest.
Arguments:
- samples: bfloat16 [512, 512], replicated, may hold values from -6 to 6
- w_first: bfloat16 [16, 512, 2048], P('member', None, 'pair'), may hold values from -6 to 6
- b_first: bfloat16 [16, 2048], P('member', 'pair'), may hold values from -6 to 6
- w_second: bfloat16 [16, 2048, 2048], P('member', None, 'pair'), may hold values from -6 to 6
- b_second: bfloat16 [16, 2048], P('member', 'pair'), may hold values from -6 to 6
- w_third: bfloat16 [16, 2048, 64], P('member', 'pair'), may hold values from -6 to 6
- observed: float32 [512, 64], replicated, may hold values from -24 to 24
- perturb: float32 [16, 512, 64], P('member'), may hold values from -6 to 6
- variance: float32 [512, 64], replicated, may hold values from 32 to 1024
Outputs:
- new_first: bfloat16 [16, 512, 2048], P('member', None, 'pair')
- new_bfirst: bfloat16 [16, 2048], P('member', 'pair')
- new_second: bfloat16 [16, 2048, 2048], P('member', None, 'pair')
- new_bsecond: bfloat16 [16, 2048], P('member', 'pair')
- new_third: bfloat16 [16, 2048, 64], P('member', 'pair')
All inputs are finite; a program needn't handle non-finite values.
Results may differ from a plain program's by a relative error of at most 0.019.
Values may be sent and summed in bfloat16 or wider, within the bound.
No kernel may reach another device: no remote copies, remote signals or barrier semaphores. Data moves between devices by JAX's collectives and lax.ppermute only.
A program may use at most 128 MiB of HBM per device.

v0:
```python
import jax
import jax.numpy as jnp
from jax import lax
from jax.sharding import PartitionSpec as P


def solve_gain(amat, bmat):
    count = amat.shape[0]
    system = amat + count * jnp.eye(count, dtype=jnp.float32)
    factor = jnp.linalg.cholesky(system)
    middle = lax.linalg.triangular_solve(
        factor, bmat, left_side=True, lower=True, transpose_a=False
    )
    return lax.linalg.triangular_solve(factor, middle, left_side=True, lower=True, transpose_a=True)


def moments(allpred, allres, var_cols):
    devpred = allpred - jnp.mean(allpred, axis=0, keepdims=True)
    scaled = devpred / var_cols
    amat = jnp.dot(scaled, devpred.T, precision=lax.Precision.HIGHEST)
    bmat = jnp.dot(scaled, allres.T, precision=lax.Precision.HIGHEST)
    return (amat, bmat)


def to_slabs(shards):
    flats = [piece.reshape(1, -1) for piece in shards]
    return (
        lax.all_to_all(flats[0], "member", split_axis=1, concat_axis=0, tiled=True),
        lax.all_to_all(flats[1], "member", split_axis=1, concat_axis=0, tiled=True),
        lax.all_to_all(flats[2], "member", split_axis=1, concat_axis=0, tiled=True),
        lax.all_to_all(flats[3], "member", split_axis=1, concat_axis=0, tiled=True),
        lax.all_to_all(flats[4], "member", split_axis=1, concat_axis=0, tiled=True),
    )


def mix_slab(slab, gain_tr):
    full = slab.astype(jnp.float32)
    center = (full - jnp.mean(full, axis=0, keepdims=True)).astype(jnp.bfloat16)
    return jnp.dot(gain_tr, center, preferred_element_type=jnp.float32).astype(jnp.bfloat16)


def body(samples, w_first, b_first, w_second, b_second, w_third, observed, perturb, variance):
    shards = (w_first, b_first, w_second, b_second, w_third)
    in_scale = samples.shape[1] ** (-0.5)
    hid_scale = w_second.shape[1] ** (-0.5)
    first = jax.nn.gelu(
        jnp.dot(samples, w_first[0], preferred_element_type=jnp.float32) * in_scale
        + b_first[0].astype(jnp.float32),
        approximate=True,
    ).astype(jnp.bfloat16)
    second_w = w_second[0]
    summed = jnp.dot(
        lax.all_gather(first, "pair", axis=1, tiled=True),
        second_w,
        preferred_element_type=jnp.float32,
    )
    second = jax.nn.gelu(
        summed * hid_scale + b_second[0].astype(jnp.float32), approximate=True
    ).astype(jnp.bfloat16)
    partial_out = jnp.dot(second, w_third[0], preferred_element_type=jnp.float32) * hid_scale
    pred = lax.psum(partial_out, "pair")
    resid = observed + jnp.sqrt(variance) * perturb[0] - pred
    half = pred.shape[0] // 2
    row_start = lax.axis_index("pair") * half
    pred_half = lax.dynamic_slice_in_dim(pred, row_start, half, 0).reshape(1, -1)
    res_half = lax.dynamic_slice_in_dim(resid, row_start, half, 0).reshape(1, -1)
    var_half = lax.dynamic_slice_in_dim(variance, row_start, half, 0).reshape(1, -1)
    allpred, allres = (
        lax.all_gather(pred_half, "member", axis=0, tiled=True),
        lax.all_gather(res_half, "member", axis=0, tiled=True),
    )
    amat, bmat = moments(allpred, allres, var_half)
    amat, bmat = lax.psum((amat, bmat), "pair")
    gain = solve_gain(amat, bmat)
    gain_tr = gain.astype(jnp.bfloat16).T
    slabs = to_slabs(shards)
    mixed = [mix_slab(slab, gain_tr) for slab in slabs]
    returned = (
        lax.all_to_all(mixed[0], "member", split_axis=0, concat_axis=1, tiled=True),
        lax.all_to_all(mixed[1], "member", split_axis=0, concat_axis=1, tiled=True),
        lax.all_to_all(mixed[2], "member", split_axis=0, concat_axis=1, tiled=True),
        lax.all_to_all(mixed[3], "member", split_axis=0, concat_axis=1, tiled=True),
        lax.all_to_all(mixed[4], "member", split_axis=0, concat_axis=1, tiled=True),
    )
    return tuple((back.reshape(orig.shape) for back, orig in zip(returned, shards)))


def solution(mesh):
    in_specs = (
        P(),
        P("member", None, "pair"),
        P("member", "pair"),
        P("member", None, "pair"),
        P("member", "pair"),
        P("member", "pair", None),
        P(),
        P("member", None, None),
        P(),
    )
    out_specs = (
        P("member", None, "pair"),
        P("member", "pair"),
        P("member", None, "pair"),
        P("member", "pair"),
        P("member", "pair", None),
    )
    return jax.shard_map(body, mesh=mesh, in_specs=in_specs, out_specs=out_specs, check_vma=False)
```

profile of v0, /device:TPU:12, one launch (start us, length us, event | category | flops | bytes accessed | tf_op | source)
XLA Modules:
  0.0 484.4 jit_solution(5044105605474703341)
XLA Ops:
  12.4 7.2 %all-to-all-start.2 = ((bf16[1,16,64]{2,0,1:T(2,128)(2,1)}), bf16[1,16,64]{2,0,1:T(2,128)(2,1)S(1)}, u32[]{:S(2)}, u32[]{:S(2)}) async-start(bf16[1,16,64]{2,0,1:T(2,128)(2,1)} %all_to_all.127), calls=%async_computation.2 | async-start | bytes 16384 | tf_op jit(solution)/shard_map/all_to_all | solution.py:29
  20.3 4.3 all-to-all-done.2
  24.6 5.6 %all-to-all-start.6 = ((bf16[1,16,64]{2,0,1:T(2,128)(2,1)}), bf16[1,16,64]{2,0,1:T(2,128)(2,1)S(1)}, u32[]{:S(2)}, u32[]{:S(2)}) async-start(bf16[1,16,64]{2,0,1:T(2,128)(2,1)} %all_to_all.129), calls=%async_computation.6 | async-start | bytes 16384 | tf_op jit(solution)/shard_map/all_to_all | solution.py:31
  35.2 5.7 %all-to-all-start.8 = ((bf16[16,2,2048]{2,1,0:T(2,128)(2,1)}), bf16[16,2,2048]{2,1,0:T(2,128)(2,1)S(1)}, u32[]{:S(2)}, u32[]{:S(2)}) async-start(bf16[16,2,2048]{2,1,0:T(2,128)(2,1)} %reshape.164), calls=%async_computation.8 | async-start | bytes 262144 | tf_op jit(solution)/shard_map/all_to_all | solution.py:32
  41.2 6.4 %fusion.30 = f32[512,64]{0,1:T(8,128)} fusion(bf16[512,2048]{1,0:T(8,128)(2,1)} %all-gather.6.cloned.1.call-done, bf16[1,2048,1024]{2,1,0:T(8,128)(2,1)} %param.12, f32[1024]{0:T(1024)S(1)} %bitcast.94, bf16[1,1024,64]{1,2,0:T(8,128)(2,1)S(1)} %copy-done.6), kind=kOutput, calls=%fused_computation.32 | convolution fusion | flops 2220392448 | bytes 6557696 | tf_op jit(solution)/shard_map/dot_general | solution.py:60
  47.6 4.2 all_to_all.126
  51.8 8.0 %reduce.21 = bf16[16,32768]{1,0:T(8,128)(2,1)} reduce(bf16[16,1,32768]{2,1,0:T(2,128)(2,1)S(1)} %bitcast.89, bf16[]{:T(256)} %broadcast.153), dimensions={1}, to_apply=%bitcast.67.reduce_sub_computation | reduce | bytes 2097154
  62.6 7.0 %all-to-all-start = ((bf16[16,2,16384]{2,1,0:T(2,128)(2,1)}), bf16[16,2,16384]{2,1,0:T(2,128)(2,1)S(1)}, u32[]{:S(2)}, u32[]{:S(2)}) async-start(bf16[16,2,16384]{2,1,0:T(2,128)(2,1)} %reshape.156), calls=%async_computation | async-start | bytes 2097152 | tf_op jit(solution)/shard_map/all_to_all | solution.py:28
  71.8 12.0 %all_to_all.128 = bf16[1,16,131072]{2,0,1:T(2,128)(2,1)} reshape(bf16[1,2048,1024]{2,1,0:T(8,128)(2,1)} %param.12) | data formatting | bytes 8388608 | tf_op jit(solution)/shard_map/all_to_all | solution.py:30
  83.8 26.5 %reduce.23 = bf16[16,131072]{1,0:T(8,128)(2,1)} reduce(bf16[16,1,131072]{2,1,0:T(2,128)(2,1)} %bitcast.88, bf16[]{:T(256)} %broadcast.153), dimensions={1}, to_apply=%bitcast.69.reduce_sub_computation | reduce | bytes 8388610
  110.3 6.6 %reshape.160 = bf16[16,2,65536]{2,1,0:T(2,128)(2,1)} reshape(bf16[16,131072]{1,0:T(8,128)(2,1)} %reduce.23) | data formatting | bytes 8388608
  118.7 6.9 %all-to-all-start.4 = ((bf16[16,2,65536]{2,1,0:T(2,128)(2,1)}), bf16[16,2,65536]{2,1,0:T(2,128)(2,1)}, u32[]{:S(2)}, u32[]{:S(2)}) async-start(bf16[16,2,65536]{2,1,0:T(2,128)(2,1)} %reshape.160), calls=%async_computation.4 | async-start | bytes 8388608 | tf_op jit(solution)/shard_map/all_to_all | solution.py:30
  125.6 4.3 reshape.157
  139.2 89.4 %all-gather.10.cloned.1.call-done = f32[16,1,16384]{2,1,0:T(1,128)} async-done(((f32[1,1,16384]{2,1,0:T(1,128)}), f32[16,1,16384]{2,1,0:T(1,128)}) %all-gather.10.cloned.1.call-update) | async-done | bytes 1048592 | tf_op jit(solution)/shard_map/all_gather | solution.py:70
  228.6 4.0 fusion.36
  245.6 6.6 %all-to-all-start.3 = ((bf16[16,1,64]{2,1,0:T(2,128)(2,1)}), bf16[16,1,64]{2,1,0:T(2,128)(2,1)S(1)}, u32[]{:S(2)}, u32[]{:S(2)}) async-start(bf16[16,1,64]{2,1,0:T(2,128)(2,1)} %copy.41), calls=%async_computation.3 | async-start | bytes 16384 | tf_op jit(solution)/shard_map/all_to_all | solution.py:80
  258.6 12.3 %reshape.161 = bf16[16,1,131072]{2,1,0:T(2,128)(2,1)} reshape(bf16[16,2,65536]{2,1,0:T(2,128)(2,1)} %all-to-all-done.4) | data formatting | bytes 8388608
  270.9 6.9 %all-to-all-start.7 = ((bf16[16,1,64]{2,1,0:T(2,128)(2,1)}), bf16[16,1,64]{2,1,0:T(2,128)(2,1)S(1)}, u32[]{:S(2)}, u32[]{:S(2)}) async-start(bf16[16,1,64]{2,1,0:T(2,128)(2,1)} %copy.45), calls=%async_computation.7 | async-start | bytes 16384 | tf_op jit(solution)/shard_map/all_to_all | solution.py:82
  277.8 10.8 %bitcast_convert_fusion = f32[1,16,131072]{2,0,1:T(1,128)} fusion(bf16[16,1,131072]{2,1,0:T(2,128)(2,1)} %reshape.161), kind=kLoop, calls=%fused_computation.100 | loop fusion | flops 2097152 | bytes 12582912 | tf_op jit(solution)/shard_map/convert_element_type | solution.py:37
  288.6 6.9 %all-to-all-start.9 = ((bf16[16,2,2048]{2,1,0:T(2,128)(2,1)}), bf16[16,2,2048]{2,1,0:T(2,128)(2,1)S(1)}, u32[]{:S(2)}, u32[]{:S(2)}) async-start(bf16[16,2,2048]{2,1,0:T(2,128)(2,1)} %reshape.166), calls=%async_computation.9 | async-start | bytes 262144 | tf_op jit(solution)/shard_map/all_to_all | solution.py:83
  295.6 9.0 %convert_reduce_fusion.2 = f32[131072]{0:T(1024)S(1)} fusion(bf16[16,1,131072]{2,1,0:T(2,128)(2,1)} %reshape.161), kind=kLoop, calls=%fused_computation.90 | loop fusion | flops 4063232 | bytes 4718592 | tf_op jit(solution)/shard_map/reduce_sum | solution.py:38
  304.6 6.9 %all-to-all-start.1 = ((bf16[16,2,16384]{2,1,0:T(2,128)(2,1)}), bf16[16,2,16384]{2,1,0:T(2,128)(2,1)S(1)}, u32[]{:S(2)}, u32[]{:S(2)}) async-start(bf16[16,2,16384]{2,1,0:T(2,128)(2,1)} %reshape.158), calls=%async_computation.1 | async-start | bytes 2097152 | tf_op jit(solution)/shard_map/all_to_all | solution.py:79
  311.5 10.2 %fusion = bf16[16,1,131072]{2,0,1:T(8,128)(2,1)} fusion(bf16[16,16]{1,0:T(8,128)(2,1)S(1)} %convolution_convert_fusion.5, f32[1,16,131072]{2,0,1:T(1,128)} %bitcast_convert_fusion, f32[131072]{0:T(1024)S(1)} %broadcast_multiply_fusion), kind=kOutput, calls=%fused_computation.1 | convolution fusion | flops 73400320 | bytes 13107712 | tf_op jit(solution)/shard_map/dot_general | solution.py:39
  321.8 6.7 %reduce.24 = bf16[16,131072]{1,0:T(8,128)(2,1)} reduce(bf16[16,1,131072]{2,0,1:T(8,128)(2,1)} %fusion, bf16[]{:T(256)} %broadcast.153), dimensions={1}, to_apply=%copy.43.reduce_sub_computation | reduce | bytes 8388610 | tf_op jit(solution)/shard_map/all_to_all | solution.py:81
  328.5 6.6 %reshape.162 = bf16[16,2,65536]{2,1,0:T(2,128)(2,1)} reshape(bf16[16,131072]{1,0:T(8,128)(2,1)} %reduce.24) | data formatting | bytes 8388608
  336.6 6.7 %all-to-all-start.5 = ((bf16[16,2,65536]{2,1,0:T(2,128)(2,1)}), bf16[16,2,65536]{2,1,0:T(2,128)(2,1)}, u32[]{:S(2)}, u32[]{:S(2)}) async-start(bf16[16,2,65536]{2,1,0:T(2,128)(2,1)} %reshape.162), calls=%async_computation.5 | async-start | bytes 8388608 | tf_op jit(solution)/shard_map/all_to_all | solution.py:81
  346.7 4.3 reshape.159
  351.0 7.4 %reduce.12 = bf16[16,32768]{1,0:T(8,128)(2,1)} reduce(bf16[16,1,32768]{2,1,0:T(2,128)(2,1)S(1)} %reshape.159, bf16[]{:T(256)} %constant.89), dimensions={1}, to_apply=%all_to_all.107.reduce_sub_computation | reduce | bytes 2097154 | tf_op jit(solution)/shard_map/all_to_all | solution.py:79
  360.7 74.0 %all-to-all-done.5 = bf16[16,2,65536]{2,1,0:T(2,128)(2,1)} async-done(((bf16[16,2,65536]{2,1,0:T(2,128)(2,1)}), bf16[16,2,65536]{2,1,0:T(2,128)(2,1)}, u32[]{:S(2)}, u32[]{:S(2)}) %all-to-all-start.5) | async-done | bytes 4194336 | tf_op jit(solution)/shard_map/all_to_all | solution.py:81
  434.7 12.3 %reshape.163 = bf16[16,1,131072]{2,1,0:T(2,128)(2,1)} reshape(bf16[16,2,65536]{2,1,0:T(2,128)(2,1)} %all-to-all-done.5) | data formatting | bytes 8388608
  447.0 25.8 %reduce.15 = bf16[16,131072]{1,0:T(8,128)(2,1)} reduce(bf16[16,1,131072]{2,1,0:T(2,128)(2,1)} %reshape.163, bf16[]{:T(256)} %constant.89), dimensions={1}, to_apply=%all_to_all.116.reduce_sub_computation | reduce | bytes 8388610 | tf_op jit(solution)/shard_map/all_to_all | solution.py:81
  472.8 4.9 %reshape.139 = bf16[1,2048,1024]{2,1,0:T(8,128)(2,1)} reshape(bf16[16,131072]{1,0:T(8,128)(2,1)} %reduce.15) | data formatting | bytes 8388608 | tf_op jit(solution)/shard_map/reshape | solution.py:85
  (103 shorter events, 53.7 us)
Async XLA Ops:
  7.2 1.1 copy-start
  7.2 34.0 %all-gather.6.cloned.1.call-start = ((), (), s32[]{:S(2)}) async-start(), calls=%async_computation.10 | async-start | bytes 3145728 | tf_op jit(solution)/shard_map/all_gather | solution.py:53
  8.3 21.9 %copy-start.6 = (bf16[1,1024,64]{1,2,0:T(8,128)(2,1)S(1)}, bf16[1,1024,64]{1,2,0:T(8,128)(2,1)}, u32[]{:S(2)}) copy-start(bf16[1,1024,64]{1,2,0:T(8,128)(2,1)} %param.14) | copy-start | bytes 393220
  12.4 12.1 %all-to-all-start.2 = ((bf16[1,16,64]{2,0,1:T(2,128)(2,1)}), bf16[1,16,64]{2,0,1:T(2,128)(2,1)S(1)}, u32[]{:S(2)}, u32[]{:S(2)}) async-start(bf16[1,16,64]{2,0,1:T(2,128)(2,1)} %all_to_all.127), calls=%async_computation.2 | async-start | bytes 16384 | tf_op jit(solution)/shard_map/all_to_all | solution.py:29
  24.6 10.7 %all-to-all-start.6 = ((bf16[1,16,64]{2,0,1:T(2,128)(2,1)}), bf16[1,16,64]{2,0,1:T(2,128)(2,1)S(1)}, u32[]{:S(2)}, u32[]{:S(2)}) async-start(bf16[1,16,64]{2,0,1:T(2,128)(2,1)} %all_to_all.129), calls=%async_computation.6 | async-start | bytes 16384 | tf_op jit(solution)/shard_map/all_to_all | solution.py:31
  35.2 27.3 %all-to-all-start.8 = ((bf16[16,2,2048]{2,1,0:T(2,128)(2,1)}), bf16[16,2,2048]{2,1,0:T(2,128)(2,1)S(1)}, u32[]{:S(2)}, u32[]{:S(2)}) async-start(bf16[16,2,2048]{2,1,0:T(2,128)(2,1)} %reshape.164), calls=%async_computation.8 | async-start | bytes 262144 | tf_op jit(solution)/shard_map/all_to_all | solution.py:32
  40.9 29.1 %all-reduce.3.cloned.1.call-start = ((), (), s32[]{:S(2)}) async-start(), calls=%async_computation.11 | async-start | bytes 262144 | tf_op jit(solution)/shard_map/psum | solution.py:61
  59.8 10.2 %copy-start.7 = (f32[512,64]{0,1:T(8,128)S(1)}, f32[512,64]{0,1:T(8,128)}, u32[]{:S(2)}) copy-start(f32[512,64]{0,1:T(8,128)} %param.17) | copy-start | bytes 393220
  59.8 10.2 %copy-start.8 = (f32[1,512,64]{1,2,0:T(8,128)S(1)}, f32[1,512,64]{1,2,0:T(8,128)}, u32[]{:S(2)}) copy-start(f32[1,512,64]{1,2,0:T(8,128)} %param.16) | copy-start | bytes 393220
  59.8 10.2 %copy-start.9 = (f32[512,64]{0,1:T(8,128)S(1)}, f32[512,64]{0,1:T(8,128)}, u32[]{:S(2)}) copy-start(f32[512,64]{0,1:T(8,128)} %param.15) | copy-start | bytes 393220
  62.6 55.1 %all-to-all-start = ((bf16[16,2,16384]{2,1,0:T(2,128)(2,1)}), bf16[16,2,16384]{2,1,0:T(2,128)(2,1)S(1)}, u32[]{:S(2)}, u32[]{:S(2)}) async-start(bf16[16,2,16384]{2,1,0:T(2,128)(2,1)} %reshape.156), calls=%async_computation | async-start | bytes 2097152 | tf_op jit(solution)/shard_map/all_to_all | solution.py:28
  69.6 67.7 %all-gather.8.cloned.1.call-start = ((), (), s32[]{:S(2)}) async-start(), calls=%async_computation.12 | async-start | bytes 1114112 | tf_op jit(solution)/shard_map/all_gather | solution.py:69
  117.7 1.0 copy-start.3
  118.7 126.9 %all-to-all-start.4 = ((bf16[16,2,65536]{2,1,0:T(2,128)(2,1)}), bf16[16,2,65536]{2,1,0:T(2,128)(2,1)}, u32[]{:S(2)}, u32[]{:S(2)}) async-start(bf16[16,2,65536]{2,1,0:T(2,128)(2,1)} %reshape.160), calls=%async_computation.4 | async-start | bytes 8388608 | tf_op jit(solution)/shard_map/all_to_all | solution.py:30
  125.6 103.0 %all-gather.10.cloned.1.call-start = ((), (), s32[]{:S(2)}) async-start(), calls=%async_computation.13 | async-start | bytes 1114112 | tf_op jit(solution)/shard_map/all_gather | solution.py:70
  228.6 4.0 copy-start.5
  232.6 10.7 %copy-start.2 = (f32[1,16,32768]{2,0,1:T(1,128)S(1)}, f32[1,16,32768]{2,0,1:T(1,128)}, u32[]{:S(2)}) copy-start(f32[1,16,32768]{2,0,1:T(1,128)} %bitcast_convert_fusion.1) | copy-start | bytes 6291460
  245.6 25.3 %all-to-all-start.3 = ((bf16[16,1,64]{2,1,0:T(2,128)(2,1)}), bf16[16,1,64]{2,1,0:T(2,128)(2,1)S(1)}, u32[]{:S(2)}, u32[]{:S(2)}) async-start(bf16[16,1,64]{2,1,0:T(2,128)(2,1)} %copy.41), calls=%async_computation.3 | async-start | bytes 16384 | tf_op jit(solution)/shard_map/all_to_all | solution.py:80
  270.9 17.7 %all-to-all-start.7 = ((bf16[16,1,64]{2,1,0:T(2,128)(2,1)}), bf16[16,1,64]{2,1,0:T(2,128)(2,1)S(1)}, u32[]{:S(2)}, u32[]{:S(2)}) async-start(bf16[16,1,64]{2,1,0:T(2,128)(2,1)} %copy.45), calls=%async_computation.7 | async-start | bytes 16384 | tf_op jit(solution)/shard_map/all_to_all | solution.py:82
  288.6 15.9 %all-to-all-start.9 = ((bf16[16,2,2048]{2,1,0:T(2,128)(2,1)}), bf16[16,2,2048]{2,1,0:T(2,128)(2,1)S(1)}, u32[]{:S(2)}, u32[]{:S(2)}) async-start(bf16[16,2,2048]{2,1,0:T(2,128)(2,1)} %reshape.166), calls=%async_computation.9 | async-start | bytes 262144 | tf_op jit(solution)/shard_map/all_to_all | solution.py:83
  304.6 31.1 %all-to-all-start.1 = ((bf16[16,2,16384]{2,1,0:T(2,128)(2,1)}), bf16[16,2,16384]{2,1,0:T(2,128)(2,1)S(1)}, u32[]{:S(2)}, u32[]{:S(2)}) async-start(bf16[16,2,16384]{2,1,0:T(2,128)(2,1)} %reshape.158), calls=%async_computation.1 | async-start | bytes 2097152 | tf_op jit(solution)/shard_map/all_to_all | solution.py:79
  335.7 1.0 copy-start.4
  336.6 98.0 %all-to-all-start.5 = ((bf16[16,2,65536]{2,1,0:T(2,128)(2,1)}), bf16[16,2,65536]{2,1,0:T(2,128)(2,1)}, u32[]{:S(2)}, u32[]{:S(2)}) async-start(bf16[16,2,65536]{2,1,0:T(2,128)(2,1)} %reshape.162), calls=%async_computation.5 | async-start | bytes 8388608 | tf_op jit(solution)/shard_map/all_to_all | solution.py:81
  472.8 4.9 %copy-start.1 = (bf16[512,512]{1,0:T(8,128)(2,1)S(1)}, bf16[512,512]{1,0:T(8,128)(2,1)}, u32[]{:S(2)}) copy-start(bf16[512,512]{1,0:T(8,128)(2,1)} %param.9) | copy-start | bytes 1572868
Sparse Core Ops, SparseCore 0:
  11.9 11.9 all-gather.5
  47.7 19.0 all-reduce.2
  73.1 57.7 all-gather.7
  134.1 94.4 all-gather.9
where the time goes:
time: 490 us; the launch traced here: 484 us
  waiting for transfers between devices  170 us (35%)
  other arithmetic  114 us (23%)
  local copies, waits for them, and re-layouts  85.8 us (18%)
  starting transfers between devices  67.1 us (14%)
  matrix products  29.2 us (6%)
  between operations  14.3 us (3%)
    all_gather x1, waiting for transfers between devices, body(): lax.all_gather(res_half, 'member', axis=0, tiled=True)  89.4 us
    all_to_all x1, waiting for transfers between devices, body(): lax.all_to_all(mixed[2], 'member', split_axis=0, concat_axis=1, tiled=True)  74 us
    unnamed x37, local copies, waits for them, and re-layouts  57.7 us
    unnamed x4, other arithmetic  36.6 us
    all_to_all x2, other arithmetic, body(): lax.all_to_all(mixed[2], 'member', split_axis=0, concat_axis=1, tiled=True)  32.5 us
    convert_element_type x5, other arithmetic, mix_slab(): full = slab.astype(jnp.float32)  14.7 us
    dot_general x5, matrix products, mix_slab(): jnp.dot(gain_tr, center, preferred_element_type=jnp.float32)  13.1 us
    all_to_all x1, local copies, waits for them, and re-layouts, to_slabs(): lax.all_to_all(flats[2], 'member', split_axis=1, concat_axis=0, tiled=True)  12 us
  transfers between devices with their start and end apart: 14, of which 5 were waited for; matrix products, arithmetic and copies ran while one was open for 33% of the time, Pallas kernels for 0%

commit v1 on v0

v1 whole, which is shorter than its diff:
```python
import functools

import jax
import jax.numpy as jnp
from jax import lax
from jax.experimental import pallas as pl
from jax.experimental.pallas import tpu as pltpu
from jax.sharding import PartitionSpec as P

ROWS = 16
EARLY = 32
PLANE = 4
TILE = 256
LIGHT = pl.CostEstimate(flops=1, bytes_accessed=1, transcendentals=0)


def solve_gain(amat, bmat):
    count = amat.shape[0]
    system = amat + count * jnp.eye(count, dtype=jnp.float32)
    factor = jnp.linalg.cholesky(system)
    middle = lax.linalg.triangular_solve(
        factor, bmat, left_side=True, lower=True, transpose_a=False
    )
    return lax.linalg.triangular_solve(factor, middle, left_side=True, lower=True, transpose_a=True)


def mix_block(spread, x):
    members, rows, width = x.shape
    full = x.astype(jnp.float32)
    mean = jnp.sum(full, axis=0, keepdims=True) * (1.0 / members)
    center = (full - mean).astype(jnp.bfloat16).reshape(members * rows, width)
    mixed = jnp.dot(spread, center, preferred_element_type=jnp.float32)
    return mixed.astype(jnp.bfloat16).reshape(members, rows, width)


def mix_kernel(spread_ref, x_ref, y_ref):
    y_ref[...] = mix_block(spread_ref[...], x_ref[...])


def mix_two_kernel(split, spread_c_ref, spread_b_ref, c_ref, b_ref, y_ref):
    @pl.when(pl.program_id(0) < split)
    def _():
        y_ref[...] = mix_block(spread_c_ref[...], c_ref[...])

    @pl.when(pl.program_id(0) >= split)
    def _():
        y_ref[...] = mix_block(spread_b_ref[...], b_ref[...])


def spread_gain(gain_tr):
    members = gain_tr.shape[0]
    size = members * ROWS
    row = lax.broadcasted_iota(jnp.int32, (size, members), 0)
    col = lax.broadcasted_iota(jnp.int32, (size, members), 1)
    expand = (row // ROWS == col).astype(jnp.bfloat16)
    wide = jnp.dot(expand, gain_tr, preferred_element_type=jnp.float32).astype(jnp.bfloat16)
    wide = lax.dot_general(
        wide, expand, (((1,), (1,)), ((), ())), preferred_element_type=jnp.float32
    ).astype(jnp.bfloat16)
    at_row = lax.broadcasted_iota(jnp.int32, (size, size), 0) % ROWS
    at_col = lax.broadcasted_iota(jnp.int32, (size, size), 1) % ROWS
    return jnp.where(at_row == at_col, wide, jnp.bfloat16(0))


def mix_plain(slab, gain_tr):
    full = slab.astype(jnp.float32)
    center = (full - jnp.mean(full, axis=0, keepdims=True)).astype(jnp.bfloat16)
    return jnp.einsum(
        "jk,krc->jrc", gain_tr, center, preferred_element_type=jnp.float32
    ).astype(jnp.bfloat16)


def mix(slab, spread):
    members, rows, width = slab.shape
    block = pl.BlockSpec((members, ROWS, width), lambda i: (0, i, 0))
    return pl.pallas_call(
        mix_kernel,
        grid=(rows // ROWS,),
        in_specs=[pl.BlockSpec(spread.shape, lambda i: (0, 0)), block],
        out_specs=block,
        out_shape=jax.ShapeDtypeStruct(slab.shape, jnp.bfloat16),
        compiler_params=pltpu.CompilerParams(vmem_limit_bytes=32 << 20),
        cost_estimate=LIGHT,
    )(spread, slab)


def mix_two(slab_c, spread_c, slab_b, kept, spread_b):
    members, rows, width = slab_c.shape
    split = rows // ROWS
    rows = rows + kept
    out = jax.ShapeDtypeStruct((members, rows, width), jnp.bfloat16)
    whole = pl.BlockSpec(spread_c.shape, lambda i: (0, 0))
    shape = (members, ROWS, width)
    return pl.pallas_call(
        functools.partial(mix_two_kernel, split),
        grid=(rows // ROWS,),
        in_specs=[
            whole,
            whole,
            pl.BlockSpec(shape, lambda i: (0, jnp.minimum(i, split - 1), 0)),
            pl.BlockSpec(shape, lambda i: (0, jnp.maximum(i - split, 0), 0)),
        ],
        out_specs=pl.BlockSpec(shape, lambda i: (0, i, 0)),
        out_shape=out,
        compiler_params=pltpu.CompilerParams(vmem_limit_bytes=32 << 20),
        cost_estimate=LIGHT,
    )(spread_c, spread_b, slab_c, slab_b)


def first_kernel(scale, x_ref, w_ref, b_ref, y_ref):
    summed = jnp.dot(x_ref[...], w_ref[...], preferred_element_type=jnp.float32)
    y = jax.nn.gelu(summed * scale + b_ref[...].astype(jnp.float32), approximate=True)
    y_ref[...] = y.astype(jnp.bfloat16)


def first_layer(x, w, b):
    rows, depth = x.shape
    step = min(TILE, w.shape[1])
    return pl.pallas_call(
        functools.partial(first_kernel, depth ** (-0.5)),
        grid=(w.shape[1] // step,),
        in_specs=[
            pl.BlockSpec((rows, depth), lambda i: (0, 0)),
            pl.BlockSpec((depth, step), lambda i: (0, i)),
            pl.BlockSpec((1, step), lambda i: (0, i)),
        ],
        out_specs=pl.BlockSpec((rows, step), lambda i: (0, i)),
        out_shape=jax.ShapeDtypeStruct((rows, w.shape[1]), jnp.bfloat16),
        compiler_params=pltpu.CompilerParams(vmem_limit_bytes=32 << 20),
        cost_estimate=LIGHT,
    )(x, w, b)


def second_kernel(scale, side_ref, mine_ref, other_ref, wm_ref, wo_ref, b_ref, third_ref, y_ref):
    summed = jnp.dot(mine_ref[...], wm_ref[...], preferred_element_type=jnp.float32)
    summed += jnp.dot(other_ref[...], wo_ref[...], preferred_element_type=jnp.float32)
    y = jax.nn.gelu(summed * scale + b_ref[...].astype(jnp.float32), approximate=True)
    part = lax.dot_general(
        third_ref[...],
        y.astype(jnp.bfloat16),
        (((1,), (1,)), ((), ())),
        preferred_element_type=jnp.float32,
    )

    @pl.when(pl.program_id(0) == 0)
    def _():
        y_ref[...] = jnp.zeros_like(y_ref)

    y_ref[...] += part * scale


def second_and_third(side, mine, other, w, b, third):
    rows, depth = mine.shape
    outs = third.shape[0]
    step = min(TILE, w.shape[1])
    return pl.pallas_call(
        functools.partial(second_kernel, w.shape[0] ** (-0.5)),
        grid_spec=pltpu.PrefetchScalarGridSpec(
            num_scalar_prefetch=1,
            grid=(w.shape[1] // step,),
            in_specs=[
                pl.BlockSpec((rows, depth), lambda i, side: (0, 0)),
                pl.BlockSpec((rows, depth), lambda i, side: (0, 0)),
                pl.BlockSpec((depth, step), lambda i, side: (side[0], i)),
                pl.BlockSpec((depth, step), lambda i, side: (1 - side[0], i)),
                pl.BlockSpec((1, step), lambda i, side: (0, i)),
                pl.BlockSpec((outs, step), lambda i, side: (0, i)),
            ],
            out_specs=pl.BlockSpec((outs, rows), lambda i, side: (0, 0)),
        ),
        out_shape=jax.ShapeDtypeStruct((outs, rows), jnp.float32),
        compiler_params=pltpu.CompilerParams(vmem_limit_bytes=32 << 20),
        cost_estimate=LIGHT,
    )(side[None], mine, other, w, w, b, third)


def exchange(x):
    return lax.all_to_all(x, "member", split_axis=0, concat_axis=0, tiled=True)


def swap(x, axis, bit):
    count = lax.axis_size(axis)
    return lax.ppermute(x, axis, [(i, i ^ bit) for i in range(count)])


def reorder(gain_tr, order):
    pick = (order[None, :] == jnp.arange(gain_tr.shape[1])[:, None]).astype(jnp.bfloat16)
    return jnp.dot(gain_tr, pick, preferred_element_type=jnp.float32).astype(jnp.bfloat16)


def pick(x, at, axis=0):
    return lax.dynamic_index_in_dim(x, at, axis, keepdims=False)


def after(value, earlier):
    return lax.optimization_barrier((value, earlier))[0]


def body(samples, w_first, b_first, w_second, b_second, w_third, observed, perturb, variance):
    members = lax.axis_size("member")
    me = lax.axis_index("member")
    side = lax.axis_index("pair")
    width = w_first.shape[2]
    first_w, second_w, third_w = w_first[0], w_second[0], w_third[0]
    slabs_first = first_w.reshape(members, -1, width)
    slabs_second = second_w.reshape(members, -1, width)
    outs = third_w.shape[1]
    fast = members == PLANE * PLANE and outs % members == 0 and EARLY < slabs_second.shape[1]
    planes = members // PLANE
    plane, place = me // PLANE, me % PLANE

    def across(slabs, flip):
        blocks = slabs.reshape((planes, PLANE) + slabs.shape[1:])
        return swap(pick(blocks, plane ^ flip), "member", flip * PLANE)

    def within(parts):
        got = []
        for flip in range(PLANE):
            block = jnp.stack([pick(part, place ^ flip) for part in parts])
            got.append(swap(block, "member", flip) if flip else block)
        return got

    def own_plane(slabs):
        return pick(slabs.reshape((planes, PLANE) + slabs.shape[1:]), plane)

    first = first_layer(samples, first_w, b_first)
    partial_out = second_and_third(
        side, first, swap(first, "pair", 1), second_w, b_second, third_w.T
    )

    half = partial_out.shape[1] // 2
    start = side * half
    keep = lax.dynamic_slice_in_dim(partial_out, start, half, 1)
    give = lax.dynamic_slice_in_dim(partial_out, (1 - side) * half, half, 1)
    pred = keep + swap(give, "pair", 1)
    observed_half = lax.dynamic_slice_in_dim(observed.T, start, half, 1)
    variance_half = lax.dynamic_slice_in_dim(variance.T, start, half, 1)
    perturb_half = lax.dynamic_slice_in_dim(perturb[0].T, start, half, 1)
    resid = observed_half + jnp.sqrt(variance_half) * perturb_half - pred
    count = pred.size // members
    both = jnp.concatenate(
        [pred.reshape(members, 1, count), resid.reshape(members, 1, count)], axis=1
    )
    if fast:
        early = slabs_second[:, :EARLY]
        biases = jnp.concatenate([b_first.reshape(members, -1), b_second.reshape(members, -1)], 1)
        biases = jnp.pad(biases, ((0, 0), (0, width - biases.shape[1])))
        small = jnp.concatenate([third_w.T.reshape(members, -1, width), biases[:, None]], axis=1)
        small = jnp.pad(small, ((0, 0), (0, -small.shape[1] % 8), (0, 0)))
        late = jnp.concatenate([slabs_second[:, EARLY:], small], axis=1)
        parts = [own_plane(slabs_first)] + [across(slabs_first, i) for i in range(1, planes)]
        both, parts, late, early = lax.optimization_barrier((both, parts, late, early))
        both, got_first, far2 = lax.optimization_barrier(
            (exchange(both), within(parts), across(early, 2))
        )
    else:
        both = exchange(both)
    allpred, allres = both[:, 0], both[:, 1]
    var_part = lax.dynamic_index_in_dim(variance_half.reshape(members, count), me, 0)
    devpred = allpred - jnp.mean(allpred, axis=0, keepdims=True)
    scaled = devpred / var_part
    sums = jnp.dot(
        scaled, jnp.concatenate([devpred, allres], axis=0).T, precision=lax.Precision.HIGHEST
    )
    if fast:
        sums = sums + swap(sums, "pair", 1)
        sums = jnp.broadcast_to(sums[None], (members,) + sums.shape)
        sums, early = lax.optimization_barrier((sums, early))
        sums, far1, far3 = lax.optimization_barrier(
            (exchange(sums), across(early, 1), across(early, 3))
        )
        sums = jnp.sum(sums, axis=0)
        got_late = exchange(after(late, sums))
    else:
        sums = lax.psum(sums, ("member", "pair"))

    gain = solve_gain(sums[:, :members], sums[:, members:])
    gain_tr = gain.astype(jnp.bfloat16).T
    if fast:
        flips = jnp.arange(members)
        order = me ^ (flips // planes + flips % planes * PLANE)
        gain_in = reorder(gain_tr, order)
        spread = spread_gain(gain_tr)
        spread_in = spread_gain(gain_in)
        spread_both = spread_gain(reorder(gain_in.T, order).T)

        mixed_first = mix(jnp.concatenate(got_first, axis=0), spread_both)
        mixed_first = mixed_first.reshape((PLANE, planes) + mixed_first.shape[1:])
        back = jnp.stack(
            [mixed_first[0]] + [swap(mixed_first[i], "member", i) for i in range(1, PLANE)]
        )
        early_parts = after([own_plane(early), far1, far2, far3], mixed_first)
        got_early = within(early_parts)
        back, got_late, got_early = lax.optimization_barrier((back, got_late, got_early))
        homes = []
        for flip in range(planes):
            block = jnp.stack([pick(back, place ^ i)[flip] for i in range(PLANE)])
            homes.append(swap(block, "member", flip * PLANE) if flip else block)

        kept = slabs_second.shape[1] - EARLY
        mixed_second = mix_two(
            jnp.concatenate(got_early, axis=0), spread_in, got_late, kept, spread
        )
        mixed_small = mix_plain(got_late[:, kept:], gain_tr)
        mixed_second = jnp.concatenate([mixed_second, mixed_small], axis=1)
        mixed_second, homes = lax.optimization_barrier((mixed_second, homes))
        new_second = exchange(mixed_second)
        new_first = jnp.zeros(first_w.shape, jnp.bfloat16)
        size = first_w.shape[0] // planes
        for flip, home in enumerate(homes):
            new_first = lax.dynamic_update_slice_in_dim(
                new_first, home.reshape(size, width), (plane ^ flip) * size, 0
            )
        new_small = new_second[:, kept + EARLY :]
        new_second = new_second[:, : kept + EARLY]
        rows = outs // members
        new_third = new_small[:, :rows].reshape(outs, width).T
        cut = width // members
        new_bfirst = new_small[:, rows, :cut].reshape(b_first.shape)
        new_bsecond = new_small[:, rows, cut : 2 * cut].reshape(b_second.shape)
    else:
        new_first = exchange(mix_plain(exchange(slabs_first), gain_tr))
        new_second = exchange(mix_plain(exchange(slabs_second), gain_tr))
        small = jnp.concatenate([third_w.T, b_first, b_second], axis=0)
        full = lax.all_gather(small, "member", axis=0)
        new_small = mix_plain(full, lax.dynamic_index_in_dim(gain_tr, me, 0))[0]
        new_third = new_small[:outs].T
        new_bfirst = new_small[outs : outs + 1]
        new_bsecond = new_small[outs + 1 :]
    return (
        new_first.reshape(w_first.shape),
        new_bfirst,
        new_second.reshape(w_second.shape),
        new_bsecond,
        new_third[None],
    )


def solution(mesh):
    in_specs = (
        P(),
        P("member", None, "pair"),
        P("member", "pair"),
        P("member", None, "pair"),
        P("member", "pair"),
        P("member", "pair", None),
        P(),
        P("member", None, None),
        P(),
    )
    out_specs = (
        P("member", None, "pair"),
        P("member", "pair"),
        P("member", None, "pair"),
        P("member", "pair"),
        P("member", "pair", None),
    )
    return jax.shard_map(body, mesh=mesh, in_specs=in_specs, out_specs=out_specs, check_vma=False)
```

time: 490 us -> 305 us (0.62)
  other arithmetic: 114 us -> 23.8 us
  local copies, waits for them, and re-layouts: 85.8 us -> 34.9 us
  starting transfers between devices: 67.1 us -> 41.2 us
  matrix products: 29.2 us -> 5.74 us
  between operations: 14.3 us -> 1.29 us
  Pallas kernels: 0 us -> 11.5 us
  blocking collectives: 3.3 us -> 13.5 us
    all_gather x3 -> x0, waiting for transfers between devices: 89.4 us -> none  [the longest x1 89.4 us: body(): lax.all_gather(res_half, 'member', axis=0, tiled=True)]
    ppermute x0 -> x21, waiting for transfers between devices: none -> 60.7 us  [swap(): return lax.ppermute(x, axis, [(i, i ^ bit) for i in range(count)])]
    unnamed x37 -> x52, local copies, waits for them, and re-layouts: 57.7 us -> 7.29 us
    all_to_all x10 -> x3, starting transfers between devices: 66.4 us -> 18.1 us  [exchange(): return lax.all_to_all(x, 'member', split_axis=0, concat_axis=0, tiled=True)]
    all_to_all x8 -> x1, other arithmetic: 44 us -> 0.72 us  [exchange(): return lax.all_to_all(x, 'member', split_axis=0, concat_axis=0, tiled=True)]
    unnamed x4 -> x2, other arithmetic: 36.6 us -> 0.05 us
    all_to_all x10 -> x3, waiting for transfers between devices: 80.9 us -> 111 us  [exchange(): return lax.all_to_all(x, 'member', split_axis=0, concat_axis=0, tiled=True)]
    dot_general x9 -> x7, matrix products: 28.9 us -> 5.38 us  [the longest x3 4.54 us: spread_gain(): lax.dot_general(wide, expand, (((1,), (1,)), ((), ())), preferred_element...]
  transfers between devices with their start and end apart: 14 -> 24, of which waited for: 5 -> 15; matrix products, arithmetic and copies ran while one was open for 33% -> 15% of each run, Pallas kernels for 0% -> 3%
where the time goes in v1:
time: 305 us; the launch traced here: 303 us
  waiting for transfers between devices  171 us (56%)
  starting transfers between devices  41.2 us (14%)
  local copies, waits for them, and re-layouts  34.9 us (11%)
  other arithmetic  23.8 us (8%)
  blocking collectives  13.5 us (4%)
  Pallas kernels  11.5 us (4%)
  matrix products  5.74 us (2%)
    all_to_all x3, waiting for transfers between devices, exchange(): return lax.all_to_all(x, 'member', split_axis=0, concat_axis=0, tiled=True)  111 us
    ppermute x21, waiting for transfers between devices, swap(): return lax.ppermute(x, axis, [(i, i ^ bit) for i in range(count)])  60.7 us
    ppermute x21, starting transfers between devices, swap(): return lax.ppermute(x, axis, [(i, i ^ bit) for i in range(count)])  23.1 us
    all_to_all x3, starting transfers between devices, exchange(): return lax.all_to_all(x, 'member', split_axis=0, concat_axis=0, tiled=True)  18.1 us
    all_to_all x1, blocking collectives, exchange(): return lax.all_to_all(x, 'member', split_axis=0, concat_axis=0, tiled=True)  13.5 us
    unnamed x52, local copies, waits for them, and re-layouts  7.29 us
  transfers between devices with their start and end apart: 24, of which 15 were waited for; matrix products, arithmetic and copies ran while one was open for 15% of the time, Pallas kernels for 3%

profile of v1, /device:TPU:12, one launch (start us, length us, event | category | flops | bytes accessed | tf_op | source)
XLA Modules:
  0.0 303.2 jit_solution(2155448368152269721)
XLA Ops:
  3.6 1.8 shard_map.128.mine_ref
  7.3 2.6 collective-permute-start.3
  10.8 4.0 %slice.211 = bf16[16,96,1024]{2,1,0:T(8,128)(2,1)} slice(bf16[16,128,1024]{2,1,0:T(8,128)(2,1)} %bitcast.121), slice={[0:16], [32:128], [0:1024]} | slice | bytes 6291456 | tf_op jit(solution)/shard_map/slice | solution.py:250
  15.0 2.2 copy-done
  17.2 4.7 %shard_map.129 = f32[64,512]{1,0:T(8,128)S(1)} custom-call(s32[1]{0:T(128)} %bitcast.side_ref, bf16[512,1024]{1,0:T(8,128)(2,1)S(1)} %shard_map.128.mine_ref, bf16[512,1024]{1,0:T(8,128)(2,1)S(1)} %collective-permute-done.other_ref, bf16[2048,1024]{1,0:T(8,128)(2,1)S(1)} %bitcast.123, bf16[2048,1024]{1,0:T(8,128)(2,1)S(1)} %bitcast.124, ...), custom_call_target="tpu_custom_call" | custom-call | flops 1 | bytes 1 | tf_op jit(solution)/shard_map/pallas_call | solution.py:156
  22.0 2.1 pad_maximum_fusion.1
  27.9 5.9 %collective-permute-done.4 = bf16[4,32,1024]{2,1,0:T(8,128)(2,1)} collective-permute-done((bf16[4,32,1024]{2,1,0:T(8,128)(2,1)S(1)}, bf16[4,32,1024]{2,1,0:T(8,128)(2,1)}, u32[]{:S(2)}, u32[]{:S(2)}) %collective-permute-start.4) | collective-permute-done | bytes 262176 | tf_op jit(solution)/shard_map/ppermute | solution.py:183
  33.7 6.2 %all-to-all-start = ((f32[16,2,1024]{2,1,0:T(2,128)}), f32[16,2,1024]{2,1,0:T(2,128)S(1)}, u32[]{:S(2)}, u32[]{:S(2)}) async-start(f32[16,2,1024]{2,1,0:T(2,128)} %pad_maximum_fusion.17), calls=%async_computation | async-start | bytes 262144 | tf_op jit(solution)/shard_map/all_to_all | solution.py:178
  45.8 2.4 collective-permute-start.8
  49.0 2.4 collective-permute-done.5
  51.5 4.7 %collective-permute-done.6 = bf16[4,32,1024]{2,1,0:T(8,128)(2,1)S(1)} collective-permute-done((bf16[4,32,1024]{2,1,0:T(8,128)(2,1)S(1)}, bf16[4,32,1024]{2,1,0:T(8,128)(2,1)S(1)}, u32[]{:S(2)}, u32[]{:S(2)}) %collective-permute-start.6) | collective-permute-done | bytes 262176 | tf_op jit(solution)/shard_map/ppermute | solution.py:183
  61.5 2.4 collective-permute-start.11
  64.0 13.5 %all_to_all.20 = f32[16,1,512]{2,1,0:T(1,128)S(1)} all-to-all(f32[16,1,512]{2,1,0:T(1,128)S(1)} %reshape.162), channel_id=1, replica_groups=mesh['member'=16,'pair'=2] {'member'}, dimensions={0} | all-to-all | bytes 65536 | tf_op jit(solution)/shard_map/all_to_all | solution.py:178
  79.6 6.3 %all-to-all-start.2 = ((bf16[16,104,1024]{2,1,0:T(8,128)(2,1)}), bf16[16,104,1024]{2,1,0:T(8,128)(2,1)S(1)}, u32[]{:S(2)}, u32[]{:S(2)}) async-start(bf16[16,104,1024]{2,1,0:T(8,128)(2,1)} %pad_maximum_fusion.1), calls=%async_computation.2 | async-start | bytes 6815744 | tf_op jit(solution)/shard_map/all_to_all | solution.py:178
  87.6 2.3 pad_maximum_fusion.2.x_ref
  112.4 1.9 fusion.1.spread_b_ref
  114.3 1.7 pad_maximum_fusion.9
  116.0 2.1 collective-permute-done.13
  118.1 7.1 %collective-permute-done.12 = bf16[4,32,1024]{2,1,0:T(8,128)(2,1)} collective-permute-done((bf16[4,32,1024]{2,1,0:T(8,128)(2,1)}, bf16[4,32,1024]{2,1,0:T(8,128)(2,1)}, u32[]{:S(2)}, u32[]{:S(2)}) %collective-permute-start.12) | collective-permute-done | bytes 262176 | tf_op jit(solution)/shard_map/ppermute | solution.py:183
  125.2 2.3 pad_maximum_fusion.3
  127.4 10.9 %collective-permute-done.15 = bf16[4,32,1024]{2,1,0:T(8,128)(2,1)} collective-permute-done((bf16[4,32,1024]{2,1,0:T(8,128)(2,1)}, bf16[4,32,1024]{2,1,0:T(8,128)(2,1)}, u32[]{:S(2)}, u32[]{:S(2)}) %collective-permute-start.15) | collective-permute-done | bytes 262176 | tf_op jit(solution)/shard_map/ppermute | solution.py:183
  138.3 9.4 %collective-permute-done.17 = bf16[4,32,1024]{2,1,0:T(8,128)(2,1)} collective-permute-done((bf16[4,32,1024]{2,1,0:T(8,128)(2,1)}, bf16[4,32,1024]{2,1,0:T(8,128)(2,1)}, u32[]{:S(2)}, u32[]{:S(2)}) %collective-permute-start.17) | collective-permute-done | bytes 262176 | tf_op jit(solution)/shard_map/ppermute | solution.py:183
  147.7 16.0 %all-to-all-done.2.b_ref = bf16[16,104,1024]{2,1,0:T(8,128)(2,1)S(1)} async-done(((bf16[16,104,1024]{2,1,0:T(8,128)(2,1)}), bf16[16,104,1024]{2,1,0:T(8,128)(2,1)S(1)}, u32[]{:S(2)}, u32[]{:S(2)}) %all-to-all-start.2) | async-done | bytes 3407904 | tf_op jit(solution)/shard_map/all_to_all | solution.py:178
  165.6 1.9 collective-permute-start.19
  167.5 1.7 collective-permute-start.20
  171.2 4.1 %shard_map.131 = bf16[16,128,1024]{2,1,0:T(8,128)(2,1)S(1)} custom-call(bf16[256,256]{1,0:T(8,128)(2,1)S(1)} %fusion.spread_c_ref, bf16[256,256]{1,0:T(8,128)(2,1)S(1)} %copy-done.5, bf16[16,32,1024]{2,1,0:T(8,128)(2,1)S(1)} %pad_maximum_fusion.4.c_ref, bf16[16,104,1024]{2,1,0:T(8,128)(2,1)S(1)} %all-to-all-done.2.b_ref), custom_call_target="tpu_custom_call" | custom-call | flops 1 | bytes 1 | tf_op jit(solution)/shard_map/pallas_call | solution.py:94
  175.4 2.6 pad_maximum_fusion
  178.0 7.5 %collective-permute-done.19 = bf16[4,32,1024]{2,1,0:T(8,128)(2,1)} collective-permute-done((bf16[4,32,1024]{2,1,0:T(8,128)(2,1)S(1)}, bf16[4,32,1024]{2,1,0:T(8,128)(2,1)}, u32[]{:S(2)}, u32[]{:S(2)}) %collective-permute-start.19) | collective-permute-done | bytes 262176 | tf_op jit(solution)/shard_map/ppermute | solution.py:183
  185.5 5.6 %collective-permute-done.20 = bf16[4,32,1024]{2,1,0:T(8,128)(2,1)} collective-permute-done((bf16[4,32,1024]{2,1,0:T(8,128)(2,1)S(1)}, bf16[4,32,1024]{2,1,0:T(8,128)(2,1)}, u32[]{:S(2)}, u32[]{:S(2)}) %collective-permute-start.20) | collective-permute-done | bytes 262176 | tf_op jit(solution)/shard_map/ppermute | solution.py:183
  191.0 5.7 %all-to-all-start.3 = ((bf16[16,136,1024]{2,1,0:T(8,128)(2,1)}), bf16[16,136,1024]{2,1,0:T(8,128)(2,1)}, u32[]{:S(2)}, u32[]{:S(2)}) async-start(bf16[16,136,1024]{2,1,0:T(8,128)(2,1)} %pad_maximum_fusion), calls=%async_computation.3 | async-start | bytes 8912896 | tf_op jit(solution)/shard_map/all_to_all | solution.py:178
  199.8 94.6 %all-to-all-done.3 = bf16[16,136,1024]{2,1,0:T(8,128)(2,1)} async-done(((bf16[16,136,1024]{2,1,0:T(8,128)(2,1)}), bf16[16,136,1024]{2,1,0:T(8,128)(2,1)}, u32[]{:S(2)}, u32[]{:S(2)}) %all-to-all-start.3) | async-done | bytes 4456480 | tf_op jit(solution)/shard_map/all_to_all | solution.py:178
  298.4 4.8 %slice.220 = bf16[16,128,1024]{2,1,0:T(8,128)(2,1)} slice(bf16[16,136,1024]{2,1,0:T(8,128)(2,1)} %all-to-all-done.3), slice={[0:16], [0:128], [0:1024]} | slice | bytes 8388608 | tf_op jit(solution)/shard_map/slice | solution.py:315
  (166 shorter events, 59.0 us)
Async XLA Ops:
  3.6 7.1 %copy-start.3 = (bf16[1,1024,64]{1,2,0:T(8,128)(2,1)S(1)}, bf16[1,1024,64]{1,2,0:T(8,128)(2,1)}, u32[]{:S(2)}) copy-start(bf16[1,1024,64]{1,2,0:T(8,128)(2,1)} %param.14) | copy-start | bytes 393220
  5.4 9.5 %collective-permute-start = (bf16[512,1024]{1,0:T(8,128)(2,1)S(1)}, bf16[512,1024]{1,0:T(8,128)(2,1)S(1)}, u32[]{:S(2)}, u32[]{:S(2)}) collective-permute-start(bf16[512,1024]{1,0:T(8,128)(2,1)S(1)} %shard_map.128.mine_ref), channel_id=1, source_target_pairs={{0,1},{1,0},{2,3},{3,2},{4,5},{5,4},{6,7},{7,6},{8,9},{9,8},{10,11... | collective-permute-start | bytes 3145736 | tf_op jit(solution)/shard_map/ppermute | solution.py:183
  6.8 19.7 %collective-permute-start.2 = (bf16[4,32,1024]{2,1,0:T(8,128)(2,1)S(1)}, bf16[4,32,1024]{2,1,0:T(8,128)(2,1)}, u32[]{:S(2)}, u32[]{:S(2)}) collective-permute-start(bf16[4,32,1024]{2,1,0:T(8,128)(2,1)S(1)} %get-tuple-element.102), channel_id=1, source_target_pairs={{0,8},{2,10},{4,12},{6,14},{8,0},{10,2},{12,4},{14,6},{16,24},{18,... | collective-permute-start | bytes 786440 | tf_op jit(solution)/shard_map/ppermute | solution.py:183
  7.3 20.5 %collective-permute-start.3 = (bf16[4,32,1024]{2,1,0:T(8,128)(2,1)S(1)}, bf16[4,32,1024]{2,1,0:T(8,128)(2,1)}, u32[]{:S(2)}, u32[]{:S(2)}) collective-permute-start(bf16[4,32,1024]{2,1,0:T(8,128)(2,1)S(1)} %get-tuple-element.101), channel_id=1, source_target_pairs={{0,16},{2,18},{4,20},{6,22},{8,24},{10,26},{12,28},{14,30},{16,0},... | collective-permute-start | bytes 786440 | tf_op jit(solution)/shard_map/ppermute | solution.py:183
  9.9 23.8 %collective-permute-start.4 = (bf16[4,32,1024]{2,1,0:T(8,128)(2,1)S(1)}, bf16[4,32,1024]{2,1,0:T(8,128)(2,1)}, u32[]{:S(2)}, u32[]{:S(2)}) collective-permute-start(bf16[4,32,1024]{2,1,0:T(8,128)(2,1)S(1)} %get-tuple-element.100), channel_id=1, source_target_pairs={{0,24},{2,26},{4,28},{6,30},{8,16},{10,18},{12,20},{14,22},{16,8},... | collective-permute-start | bytes 786440 | tf_op jit(solution)/shard_map/ppermute | solution.py:183
  21.9 3.6 %collective-permute-start.1 = (f32[64,256]{1,0:T(8,128)S(1)}, f32[64,256]{1,0:T(8,128)S(1)}, u32[]{:S(2)}, u32[]{:S(2)}) collective-permute-start(f32[64,256]{1,0:T(8,128)S(1)} %constant_dynamic-slice_fusion.33), channel_id=1, source_target_pairs={{0,1},{1,0},{2,3},{3,2},{4,5},{5,4},{6,7},{7,6},{8,9},{9,8},{10,11... | collective-permute-start | bytes 196616 | tf_op jit(solution)/shard_map/ppermute | solution.py:183
  33.7 15.3 %all-to-all-start = ((f32[16,2,1024]{2,1,0:T(2,128)}), f32[16,2,1024]{2,1,0:T(2,128)S(1)}, u32[]{:S(2)}, u32[]{:S(2)}) async-start(f32[16,2,1024]{2,1,0:T(2,128)} %pad_maximum_fusion.17), calls=%async_computation | async-start | bytes 262144 | tf_op jit(solution)/shard_map/all_to_all | solution.py:178
  42.0 9.4 %collective-permute-start.5 = (bf16[4,32,1024]{2,1,0:T(8,128)(2,1)S(1)}, bf16[4,32,1024]{2,1,0:T(8,128)(2,1)S(1)}, u32[]{:S(2)}, u32[]{:S(2)}) collective-permute-start(bf16[4,32,1024]{2,1,0:T(8,128)(2,1)S(1)} %pad_maximum_fusion.6), channel_id=1, source_target_pairs={{0,2},{2,0},{4,6},{6,4},{8,10},{10,8},{12,14},{14,12},{16,18},{18,... | collective-permute-start | bytes 786440 | tf_op jit(solution)/shard_map/ppermute | solution.py:183
  43.6 12.5 %collective-permute-start.6 = (bf16[4,32,1024]{2,1,0:T(8,128)(2,1)S(1)}, bf16[4,32,1024]{2,1,0:T(8,128)(2,1)S(1)}, u32[]{:S(2)}, u32[]{:S(2)}) collective-permute-start(bf16[4,32,1024]{2,1,0:T(8,128)(2,1)S(1)} %pad_maximum_fusion.7), channel_id=1, source_target_pairs={{0,4},{2,6},{4,0},{6,2},{8,12},{10,14},{12,8},{14,10},{16,20},{18,... | collective-permute-start | bytes 786440 | tf_op jit(solution)/shard_map/ppermute | solution.py:183
  44.3 11.9 %collective-permute-start.7 = (bf16[4,32,1024]{2,1,0:T(8,128)(2,1)S(1)}, bf16[4,32,1024]{2,1,0:T(8,128)(2,1)}, u32[]{:S(2)}, u32[]{:S(2)}) collective-permute-start(bf16[4,32,1024]{2,1,0:T(8,128)(2,1)S(1)} %pad_maximum_fusion.8), channel_id=1, source_target_pairs={{0,6},{2,4},{4,2},{6,0},{8,14},{10,12},{12,10},{14,8},{16,22},{18,... | collective-permute-start | bytes 786440 | tf_op jit(solution)/shard_map/ppermute | solution.py:183
  45.8 11.7 %collective-permute-start.8 = (bf16[4,32,1024]{2,1,0:T(8,128)(2,1)S(1)}, bf16[4,32,1024]{2,1,0:T(8,128)(2,1)S(1)}, u32[]{:S(2)}, u32[]{:S(2)}) collective-permute-start(bf16[4,32,1024]{2,1,0:T(8,128)(2,1)S(1)} %dynamic-slice_bitcast_fusion.3), channel_id=1, source_target_pairs={{0,16},{2,18},{4,20},{6,22},{8,24},{10,26},{12,28},{14,30},{16,0},... | collective-permute-start | bytes 786440 | tf_op jit(solution)/shard_map/ppermute | solution.py:183
  51.5 27.4 %copy-start.19 = (bf16[4,32,1024]{2,1,0:T(8,128)(2,1)}, bf16[4,32,1024]{2,1,0:T(8,128)(2,1)S(1)}, u32[]{:S(2)}) copy-start(bf16[4,32,1024]{2,1,0:T(8,128)(2,1)S(1)} %collective-permute-done.5) | copy-start | bytes 786436
  56.1 22.8 %copy-start.20 = (bf16[4,32,1024]{2,1,0:T(8,128)(2,1)}, bf16[4,32,1024]{2,1,0:T(8,128)(2,1)S(1)}, u32[]{:S(2)}) copy-start(bf16[4,32,1024]{2,1,0:T(8,128)(2,1)S(1)} %collective-permute-done.6) | copy-start | bytes 786436
  57.9 1.2 collective-permute-start.9
  59.9 18.9 %collective-permute-start.10 = (bf16[4,32,1024]{2,1,0:T(8,128)(2,1)S(1)}, bf16[4,32,1024]{2,1,0:T(8,128)(2,1)S(1)}, u32[]{:S(2)}, u32[]{:S(2)}) collective-permute-start(bf16[4,32,1024]{2,1,0:T(8,128)(2,1)S(1)} %get-tuple-element.95), channel_id=1, source_target_pairs={{0,8},{2,10},{4,12},{6,14},{8,0},{10,2},{12,4},{14,6},{16,24},{18,... | collective-permute-start | bytes 786440 | tf_op jit(solution)/shard_map/ppermute | solution.py:183
  61.5 17.3 %collective-permute-start.11 = (bf16[4,32,1024]{2,1,0:T(8,128)(2,1)S(1)}, bf16[4,32,1024]{2,1,0:T(8,128)(2,1)S(1)}, u32[]{:S(2)}, u32[]{:S(2)}) collective-permute-start(bf16[4,32,1024]{2,1,0:T(8,128)(2,1)S(1)} %get-tuple-element.94), channel_id=1, source_target_pairs={{0,24},{2,26},{4,28},{6,30},{8,16},{10,18},{12,20},{14,22},{16,8},... | collective-permute-start | bytes 786440 | tf_op jit(solution)/shard_map/ppermute | solution.py:183
  79.6 84.0 %all-to-all-start.2 = ((bf16[16,104,1024]{2,1,0:T(8,128)(2,1)}), bf16[16,104,1024]{2,1,0:T(8,128)(2,1)S(1)}, u32[]{:S(2)}, u32[]{:S(2)}) async-start(bf16[16,104,1024]{2,1,0:T(8,128)(2,1)} %pad_maximum_fusion.1), calls=%async_computation.2 | async-start | bytes 6815744 | tf_op jit(solution)/shard_map/all_to_all | solution.py:178
  96.0 13.5 %copy-start.24 = (s32[256]{0:T(256)S(1)}, s32[256]{0:T(256)}, u32[]{:S(2)}) copy-start(s32[256]{0:T(256)} %get-tuple-element.147) | copy-start | bytes 3076
  97.3 7.4 %copy-start.9 = (bf16[4,32,1024]{2,1,0:T(8,128)(2,1)S(1)}, bf16[4,32,1024]{2,1,0:T(8,128)(2,1)}, u32[]{:S(2)}) copy-start(bf16[4,32,1024]{2,1,0:T(8,128)(2,1)} %get-tuple-element.58) | copy-start | bytes 786436
  99.2 13.0 %collective-permute-start.14 = (bf16[4,32,1024]{2,1,0:T(8,128)(2,1)}, bf16[4,32,1024]{2,1,0:T(8,128)(2,1)}, u32[]{:S(2)}, u32[]{:S(2)}) collective-permute-start(bf16[4,32,1024]{2,1,0:T(8,128)(2,1)} %get-tuple-element.97), channel_id=1, source_target_pairs={{0,6},{2,4},{4,2},{6,0},{8,14},{10,12},{12,10},{14,8},{16,22},{18,... | collective-permute-start | bytes 786440 | tf_op jit(solution)/shard_map/ppermute | solution.py:183
  100.7 17.4 %collective-permute-start.13 = (bf16[4,32,1024]{2,1,0:T(8,128)(2,1)}, bf16[4,32,1024]{2,1,0:T(8,128)(2,1)}, u32[]{:S(2)}, u32[]{:S(2)}) collective-permute-start(bf16[4,32,1024]{2,1,0:T(8,128)(2,1)} %get-tuple-element.98), channel_id=1, source_target_pairs={{0,4},{2,6},{4,0},{6,2},{8,12},{10,14},{12,8},{14,10},{16,20},{18,... | collective-permute-start | bytes 786440 | tf_op jit(solution)/shard_map/ppermute | solution.py:183
  102.1 23.0 %collective-permute-start.12 = (bf16[4,32,1024]{2,1,0:T(8,128)(2,1)}, bf16[4,32,1024]{2,1,0:T(8,128)(2,1)}, u32[]{:S(2)}, u32[]{:S(2)}) collective-permute-start(bf16[4,32,1024]{2,1,0:T(8,128)(2,1)} %get-tuple-element.99), channel_id=1, source_target_pairs={{0,2},{2,0},{4,6},{6,4},{8,10},{10,8},{12,14},{14,12},{16,18},{18,... | collective-permute-start | bytes 786440 | tf_op jit(solution)/shard_map/ppermute | solution.py:183
  106.0 32.3 %collective-permute-start.15 = (bf16[4,32,1024]{2,1,0:T(8,128)(2,1)}, bf16[4,32,1024]{2,1,0:T(8,128)(2,1)}, u32[]{:S(2)}, u32[]{:S(2)}) collective-permute-start(bf16[4,32,1024]{2,1,0:T(8,128)(2,1)} %pad_maximum_fusion.10), channel_id=1, source_target_pairs={{0,2},{2,0},{4,6},{6,4},{8,10},{10,8},{12,14},{14,12},{16,18},{18,... | collective-permute-start | bytes 786440 | tf_op jit(solution)/shard_map/ppermute | solution.py:183
  108.2 30.1 %collective-permute-start.16 = (bf16[4,32,1024]{2,1,0:T(8,128)(2,1)}, bf16[4,32,1024]{2,1,0:T(8,128)(2,1)}, u32[]{:S(2)}, u32[]{:S(2)}) collective-permute-start(bf16[4,32,1024]{2,1,0:T(8,128)(2,1)} %pad_maximum_fusion.11), channel_id=1, source_target_pairs={{0,4},{2,6},{4,0},{6,2},{8,12},{10,14},{12,8},{14,10},{16,20},{18,... | collective-permute-start | bytes 786440 | tf_op jit(solution)/shard_map/ppermute | solution.py:183
  112.2 35.4 %collective-permute-start.17 = (bf16[4,32,1024]{2,1,0:T(8,128)(2,1)}, bf16[4,32,1024]{2,1,0:T(8,128)(2,1)}, u32[]{:S(2)}, u32[]{:S(2)}) collective-permute-start(bf16[4,32,1024]{2,1,0:T(8,128)(2,1)} %pad_maximum_fusion.12), channel_id=1, source_target_pairs={{0,6},{2,4},{4,2},{6,0},{8,14},{10,12},{12,10},{14,8},{16,22},{18,... | collective-permute-start | bytes 786440 | tf_op jit(solution)/shard_map/ppermute | solution.py:183
  163.6 7.6 %copy-start.5 = (bf16[256,256]{1,0:T(8,128)(2,1)S(1)}, bf16[256,256]{1,0:T(8,128)(2,1)}, u32[]{:S(2)}) copy-start(bf16[256,256]{1,0:T(8,128)(2,1)} %fusion.1.spread_b_ref) | copy-start | bytes 393220
  165.5 12.6 %collective-permute-start.18 = (bf16[4,32,1024]{2,1,0:T(8,128)(2,1)S(1)}, bf16[4,32,1024]{2,1,0:T(8,128)(2,1)}, u32[]{:S(2)}, u32[]{:S(2)}) collective-permute-start(bf16[4,32,1024]{2,1,0:T(8,128)(2,1)S(1)} %pad_maximum_fusion.14), channel_id=1, source_target_pairs={{0,8},{2,10},{4,12},{6,14},{8,0},{10,2},{12,4},{14,6},{16,24},{18,... | collective-permute-start | bytes 786440 | tf_op jit(solution)/shard_map/ppermute | solution.py:183
  165.6 19.9 %collective-permute-start.19 = (bf16[4,32,1024]{2,1,0:T(8,128)(2,1)S(1)}, bf16[4,32,1024]{2,1,0:T(8,128)(2,1)}, u32[]{:S(2)}, u32[]{:S(2)}) collective-permute-start(bf16[4,32,1024]{2,1,0:T(8,128)(2,1)S(1)} %pad_maximum_fusion.15), channel_id=1, source_target_pairs={{0,16},{2,18},{4,20},{6,22},{8,24},{10,26},{12,28},{14,30},{16,0},... | collective-permute-start | bytes 786440 | tf_op jit(solution)/shard_map/ppermute | solution.py:183
  167.5 23.5 %collective-permute-start.20 = (bf16[4,32,1024]{2,1,0:T(8,128)(2,1)S(1)}, bf16[4,32,1024]{2,1,0:T(8,128)(2,1)}, u32[]{:S(2)}, u32[]{:S(2)}) collective-permute-start(bf16[4,32,1024]{2,1,0:T(8,128)(2,1)S(1)} %pad_maximum_fusion.16), channel_id=1, source_target_pairs={{0,24},{2,26},{4,28},{6,30},{8,16},{10,18},{12,20},{14,22},{16,8},... | collective-permute-start | bytes 786440 | tf_op jit(solution)/shard_map/ppermute | solution.py:183
  178.0 18.9 %copy-start.10 = (bf16[4,32,1024]{2,1,0:T(8,128)(2,1)S(1)}, bf16[4,32,1024]{2,1,0:T(8,128)(2,1)}, u32[]{:S(2)}) copy-start(bf16[4,32,1024]{2,1,0:T(8,128)(2,1)} %pad_maximum_fusion.13) | copy-start | bytes 786436
  191.0 103.4 %all-to-all-start.3 = ((bf16[16,136,1024]{2,1,0:T(8,128)(2,1)}), bf16[16,136,1024]{2,1,0:T(8,128)(2,1)}, u32[]{:S(2)}, u32[]{:S(2)}) async-start(bf16[16,136,1024]{2,1,0:T(8,128)(2,1)} %pad_maximum_fusion), calls=%async_computation.3 | async-start | bytes 8912896 | tf_op jit(solution)/shard_map/all_to_all | solution.py:178
  199.8 103.4 %copy-start.11 = (bf16[1,512,1024]{2,1,0:T(8,128)(2,1)}, bf16[1,512,1024]{2,1,0:T(8,128)(2,1)S(1)}, u32[]{:S(2)}) copy-start(bf16[1,512,1024]{2,1,0:T(8,128)(2,1)S(1)} %bitcast_dynamic-update-slice_fusion) | copy-start | bytes 3145732
  (17 other events, 55.8 us)

commit v2 on v1

v2 whole, which is shorter than its diff:
```python
import functools

import jax
import jax.numpy as jnp
from jax import lax
from jax.experimental import pallas as pl
from jax.experimental.pallas import tpu as pltpu
from jax.sharding import PartitionSpec as P

ROWS = 16
PLANE = 4
TILE = 256
VMEM = 56 << 20
LIGHT = pl.CostEstimate(flops=1, bytes_accessed=1, transcendentals=0)


def solve_gain(amat, bmat):
    count = amat.shape[0]
    system = amat + count * jnp.eye(count, dtype=jnp.float32)
    factor = jnp.linalg.cholesky(system)
    middle = lax.linalg.triangular_solve(
        factor, bmat, left_side=True, lower=True, transpose_a=False
    )
    return lax.linalg.triangular_solve(factor, middle, left_side=True, lower=True, transpose_a=True)


def mix_kernel(spread_ref, x_ref, y_ref):
    members, rows, width = x_ref.shape
    for at in range(0, rows, ROWS):
        for left in range(0, width, TILE):
            piece = (slice(None), pl.ds(at, ROWS), pl.ds(left, TILE))
            full = x_ref[piece].astype(jnp.float32)
            mean = jnp.sum(full, axis=0, keepdims=True) * (1.0 / members)
            center = (full - mean).astype(jnp.bfloat16).reshape(members * ROWS, TILE)
            mixed = jnp.dot(spread_ref[...], center, preferred_element_type=jnp.float32)
            y_ref[piece] = mixed.astype(jnp.bfloat16).reshape(members, ROWS, TILE)


def copy_kernel(x_ref, y_ref):
    y_ref[...] = x_ref[...]


def blocked(kernel, x, *wholes):
    members, total, width = x.shape
    rows = min(total, 4 * ROWS)
    block = pl.BlockSpec((members, rows, width), lambda i: (0, i, 0))
    return pl.pallas_call(
        kernel,
        grid=(total // rows,),
        in_specs=[pl.BlockSpec(w.shape, lambda i: (0, 0)) for w in wholes] + [block],
        out_specs=block,
        out_shape=jax.ShapeDtypeStruct(x.shape, jnp.bfloat16),
        compiler_params=pltpu.CompilerParams(vmem_limit_bytes=VMEM),
        cost_estimate=LIGHT,
    )(*wholes, x)


def moments_kernel(both_ref, var_ref, sums_ref):
    pred, resid = both_ref[:, 0, :], both_ref[:, 1, :]
    dev = pred - jnp.sum(pred, axis=0, keepdims=True) * (1.0 / pred.shape[0])
    scaled = dev / var_ref[...]
    sums_ref[...] = lax.dot_general(
        scaled,
        jnp.concatenate([dev, resid], axis=0),
        (((1,), (1,)), ((), ())),
        precision=lax.Precision.HIGHEST,
        preferred_element_type=jnp.float32,
    )


def whole_call(kernel, out_shape, *args):
    return pl.pallas_call(kernel, out_shape=out_shape, cost_estimate=LIGHT)(*args)


def solve_kernel(sums_ref, gain_ref, spread_ref):
    total = sums_ref[...]
    count = total.shape[0]
    row = lax.broadcasted_iota(jnp.int32, total.shape, 0)
    col = lax.broadcasted_iota(jnp.int32, total.shape, 1)
    total = total + jnp.where(row == col, float(count), 0.0)
    for k in range(count):
        pivot = total[k : k + 1, :] / total[k : k + 1, k : k + 1]
        factor = jnp.where(row == k, total - 1.0, total)[:, k : k + 1]
        total = total - factor * pivot
    gain = total[:, count:].astype(jnp.bfloat16)
    gain_ref[...] = gain
    size = count * ROWS
    row = lax.broadcasted_iota(jnp.int32, (size, count), 0)
    col = lax.broadcasted_iota(jnp.int32, (size, count), 1)
    expand = (row // ROWS == col).astype(jnp.bfloat16)
    wide = lax.dot_general(
        expand, gain, (((1,), (1,)), ((), ())), preferred_element_type=jnp.float32
    ).astype(jnp.bfloat16)
    wide = lax.dot_general(
        wide, expand, (((1,), (1,)), ((), ())), preferred_element_type=jnp.float32
    )
    at_row = lax.broadcasted_iota(jnp.int32, (size, size), 0) % ROWS
    at_col = lax.broadcasted_iota(jnp.int32, (size, size), 1) % ROWS
    spread_ref[...] = jnp.where(at_row == at_col, wide, 0.0).astype(jnp.bfloat16)


def spread_gain(gain_tr):
    members = gain_tr.shape[0]
    size = members * ROWS
    row = lax.broadcasted_iota(jnp.int32, (size, members), 0)
    col = lax.broadcasted_iota(jnp.int32, (size, members), 1)
    expand = (row // ROWS == col).astype(jnp.bfloat16)
    wide = jnp.dot(expand, gain_tr, preferred_element_type=jnp.float32).astype(jnp.bfloat16)
    wide = lax.dot_general(
        wide, expand, (((1,), (1,)), ((), ())), preferred_element_type=jnp.float32
    ).astype(jnp.bfloat16)
    at_row = lax.broadcasted_iota(jnp.int32, (size, size), 0) % ROWS
    at_col = lax.broadcasted_iota(jnp.int32, (size, size), 1) % ROWS
    return jnp.where(at_row == at_col, wide, jnp.bfloat16(0))


def mix_plain(slab, gain_tr):
    full = slab.astype(jnp.float32)
    center = (full - jnp.mean(full, axis=0, keepdims=True)).astype(jnp.bfloat16)
    return jnp.einsum(
        "jk,krc->jrc", gain_tr, center, preferred_element_type=jnp.float32
    ).astype(jnp.bfloat16)


def mix_one_kernel(column_ref, *refs):
    y_ref = refs[-1]
    blocks = [ref[...].astype(jnp.float32) for ref in refs[:-1]]
    members = column_ref.shape[0]
    mean = sum(jnp.sum(block, axis=0) for block in blocks) * (1.0 / members)
    total = jnp.zeros_like(mean)
    at = 0
    for block in blocks:
        for i in range(block.shape[0]):
            center = (block[i] - mean).astype(jnp.bfloat16).astype(jnp.float32)
            total = total + center * column_ref[at]
            at += 1
    y_ref[...] = total.astype(jnp.bfloat16)


def mix_one(column, blocks):
    rows, width = blocks[0].shape[1:]
    step = rows if rows % ROWS else ROWS
    return pl.pallas_call(
        mix_one_kernel,
        grid=(rows // step,),
        in_specs=[pl.BlockSpec(memory_space=pltpu.SMEM)]
        + [pl.BlockSpec((x.shape[0], step, width), lambda i: (0, i, 0)) for x in blocks],
        out_specs=pl.BlockSpec((step, width), lambda i: (i, 0)),
        out_shape=jax.ShapeDtypeStruct((rows, width), jnp.bfloat16),
        compiler_params=pltpu.CompilerParams(vmem_limit_bytes=VMEM),
        cost_estimate=LIGHT,
    )(column, *blocks)


def first_kernel(scale, x_ref, w_ref, b_ref, y_ref):
    summed = jnp.dot(x_ref[...], w_ref[...], preferred_element_type=jnp.float32)
    y = jax.nn.gelu(summed * scale + b_ref[...].astype(jnp.float32), approximate=True)
    y_ref[...] = y.astype(jnp.bfloat16)


def first_layer(x, w, b, part):
    rows, depth = x.shape
    half = w.shape[1] // 2
    step = min(TILE, half)
    first = part * (half // step)
    return pl.pallas_call(
        functools.partial(first_kernel, depth ** (-0.5)),
        grid=(half // step,),
        in_specs=[
            pl.BlockSpec((rows, depth), lambda i: (0, 0)),
            pl.BlockSpec((depth, step), lambda i: (0, i + first)),
            pl.BlockSpec((1, step), lambda i: (0, i + first)),
        ],
        out_specs=pl.BlockSpec((rows, step), lambda i: (0, i)),
        out_shape=jax.ShapeDtypeStruct((rows, half), jnp.bfloat16),
        compiler_params=pltpu.CompilerParams(vmem_limit_bytes=32 << 20),
        cost_estimate=LIGHT,
    )(x, w, b)


def second_kernel(scale, side_ref, *refs):
    inputs, weights, (b_ref, third_ref, y_ref) = refs[:4], refs[4:8], refs[8:]
    summed = sum(
        jnp.dot(x_ref[...], w_ref[...], preferred_element_type=jnp.float32)
        for x_ref, w_ref in zip(inputs, weights)
    )
    y = jax.nn.gelu(summed * scale + b_ref[...].astype(jnp.float32), approximate=True)
    part = lax.dot_general(
        third_ref[...],
        y.astype(jnp.bfloat16),
        (((1,), (1,)), ((), ())),
        preferred_element_type=jnp.float32,
    )

    @pl.when(pl.program_id(0) == 0)
    def _():
        y_ref[...] = jnp.zeros_like(y_ref)

    y_ref[...] += part * scale


def second_and_third(side, mine, other, w, b, third):
    rows, depth = mine[0].shape
    outs = third.shape[0]
    step = min(TILE, w.shape[1])
    whole = pl.BlockSpec((rows, depth), lambda i, side: (0, 0))
    return pl.pallas_call(
        functools.partial(second_kernel, w.shape[0] ** (-0.5)),
        grid_spec=pltpu.PrefetchScalarGridSpec(
            num_scalar_prefetch=1,
            grid=(w.shape[1] // step,),
            in_specs=[whole] * 4
            + [
                pl.BlockSpec((depth, step), lambda i, side: (2 * side[0], i)),
                pl.BlockSpec((depth, step), lambda i, side: (2 * side[0] + 1, i)),
                pl.BlockSpec((depth, step), lambda i, side: (2 - 2 * side[0], i)),
                pl.BlockSpec((depth, step), lambda i, side: (3 - 2 * side[0], i)),
                pl.BlockSpec((1, step), lambda i, side: (0, i)),
                pl.BlockSpec((outs, step), lambda i, side: (0, i)),
            ],
            out_specs=pl.BlockSpec((outs, rows), lambda i, side: (0, 0)),
        ),
        out_shape=jax.ShapeDtypeStruct((outs, rows), jnp.float32),
        compiler_params=pltpu.CompilerParams(vmem_limit_bytes=32 << 20),
        cost_estimate=LIGHT,
    )(side[None], *mine, *other, w, w, w, w, b, third)


def exchange(x):
    return lax.all_to_all(x, "member", split_axis=0, concat_axis=0, tiled=True)


def swap(x, axis, bit):
    count = lax.axis_size(axis)
    return lax.ppermute(x, axis, [(i, i ^ bit) for i in range(count)])


def reorder(gain_tr, order):
    pick = (order[None, :] == jnp.arange(gain_tr.shape[1])[:, None]).astype(jnp.bfloat16)
    return jnp.dot(gain_tr, pick, preferred_element_type=jnp.float32).astype(jnp.bfloat16)


def pick(x, at, axis=0):
    return lax.dynamic_index_in_dim(x, at, axis, keepdims=False)


def after(value, earlier):
    return lax.optimization_barrier((value, earlier))[0]


def body(samples, w_first, b_first, w_second, b_second, w_third, observed, perturb, variance):
    members = lax.axis_size("member")
    me = lax.axis_index("member")
    side = lax.axis_index("pair")
    width = w_first.shape[2]
    first_w, second_w, third_w = w_first[0], w_second[0], w_third[0]
    slabs_first = first_w.reshape(members, -1, width)
    slabs_second = second_w.reshape(members, -1, width)
    outs = third_w.shape[1]
    fast = members == PLANE * PLANE and width % TILE == 0
    planes = members // PLANE
    plane, place = me // PLANE, me % PLANE

    def across(x, flip):
        return swap(x, "member", flip * PLANE)

    first = [first_layer(samples, first_w, b_first, i) for i in range(2)]
    other = [swap(x, "pair", 1) for x in first]
    partial_out = second_and_third(side, first, other, second_w, b_second, third_w.T)

    half = partial_out.shape[1] // 2
    start = side * half
    keep = lax.dynamic_slice_in_dim(partial_out, start, half, 1)
    give = lax.dynamic_slice_in_dim(partial_out, (1 - side) * half, half, 1)
    pred = keep + swap(give, "pair", 1)
    observed_half = lax.dynamic_slice_in_dim(observed.T, start, half, 1)
    variance_half = lax.dynamic_slice_in_dim(variance.T, start, half, 1)
    perturb_half = lax.dynamic_slice_in_dim(perturb[0].T, start, half, 1)
    resid = observed_half + jnp.sqrt(variance_half) * perturb_half - pred
    count = pred.size // members
    both = jnp.concatenate(
        [pred.reshape(members, 1, count), resid.reshape(members, 1, count)], axis=1
    )
    got_first = exchange(slabs_first)
    var_part = lax.dynamic_index_in_dim(variance_half.reshape(members, count), me, 0)
    if fast:
        both = both.reshape((planes, PLANE) + both.shape[1:])
        parts = [pick(both, plane ^ i) for i in range(planes)]
        parts = jnp.stack([parts[0]] + [across(parts[i], i) for i in range(1, planes)])
        pad = jnp.zeros((-(outs + 2) % 8, width), jnp.bfloat16)
        small = jnp.concatenate([third_w.T, b_first, b_second, pad], axis=0)[None]
        held = [small, swap(after(small, both), "member", 8)]
        slabs_second, parts, held[1], got_first = lax.optimization_barrier(
            (slabs_second, parts, held[1], got_first)
        )
        got_second = exchange(slabs_second)
        held.append(swap(jnp.concatenate(held, axis=0), "member", 4))
        both = jnp.stack([pick(parts, plane ^ i) for i in range(planes)])
        parts = [pick(both, place ^ i, 1) for i in range(PLANE)]
        parts = jnp.stack([parts[0]] + [swap(parts[i], "member", i) for i in range(1, PLANE)])
        both = jnp.stack([pick(parts, place ^ i) for i in range(PLANE)], axis=1)
        both = both.reshape((members,) + both.shape[2:])
        sums = whole_call(
            moments_kernel,
            jax.ShapeDtypeStruct((members, 2 * members), jnp.float32),
            both,
            var_part,
        )
        sums = sums + swap(sums, "pair", 1)
        sums = sums + swap(sums, "member", 1)
        sums = sums + swap(sums, "member", 2)
        held[2] = after(held[2], sums)
        held.append(swap(jnp.concatenate(held, axis=0), "member", 2))
        far = [across(sums, i) for i in range(1, planes)]
        sums, got_second = lax.optimization_barrier(
            ((sums + far[0]) + (far[1] + far[2]), got_second)
        )
        gain, spread = whole_call(
            solve_kernel,
            [
                jax.ShapeDtypeStruct((members, members), jnp.bfloat16),
                jax.ShapeDtypeStruct((members * ROWS, members * ROWS), jnp.bfloat16),
            ],
            sums,
        )
        mixed_second = blocked(mix_kernel, got_second, spread)
        mixed_second, got_first, held[3] = lax.optimization_barrier(
            (mixed_second, got_first, held[3])
        )
        new_second = exchange(mixed_second)

        mixed_first = blocked(mix_kernel, got_first, spread)
        mixed_first = mixed_first.reshape((planes, PLANE) + mixed_first.shape[1:])
        parts = [pick(mixed_first, place ^ i, 1) for i in range(PLANE)]
        parts = jnp.stack([parts[0]] + [swap(parts[i], "member", i) for i in range(1, PLANE)])
        held[3] = after(held[3], parts)
        held.append(swap(jnp.concatenate(held, axis=0), "member", 1))
        homes = []
        for flip in range(planes):
            block = jnp.stack([pick(pick(parts, place ^ i), plane ^ flip) for i in range(PLANE)])
            homes.append(across(block, flip) if flip else block)

        order = me[None]
        for bit in (8, 4, 2, 1):
            order = jnp.concatenate([order, order ^ bit])
        column = reorder(pick(gain, me, 1)[None], order)[0].astype(jnp.float32)
        new_small = mix_one(column, held)
        new_third = new_small[:outs].T
        new_bfirst = new_small[outs : outs + 1]
        new_bsecond = new_small[outs + 1 : outs + 2]
        new_second = blocked(copy_kernel, new_second)
        homes, new_second, new_third, new_bfirst, new_bsecond = lax.optimization_barrier(
            (homes, new_second, new_third, new_bfirst, new_bsecond)
        )
        new_first = jnp.zeros(slabs_first.shape, jnp.bfloat16)
        for flip, part in enumerate(homes):
            new_first = lax.dynamic_update_slice_in_dim(
                new_first, part, (plane ^ flip) * PLANE, 0
            )
    else:
        both = exchange(both)
        allpred, allres = both[:, 0], both[:, 1]
        devpred = allpred - jnp.mean(allpred, axis=0, keepdims=True)
        scaled = devpred / var_part
        sums = jnp.dot(
            scaled, jnp.concatenate([devpred, allres], axis=0).T, precision=lax.Precision.HIGHEST
        )
        sums = lax.psum(sums, ("member", "pair"))
        gain = solve_gain(sums[:, :members], sums[:, members:])
        gain_tr = gain.astype(jnp.bfloat16).T
        new_second = exchange(mix_plain(exchange(slabs_second), gain_tr))
        new_first = exchange(mix_plain(got_first, gain_tr))
        small = jnp.concatenate([third_w.T, b_first, b_second], axis=0)
        full = lax.all_gather(small, "member", axis=0)
        new_small = mix_plain(full, lax.dynamic_index_in_dim(gain_tr, me, 0))[0]
        new_third = new_small[:outs].T
        new_bfirst = new_small[outs : outs + 1]
        new_bsecond = new_small[outs + 1 :]
    return (
        new_first.reshape(w_first.shape),
        new_bfirst,
        new_second.reshape(w_second.shape),
        new_bsecond,
        new_third[None],
    )


def solution(mesh):
    in_specs = (
        P(),
        P("member", None, "pair"),
        P("member", "pair"),
        P("member", None, "pair"),
        P("member", "pair"),
        P("member", "pair", None),
        P(),
        P("member", None, None),
        P(),
    )
    out_specs = (
        P("member", None, "pair"),
        P("member", "pair"),
        P("member", None, "pair"),
        P("member", "pair"),
        P("member", "pair", None),
    )
    return jax.shard_map(body, mesh=mesh, in_specs=in_specs, out_specs=out_specs, check_vma=False)
```

time: 305 us -> 271 us (0.89)
  local copies, waits for them, and re-layouts: 34.9 us -> 10.1 us
  other arithmetic: 23.8 us -> 5.31 us
  starting transfers between devices: 41.2 us -> 57.2 us
  Pallas kernels: 11.5 us -> 26.8 us
  blocking collectives: 13.5 us -> 0 us
  matrix products: 5.74 us -> 0.64 us
    all_to_all x3, waiting for transfers between devices: 111 us -> 20.2 us  [exchange(): return lax.all_to_all(x, 'member', split_axis=0, concat_axis=0, tiled=True)]
    ppermute x21 -> x25, waiting for transfers between devices: 60.7 us -> 149 us  [swap(): return lax.ppermute(x, axis, [(i, i ^ bit) for i in range(count)])]
    pallas_call x3 -> x8, Pallas kernels: 6.82 us -> 22 us  [the longest x3 11.7 us: blocked(): pl.pallas_call(kernel, grid=(total // rows,), in_specs=[pl.BlockSpec(w.sh...]
    all_to_all x1 -> x0, blocking collectives: 13.5 us -> none  [exchange(): return lax.all_to_all(x, 'member', split_axis=0, concat_axis=0, tiled=True)]
    slice x8 -> x1, local copies, waits for them, and re-layouts: 14.4 us -> 1.4 us  [body(): new_bsecond = new_small[outs + 1:outs + 2]]
    ppermute x21 -> x25, starting transfers between devices: 23.1 us -> 36.1 us  [swap(): return lax.ppermute(x, axis, [(i, i ^ bit) for i in range(count)])]
    another operation x18 -> x9, other arithmetic: 11.8 us -> 3.29 us  [the longest x4 2.26 us: body(): jnp.stack([pick(pick(parts, place ^ i), plane ^ flip) for i in range(PLAN...]
    concatenate x5 -> x3, other arithmetic: 8.41 us -> 0.21 us  [the longest x1 0.12 us: body(): held.append(swap(jnp.concatenate(held, axis=0), 'member', 1))]
  transfers between devices with their start and end apart: 24 -> 28, of which waited for: 15 -> 18; matrix products, arithmetic and copies ran while one was open for 15% -> 4% of each run, Pallas kernels for 3% -> 10%
where the time goes in v2:
time: 271 us
  waiting for transfers between devices  170 us (63%)
  starting transfers between devices  57.2 us (21%)
  Pallas kernels  26.8 us (10%)
  local copies, waits for them, and re-layouts  10.1 us (4%)
  other arithmetic  5.31 us (2%)
    ppermute x25, waiting for transfers between devices, swap(): return lax.ppermute(x, axis, [(i, i ^ bit) for i in range(count)])  149 us
    ppermute x25, starting transfers between devices, swap(): return lax.ppermute(x, axis, [(i, i ^ bit) for i in range(count)])  36.1 us
    all_to_all x3, starting transfers between devices, exchange(): return lax.all_to_all(x, 'member', split_axis=0, concat_axis=0, tiled=True)  21 us
    all_to_all x3, waiting for transfers between devices, exchange(): return lax.all_to_all(x, 'member', split_axis=0, concat_axis=0, tiled=True)  20.2 us
    pallas_call x3, Pallas kernels, blocked(): pl.pallas_call(kernel, grid=(total // rows,), in_specs=[pl.BlockSpec(w.sh...  11.7 us
  transfers between devices with their start and end apart: 28, of which 18 were waited for; matrix products, arithmetic and copies ran while one was open for 4% of the time, Pallas kernels for 10%

profile of v2, /device:TPU:12, one launch (start us, length us, event | category | flops | bytes accessed | tf_op | source)
XLA Modules:
  0.0 270.5 jit_solution(4769377138347231345)
XLA Ops:
  0.7 7.3 %all-to-all-start = ((bf16[16,32,1024]{2,1,0:T(8,128)(2,1)}), bf16[16,32,1024]{2,1,0:T(8,128)(2,1)}, u32[]{:S(2)}, u32[]{:S(2)}) async-start(bf16[16,32,1024]{2,1,0:T(8,128)(2,1)} %bitcast.117), calls=%async_computation | async-start | bytes 2097152 | tf_op jit(solution)/shard_map/all_to_all | solution.py:230
  12.0 2.2 copy-done
  14.2 4.8 %shard_map.130 = f32[64,512]{1,0:T(8,128)S(1)} custom-call(s32[1]{0:T(128)} %bitcast.1.side_ref, bf16[512,512]{1,0:T(8,128)(2,1)S(1)} %shard_map.128.refs_0_, bf16[512,512]{1,0:T(8,128)(2,1)S(1)} %shard_map.129.refs_1_, bf16[512,512]{1,0:T(8,128)(2,1)S(1)} %collective-permute-done.refs_2_, bf16[512,512]{1,0:T(8,128)(2,1)S(1)} %collective-permute-done.1.refs_3_, ...), custom_call_target="tpu_custom_call" | custom-call | flops 1 | bytes 1 | tf_op jit(solution)/shard_map/pallas_call | solution.py:207
  21.5 2.4 collective-permute-start.4
  24.5 3.3 %collective-permute-start.6 = (bf16[1,72,1024]{2,1,0:T(8,128)(2,1)S(1)}, bf16[1,72,1024]{2,1,0:T(8,128)(2,1)S(1)}, u32[]{:S(2)}, u32[]{:S(2)}) collective-permute-start(bf16[1,72,1024]{2,1,0:T(8,128)(2,1)S(1)} %maximum_bitcast_fusion.refs_0_), channel_id=1, source_target_pairs={{0,16},{2,18},{4,20},{6,22},{8,24},{10,26},{12,28},{14,30},{16,0},... | collective-permute-start | bytes 442376 | tf_op jit(solution)/shard_map/ppermute | solution.py:235
  27.9 8.6 %collective-permute-done.4 = f32[4,2,1024]{2,1,0:T(2,128)S(1)} collective-permute-done((f32[4,2,1024]{2,1,0:T(2,128)S(1)}, f32[4,2,1024]{2,1,0:T(2,128)S(1)}, u32[]{:S(2)}, u32[]{:S(2)}) %collective-permute-start.4) | collective-permute-done | bytes 32800 | tf_op jit(solution)/shard_map/ppermute | solution.py:235
  36.4 3.0 %collective-permute-done.5 = f32[4,2,1024]{2,1,0:T(2,128)S(1)} collective-permute-done((f32[4,2,1024]{2,1,0:T(2,128)S(1)}, f32[4,2,1024]{2,1,0:T(2,128)S(1)}, u32[]{:S(2)}, u32[]{:S(2)}) %collective-permute-start.5) | collective-permute-done | bytes 32800 | tf_op jit(solution)/shard_map/ppermute | solution.py:235
  39.5 7.8 %all-to-all-start.1 = ((bf16[16,128,1024]{2,1,0:T(8,128)(2,1)}), bf16[16,128,1024]{2,1,0:T(8,128)(2,1)}, u32[]{:S(2)}, u32[]{:S(2)}) async-start(bf16[16,128,1024]{2,1,0:T(8,128)(2,1)} %bitcast.112), calls=%async_computation.1 | async-start | bytes 8388608 | tf_op jit(solution)/shard_map/all_to_all | solution.py:230
  52.4 9.3 %collective-permute-done.9 = f32[4,2,1024]{2,1,0:T(2,128)S(1)} collective-permute-done((f32[4,2,1024]{2,1,0:T(2,128)S(1)}, f32[4,2,1024]{2,1,0:T(2,128)S(1)}, u32[]{:S(2)}, u32[]{:S(2)}) %collective-permute-start.9) | collective-permute-done | bytes 32800 | tf_op jit(solution)/shard_map/ppermute | solution.py:235
  61.7 5.7 %collective-permute-done.8 = f32[4,2,1024]{2,1,0:T(2,128)S(1)} collective-permute-done((f32[4,2,1024]{2,1,0:T(2,128)S(1)}, f32[4,2,1024]{2,1,0:T(2,128)S(1)}, u32[]{:S(2)}, u32[]{:S(2)}) %collective-permute-start.8) | collective-permute-done | bytes 32800 | tf_op jit(solution)/shard_map/ppermute | solution.py:235
  68.2 1.8 shard_map.131
  73.0 2.7 %collective-permute-done.11 = f32[16,32]{1,0:T(8,128)S(1)} collective-permute-done((f32[16,32]{1,0:T(8,128)S(1)}, f32[16,32]{1,0:T(8,128)S(1)}, u32[]{:S(2)}, u32[]{:S(2)}) %collective-permute-start.11) | collective-permute-done | bytes 2080 | tf_op jit(solution)/shard_map/ppermute | solution.py:235
  75.7 3.6 %collective-permute-done.12 = f32[16,32]{1,0:T(8,128)S(1)} collective-permute-done((f32[16,32]{1,0:T(8,128)S(1)}, f32[16,32]{1,0:T(8,128)S(1)}, u32[]{:S(2)}, u32[]{:S(2)}) %collective-permute-start.12) | collective-permute-done | bytes 2080 | tf_op jit(solution)/shard_map/ppermute | solution.py:235
  79.3 43.2 %collective-permute-done.16.refs_2_ = bf16[2,72,1024]{2,1,0:T(8,128)(2,1)S(1)} collective-permute-done((bf16[2,72,1024]{2,1,0:T(8,128)(2,1)S(1)}, bf16[2,72,1024]{2,1,0:T(8,128)(2,1)S(1)}, u32[]{:S(2)}, u32[]{:S(2)}) %collective-permute-start.16) | collective-permute-done | bytes 294944 | tf_op jit(solution)/shard_map/ppermute | solution.py:235
  123.2 2.6 collective-permute-start.15
  125.8 1.5 collective-permute-start.13
  127.3 13.5 %collective-permute-done.15 = f32[16,32]{1,0:T(8,128)S(1)} collective-permute-done((f32[16,32]{1,0:T(8,128)S(1)}, f32[16,32]{1,0:T(8,128)S(1)}, u32[]{:S(2)}, u32[]{:S(2)}) %collective-permute-start.15) | collective-permute-done | bytes 2080 | tf_op jit(solution)/shard_map/ppermute | solution.py:235
  141.4 3.0 %shard_map.132 = (bf16[16,16]{1,0:T(8,128)(2,1)}, bf16[256,256]{1,0:T(8,128)(2,1)}) custom-call(f32[16,32]{1,0:T(8,128)} %add_add_fusion.sums_ref), custom_call_target="tpu_custom_call" | custom-call | flops 1 | bytes 1 | tf_op jit(solution)/shard_map/pallas_call | solution.py:72
  144.4 5.1 %shard_map.133 = bf16[16,128,1024]{2,1,0:T(8,128)(2,1)} custom-call(bf16[256,256]{1,0:T(8,128)(2,1)} %get-tuple-element.31.spread_ref, bf16[16,128,1024]{2,1,0:T(8,128)(2,1)} %all-to-all-done.1.x_ref), custom_call_target="tpu_custom_call" | custom-call | flops 1 | bytes 1 | tf_op jit(solution)/shard_map/pallas_call | solution.py:47
  149.5 5.9 %all-to-all-start.2 = ((bf16[16,128,1024]{2,1,0:T(8,128)(2,1)}), bf16[16,128,1024]{2,1,0:T(8,128)(2,1)}, u32[]{:S(2)}, u32[]{:S(2)}) async-start(bf16[16,128,1024]{2,1,0:T(8,128)(2,1)} %shard_map.133), calls=%async_computation.2 | async-start | bytes 8388608 | tf_op jit(solution)/shard_map/all_to_all | solution.py:230
  155.4 2.9 %shard_map.134 = bf16[16,32,1024]{2,1,0:T(8,128)(2,1)} custom-call(bf16[256,256]{1,0:T(8,128)(2,1)} %get-tuple-element.31.spread_ref, bf16[16,32,1024]{2,1,0:T(8,128)(2,1)} %all-to-all-done.x_ref), custom_call_target="tpu_custom_call" | custom-call | flops 1 | bytes 1 | tf_op jit(solution)/shard_map/pallas_call | solution.py:47
  159.6 1.5 collective-permute-start.20
  163.1 13.0 %collective-permute-done.20 = bf16[4,32,1024]{2,1,0:T(8,128)(2,1)S(1)} collective-permute-done((bf16[4,32,1024]{2,1,0:T(8,128)(2,1)S(1)}, bf16[4,32,1024]{2,1,0:T(8,128)(2,1)S(1)}, u32[]{:S(2)}, u32[]{:S(2)}) %collective-permute-start.20) | collective-permute-done | bytes 262176 | tf_op jit(solution)/shard_map/ppermute | solution.py:235
  176.1 12.2 %collective-permute-done.19 = bf16[4,32,1024]{2,1,0:T(8,128)(2,1)S(1)} collective-permute-done((bf16[4,32,1024]{2,1,0:T(8,128)(2,1)S(1)}, bf16[4,32,1024]{2,1,0:T(8,128)(2,1)S(1)}, u32[]{:S(2)}, u32[]{:S(2)}) %collective-permute-start.19) | collective-permute-done | bytes 262176 | tf_op jit(solution)/shard_map/ppermute | solution.py:235
  192.2 7.7 %collective-permute-start.21 = (bf16[4,32,1024]{2,1,0:T(8,128)(2,1)}, bf16[4,32,1024]{2,1,0:T(8,128)(2,1)S(1)}, u32[]{:S(2)}, u32[]{:S(2)}) collective-permute-start(bf16[4,32,1024]{2,1,0:T(8,128)(2,1)} %pad_maximum_fusion.5), channel_id=1, source_target_pairs={{0,8},{2,10},{4,12},{6,14},{8,0},{10,2},{12,4},{14,6},{16,24},{18,... | collective-permute-start | bytes 786440 | tf_op jit(solution)/shard_map/ppermute | solution.py:235
  200.6 4.9 %collective-permute-start.22 = (bf16[4,32,1024]{2,1,0:T(8,128)(2,1)}, bf16[4,32,1024]{2,1,0:T(8,128)(2,1)S(1)}, u32[]{:S(2)}, u32[]{:S(2)}) collective-permute-start(bf16[4,32,1024]{2,1,0:T(8,128)(2,1)} %pad_maximum_fusion.6), channel_id=1, source_target_pairs={{0,16},{2,18},{4,20},{6,22},{8,24},{10,26},{12,28},{14,30},{16,0},... | collective-permute-start | bytes 786440 | tf_op jit(solution)/shard_map/ppermute | solution.py:235
  206.9 24.4 %collective-permute-done.24.refs_4_ = bf16[8,72,1024]{2,1,0:T(8,128)(2,1)S(1)} collective-permute-done((bf16[8,72,1024]{2,1,0:T(8,128)(2,1)S(1)}, bf16[8,72,1024]{2,1,0:T(8,128)(2,1)S(1)}, u32[]{:S(2)}, u32[]{:S(2)}) %collective-permute-start.24) | collective-permute-done | bytes 1179680 | tf_op jit(solution)/shard_map/ppermute | solution.py:235
  232.4 3.6 %shard_map.136 = bf16[72,1024]{1,0:T(8,128)(2,1)} custom-call(f32[16]{0:T(128)} %fusion.1.column_ref, bf16[1,72,1024]{2,1,0:T(8,128)(2,1)} %copy-done.6, bf16[1,72,1024]{2,1,0:T(8,128)(2,1)} %copy-done.8, bf16[2,72,1024]{2,1,0:T(8,128)(2,1)} %copy-done.7, bf16[4,72,1024]{2,1,0:T(8,128)(2,1)} %copy-done.9, bf16[8,72,1024]{2,1,0:T(8,128)(2,1)} %copy-done.10), custom_call_target="tpu_custom_call" | custom-call | flops 1 | bytes 1 | tf_op jit(solution)/shard_map/pallas_call | solution.py:143
  237.4 1.6 slice_bitcast_fusion
  239.0 20.2 %all-to-all-done.2.x_ref = bf16[16,128,1024]{2,1,0:T(8,128)(2,1)} async-done(((bf16[16,128,1024]{2,1,0:T(8,128)(2,1)}), bf16[16,128,1024]{2,1,0:T(8,128)(2,1)}, u32[]{:S(2)}, u32[]{:S(2)}) %all-to-all-start.2) | async-done | bytes 4194336 | tf_op jit(solution)/shard_map/all_to_all | solution.py:230
  259.2 3.7 %shard_map.135 = bf16[16,128,1024]{2,1,0:T(8,128)(2,1)} custom-call(bf16[16,128,1024]{2,1,0:T(8,128)(2,1)} %all-to-all-done.2.x_ref), custom_call_target="tpu_custom_call" | custom-call | flops 1 | bytes 1 | tf_op jit(solution)/shard_map/pallas_call | solution.py:47
  264.3 5.1 %collective-permute-done.23 = bf16[4,32,1024]{2,1,0:T(8,128)(2,1)S(1)} collective-permute-done((bf16[4,32,1024]{2,1,0:T(8,128)(2,1)}, bf16[4,32,1024]{2,1,0:T(8,128)(2,1)S(1)}, u32[]{:S(2)}, u32[]{:S(2)}) %collective-permute-start.23) | collective-permute-done | bytes 262176 | tf_op jit(solution)/shard_map/ppermute | solution.py:235
  (112 shorter events, 31.3 us)
Async XLA Ops:
  0.7 38.9 %all-to-all-start = ((bf16[16,32,1024]{2,1,0:T(8,128)(2,1)}), bf16[16,32,1024]{2,1,0:T(8,128)(2,1)}, u32[]{:S(2)}, u32[]{:S(2)}) async-start(bf16[16,32,1024]{2,1,0:T(8,128)(2,1)} %bitcast.117), calls=%async_computation | async-start | bytes 2097152 | tf_op jit(solution)/shard_map/all_to_all | solution.py:230
  8.9 2.0 collective-permute-start
  9.9 2.1 collective-permute-start.1
  19.1 1.3 collective-permute-start.2
  20.9 7.0 %collective-permute-start.3 = (f32[4,2,1024]{2,1,0:T(2,128)S(1)}, f32[4,2,1024]{2,1,0:T(2,128)S(1)}, u32[]{:S(2)}, u32[]{:S(2)}) collective-permute-start(f32[4,2,1024]{2,1,0:T(2,128)S(1)} %get-tuple-element.86), channel_id=1, source_target_pairs={{0,8},{2,10},{4,12},{6,14},{8,0},{10,2},{12,4},{14,6},{16,24},{18,... | collective-permute-start | bytes 98312 | tf_op jit(solution)/shard_map/ppermute | solution.py:235
  21.5 14.9 %collective-permute-start.4 = (f32[4,2,1024]{2,1,0:T(2,128)S(1)}, f32[4,2,1024]{2,1,0:T(2,128)S(1)}, u32[]{:S(2)}, u32[]{:S(2)}) collective-permute-start(f32[4,2,1024]{2,1,0:T(2,128)S(1)} %get-tuple-element.87), channel_id=1, source_target_pairs={{0,16},{2,18},{4,20},{6,22},{8,24},{10,26},{12,28},{14,30},{16,0},... | collective-permute-start | bytes 98312 | tf_op jit(solution)/shard_map/ppermute | solution.py:235
  23.9 15.6 %collective-permute-start.5 = (f32[4,2,1024]{2,1,0:T(2,128)S(1)}, f32[4,2,1024]{2,1,0:T(2,128)S(1)}, u32[]{:S(2)}, u32[]{:S(2)}) collective-permute-start(f32[4,2,1024]{2,1,0:T(2,128)S(1)} %get-tuple-element.88), channel_id=1, source_target_pairs={{0,24},{2,26},{4,28},{6,30},{8,16},{10,18},{12,20},{14,22},{16,8},... | collective-permute-start | bytes 98312 | tf_op jit(solution)/shard_map/ppermute | solution.py:235
  24.5 164.0 %copy-start.6 = (bf16[1,72,1024]{2,1,0:T(8,128)(2,1)}, bf16[1,72,1024]{2,1,0:T(8,128)(2,1)S(1)}, u32[]{:S(2)}) copy-start(bf16[1,72,1024]{2,1,0:T(8,128)(2,1)S(1)} %maximum_bitcast_fusion.refs_0_) | copy-start | bytes 442372
  24.5 15.0 %collective-permute-start.6 = (bf16[1,72,1024]{2,1,0:T(8,128)(2,1)S(1)}, bf16[1,72,1024]{2,1,0:T(8,128)(2,1)S(1)}, u32[]{:S(2)}, u32[]{:S(2)}) collective-permute-start(bf16[1,72,1024]{2,1,0:T(8,128)(2,1)S(1)} %maximum_bitcast_fusion.refs_0_), channel_id=1, source_target_pairs={{0,16},{2,18},{4,20},{6,22},{8,24},{10,26},{12,28},{14,30},{16,0},... | collective-permute-start | bytes 442376 | tf_op jit(solution)/shard_map/ppermute | solution.py:235
  39.5 149.0 %copy-start.8 = (bf16[1,72,1024]{2,1,0:T(8,128)(2,1)}, bf16[1,72,1024]{2,1,0:T(8,128)(2,1)S(1)}, u32[]{:S(2)}) copy-start(bf16[1,72,1024]{2,1,0:T(8,128)(2,1)S(1)} %collective-permute-done.6.refs_1_) | copy-start | bytes 442372
  39.5 101.9 %all-to-all-start.1 = ((bf16[16,128,1024]{2,1,0:T(8,128)(2,1)}), bf16[16,128,1024]{2,1,0:T(8,128)(2,1)}, u32[]{:S(2)}, u32[]{:S(2)}) async-start(bf16[16,128,1024]{2,1,0:T(8,128)(2,1)} %bitcast.112), calls=%async_computation.1 | async-start | bytes 8388608 | tf_op jit(solution)/shard_map/all_to_all | solution.py:230
  48.2 13.5 %collective-permute-start.9 = (f32[4,2,1024]{2,1,0:T(2,128)S(1)}, f32[4,2,1024]{2,1,0:T(2,128)S(1)}, u32[]{:S(2)}, u32[]{:S(2)}) collective-permute-start(f32[4,2,1024]{2,1,0:T(2,128)S(1)} %get-tuple-element.78), channel_id=1, source_target_pairs={{0,6},{2,4},{4,2},{6,0},{8,14},{10,12},{12,10},{14,8},{16,22},{18,... | collective-permute-start | bytes 98312 | tf_op jit(solution)/shard_map/ppermute | solution.py:235
  49.7 17.7 %collective-permute-start.8 = (f32[4,2,1024]{2,1,0:T(2,128)S(1)}, f32[4,2,1024]{2,1,0:T(2,128)S(1)}, u32[]{:S(2)}, u32[]{:S(2)}) collective-permute-start(f32[4,2,1024]{2,1,0:T(2,128)S(1)} %get-tuple-element.79), channel_id=1, source_target_pairs={{0,4},{2,6},{4,0},{6,2},{8,12},{10,14},{12,8},{14,10},{16,20},{18,... | collective-permute-start | bytes 98312 | tf_op jit(solution)/shard_map/ppermute | solution.py:235
  51.1 16.2 %collective-permute-start.7 = (f32[4,2,1024]{2,1,0:T(2,128)S(1)}, f32[4,2,1024]{2,1,0:T(2,128)S(1)}, u32[]{:S(2)}, u32[]{:S(2)}) collective-permute-start(f32[4,2,1024]{2,1,0:T(2,128)S(1)} %get-tuple-element.80), channel_id=1, source_target_pairs={{0,2},{2,0},{4,6},{6,4},{8,10},{10,8},{12,14},{14,12},{16,18},{18,... | collective-permute-start | bytes 98312 | tf_op jit(solution)/shard_map/ppermute | solution.py:235
  51.7 70.8 %collective-permute-start.16 = (bf16[2,72,1024]{2,1,0:T(8,128)(2,1)S(1)}, bf16[2,72,1024]{2,1,0:T(8,128)(2,1)S(1)}, u32[]{:S(2)}, u32[]{:S(2)}) collective-permute-start(bf16[2,72,1024]{2,1,0:T(8,128)(2,1)S(1)} %pad_maximum_fusion.3), channel_id=1, source_target_pairs={{0,8},{2,10},{4,12},{6,14},{8,0},{10,2},{12,4},{14,6},{16,24},{18,... | collective-permute-start | bytes 884744 | tf_op jit(solution)/shard_map/ppermute | solution.py:235
  69.9 1.4 collective-permute-start.10
  72.0 3.7 %collective-permute-start.11 = (f32[16,32]{1,0:T(8,128)S(1)}, f32[16,32]{1,0:T(8,128)S(1)}, u32[]{:S(2)}, u32[]{:S(2)}) collective-permute-start(f32[16,32]{1,0:T(8,128)S(1)} %add.207), channel_id=1, source_target_pairs={{0,2},{2,0},{4,6},{6,4},{8,10},{10,8},{12,14},{14,12},{16,18},{18,... | collective-permute-start | bytes 6152 | tf_op jit(solution)/shard_map/ppermute | solution.py:235
  75.7 3.7 %collective-permute-start.12 = (f32[16,32]{1,0:T(8,128)S(1)}, f32[16,32]{1,0:T(8,128)S(1)}, u32[]{:S(2)}, u32[]{:S(2)}) collective-permute-start(f32[16,32]{1,0:T(8,128)S(1)} %add.208), channel_id=1, source_target_pairs={{0,4},{2,6},{4,0},{6,2},{8,12},{10,14},{12,8},{14,10},{16,20},{18,... | collective-permute-start | bytes 6152 | tf_op jit(solution)/shard_map/ppermute | solution.py:235
  122.5 66.0 %copy-start.7 = (bf16[2,72,1024]{2,1,0:T(8,128)(2,1)}, bf16[2,72,1024]{2,1,0:T(8,128)(2,1)S(1)}, u32[]{:S(2)}) copy-start(bf16[2,72,1024]{2,1,0:T(8,128)(2,1)S(1)} %collective-permute-done.16.refs_2_) | copy-start | bytes 884740
  122.6 26.9 %collective-permute-start.17 = (bf16[4,72,1024]{2,1,0:T(8,128)(2,1)S(1)}, bf16[4,72,1024]{2,1,0:T(8,128)(2,1)S(1)}, u32[]{:S(2)}, u32[]{:S(2)}) collective-permute-start(bf16[4,72,1024]{2,1,0:T(8,128)(2,1)S(1)} %pad_maximum_fusion.2), channel_id=1, source_target_pairs={{0,4},{2,6},{4,0},{6,2},{8,12},{10,14},{12,8},{14,10},{16,20},{18,... | collective-permute-start | bytes 1769480 | tf_op jit(solution)/shard_map/ppermute | solution.py:235
  123.2 17.6 %collective-permute-start.15 = (f32[16,32]{1,0:T(8,128)S(1)}, f32[16,32]{1,0:T(8,128)S(1)}, u32[]{:S(2)}, u32[]{:S(2)}) collective-permute-start(f32[16,32]{1,0:T(8,128)S(1)} %add.209), channel_id=1, source_target_pairs={{0,24},{2,26},{4,28},{6,30},{8,16},{10,18},{12,20},{14,22},{16,8},... | collective-permute-start | bytes 6152 | tf_op jit(solution)/shard_map/ppermute | solution.py:235
  125.8 15.0 %collective-permute-start.14 = (f32[16,32]{1,0:T(8,128)S(1)}, f32[16,32]{1,0:T(8,128)S(1)}, u32[]{:S(2)}, u32[]{:S(2)}) collective-permute-start(f32[16,32]{1,0:T(8,128)S(1)} %add.209), channel_id=1, source_target_pairs={{0,16},{2,18},{4,20},{6,22},{8,24},{10,26},{12,28},{14,30},{16,0},... | collective-permute-start | bytes 6152 | tf_op jit(solution)/shard_map/ppermute | solution.py:235
  125.8 15.0 %collective-permute-start.13 = (f32[16,32]{1,0:T(8,128)S(1)}, f32[16,32]{1,0:T(8,128)S(1)}, u32[]{:S(2)}, u32[]{:S(2)}) collective-permute-start(f32[16,32]{1,0:T(8,128)S(1)} %add.209), channel_id=1, source_target_pairs={{0,8},{2,10},{4,12},{6,14},{8,0},{10,2},{12,4},{14,6},{16,24},{18,... | collective-permute-start | bytes 6152 | tf_op jit(solution)/shard_map/ppermute | solution.py:235
  149.5 39.0 %copy-start.9 = (bf16[4,72,1024]{2,1,0:T(8,128)(2,1)}, bf16[4,72,1024]{2,1,0:T(8,128)(2,1)S(1)}, u32[]{:S(2)}) copy-start(bf16[4,72,1024]{2,1,0:T(8,128)(2,1)S(1)} %collective-permute-done.17.refs_3_) | copy-start | bytes 1769476
  149.5 109.7 %all-to-all-start.2 = ((bf16[16,128,1024]{2,1,0:T(8,128)(2,1)}), bf16[16,128,1024]{2,1,0:T(8,128)(2,1)}, u32[]{:S(2)}, u32[]{:S(2)}) async-start(bf16[16,128,1024]{2,1,0:T(8,128)(2,1)} %shard_map.133), calls=%async_computation.2 | async-start | bytes 8388608 | tf_op jit(solution)/shard_map/all_to_all | solution.py:230
  159.6 16.5 %collective-permute-start.20 = (bf16[4,32,1024]{2,1,0:T(8,128)(2,1)S(1)}, bf16[4,32,1024]{2,1,0:T(8,128)(2,1)S(1)}, u32[]{:S(2)}, u32[]{:S(2)}) collective-permute-start(bf16[4,32,1024]{2,1,0:T(8,128)(2,1)S(1)} %get-tuple-element.68), channel_id=1, source_target_pairs={{0,6},{2,4},{4,2},{6,0},{8,14},{10,12},{12,10},{14,8},{16,22},{18,... | collective-permute-start | bytes 786440 | tf_op jit(solution)/shard_map/ppermute | solution.py:235
  161.1 27.2 %collective-permute-start.19 = (bf16[4,32,1024]{2,1,0:T(8,128)(2,1)S(1)}, bf16[4,32,1024]{2,1,0:T(8,128)(2,1)S(1)}, u32[]{:S(2)}, u32[]{:S(2)}) collective-permute-start(bf16[4,32,1024]{2,1,0:T(8,128)(2,1)S(1)} %get-tuple-element.69), channel_id=1, source_target_pairs={{0,4},{2,6},{4,0},{6,2},{8,12},{10,14},{12,8},{14,10},{16,20},{18,... | collective-permute-start | bytes 786440 | tf_op jit(solution)/shard_map/ppermute | solution.py:235
  162.6 25.8 %collective-permute-start.18 = (bf16[4,32,1024]{2,1,0:T(8,128)(2,1)S(1)}, bf16[4,32,1024]{2,1,0:T(8,128)(2,1)S(1)}, u32[]{:S(2)}, u32[]{:S(2)}) collective-permute-start(bf16[4,32,1024]{2,1,0:T(8,128)(2,1)S(1)} %get-tuple-element.70), channel_id=1, source_target_pairs={{0,2},{2,0},{4,6},{6,4},{8,10},{10,8},{12,14},{14,12},{16,18},{18,... | collective-permute-start | bytes 786440 | tf_op jit(solution)/shard_map/ppermute | solution.py:235
  188.7 42.7 %collective-permute-start.24 = (bf16[8,72,1024]{2,1,0:T(8,128)(2,1)S(1)}, bf16[8,72,1024]{2,1,0:T(8,128)(2,1)S(1)}, u32[]{:S(2)}, u32[]{:S(2)}) collective-permute-start(bf16[8,72,1024]{2,1,0:T(8,128)(2,1)S(1)} %pad_maximum_fusion), channel_id=1, source_target_pairs={{0,2},{2,0},{4,6},{6,4},{8,10},{10,8},{12,14},{14,12},{16,18},{18,... | collective-permute-start | bytes 3538952 | tf_op jit(solution)/shard_map/ppermute | solution.py:235
  192.2 70.8 %collective-permute-start.21 = (bf16[4,32,1024]{2,1,0:T(8,128)(2,1)}, bf16[4,32,1024]{2,1,0:T(8,128)(2,1)S(1)}, u32[]{:S(2)}, u32[]{:S(2)}) collective-permute-start(bf16[4,32,1024]{2,1,0:T(8,128)(2,1)} %pad_maximum_fusion.5), channel_id=1, source_target_pairs={{0,8},{2,10},{4,12},{6,14},{8,0},{10,2},{12,4},{14,6},{16,24},{18,... | collective-permute-start | bytes 786440 | tf_op jit(solution)/shard_map/ppermute | solution.py:235
  200.6 63.6 %collective-permute-start.22 = (bf16[4,32,1024]{2,1,0:T(8,128)(2,1)}, bf16[4,32,1024]{2,1,0:T(8,128)(2,1)S(1)}, u32[]{:S(2)}, u32[]{:S(2)}) collective-permute-start(bf16[4,32,1024]{2,1,0:T(8,128)(2,1)} %pad_maximum_fusion.6), channel_id=1, source_target_pairs={{0,16},{2,18},{4,20},{6,22},{8,24},{10,26},{12,28},{14,30},{16,0},... | collective-permute-start | bytes 786440 | tf_op jit(solution)/shard_map/ppermute | solution.py:235
  206.3 63.0 %collective-permute-start.23 = (bf16[4,32,1024]{2,1,0:T(8,128)(2,1)}, bf16[4,32,1024]{2,1,0:T(8,128)(2,1)S(1)}, u32[]{:S(2)}, u32[]{:S(2)}) collective-permute-start(bf16[4,32,1024]{2,1,0:T(8,128)(2,1)} %pad_maximum_fusion.7), channel_id=1, source_target_pairs={{0,24},{2,26},{4,28},{6,30},{8,16},{10,18},{12,20},{14,22},{16,8},... | collective-permute-start | bytes 786440 | tf_op jit(solution)/shard_map/ppermute | solution.py:235
  (12 other events, 53.0 us)

commit v3 on v2

--- a/solution.py
+++ b/solution.py
@@ -7,7 +7,8 @@
 from jax.experimental.pallas import tpu as pltpu
 from jax.sharding import PartitionSpec as P
 
-ROWS = 16
+ROW_BITS = 4
+ROWS = 1 << ROW_BITS
 PLANE = 4
 TILE = 256
 VMEM = 56 << 20
@@ -24,16 +25,20 @@
     return lax.linalg.triangular_solve(factor, middle, left_side=True, lower=True, transpose_a=True)
 
 
+def mix_rows(spread_ref, x_ref, y_ref, at):
+    members, _, width = x_ref.shape
+    for left in range(0, width, TILE):
+        piece = (slice(None), pl.ds(at, ROWS), pl.ds(left, TILE))
+        full = x_ref[piece].astype(jnp.float32)
+        mean = jnp.sum(full, axis=0, keepdims=True) * (1.0 / members)
+        center = (full - mean).astype(jnp.bfloat16).reshape(members * ROWS, TILE)
+        mixed = jnp.dot(spread_ref[...], center, preferred_element_type=jnp.float32)
+        y_ref[piece] = mixed.astype(jnp.bfloat16).reshape(members, ROWS, TILE)
+
+
 def mix_kernel(spread_ref, x_ref, y_ref):
-    members, rows, width = x_ref.shape
-    for at in range(0, rows, ROWS):
-        for left in range(0, width, TILE):
-            piece = (slice(None), pl.ds(at, ROWS), pl.ds(left, TILE))
-            full = x_ref[piece].astype(jnp.float32)
-            mean = jnp.sum(full, axis=0, keepdims=True) * (1.0 / members)
-            center = (full - mean).astype(jnp.bfloat16).reshape(members * ROWS, TILE)
-            mixed = jnp.dot(spread_ref[...], center, preferred_element_type=jnp.float32)
-            y_ref[piece] = mixed.astype(jnp.bfloat16).reshape(members, ROWS, TILE)
+    for at in range(0, x_ref.shape[1], ROWS):
+        mix_rows(spread_ref, x_ref, y_ref, at)
 
 
 def copy_kernel(x_ref, y_ref):
@@ -72,8 +77,12 @@
     return pl.pallas_call(kernel, out_shape=out_shape, cost_estimate=LIGHT)(*args)
 
 
-def solve_kernel(sums_ref, gain_ref, spread_ref):
-    total = sums_ref[...]
+def solve_kernel(
+    own_ref, far1_ref, far2_ref, far3_ref, x_ref, gain_ref, spread_ref, y_ref, x_buf, y_buf, x_sem, y_sems
+):
+    load = pltpu.make_async_copy(x_ref, x_buf, x_sem)
+    load.start()
+    total = (own_ref[...] + far1_ref[...]) + (far2_ref[...] + far3_ref[...])
     count = total.shape[0]
     row = lax.broadcasted_iota(jnp.int32, total.shape, 0)
     col = lax.broadcasted_iota(jnp.int32, total.shape, 1)
@@ -87,31 +96,51 @@
     size = count * ROWS
     row = lax.broadcasted_iota(jnp.int32, (size, count), 0)
     col = lax.broadcasted_iota(jnp.int32, (size, count), 1)
-    expand = (row // ROWS == col).astype(jnp.bfloat16)
+    expand = (row >> ROW_BITS == col).astype(jnp.bfloat16)
     wide = lax.dot_general(
         expand, gain, (((1,), (1,)), ((), ())), preferred_element_type=jnp.float32
     ).astype(jnp.bfloat16)
     wide = lax.dot_general(
         wide, expand, (((1,), (1,)), ((), ())), preferred_element_type=jnp.float32
     )
-    at_row = lax.broadcasted_iota(jnp.int32, (size, size), 0) % ROWS
-    at_col = lax.broadcasted_iota(jnp.int32, (size, size), 1) % ROWS
-    spread_ref[...] = jnp.where(at_row == at_col, wide, 0.0).astype(jnp.bfloat16)
-
-
-def spread_gain(gain_tr):
-    members = gain_tr.shape[0]
+    at_row = lax.broadcasted_iota(jnp.int32, (size, size), 0)
+    at_col = lax.broadcasted_iota(jnp.int32, (size, size), 1)
+    same = ((at_row ^ at_col) & (ROWS - 1)) == 0
+    spread_ref[...] = jnp.where(same, wide, 0.0).astype(jnp.bfloat16)
+
+    load.wait()
+    stores = []
+    for i in range(x_ref.shape[1] // ROWS):
+        rows = (slice(None), pl.ds(i * ROWS, ROWS), slice(None))
+        mix_rows(spread_ref, x_buf, y_buf, i * ROWS)
+        stores.append(pltpu.make_async_copy(y_buf.at[rows], y_ref.at[rows], y_sems.at[i]))
+        stores[-1].start()
+    for store in stores:
+        store.wait()
+
+
+def solve(sums, x):
+    members = x.shape[0]
     size = members * ROWS
-    row = lax.broadcasted_iota(jnp.int32, (size, members), 0)
-    col = lax.broadcasted_iota(jnp.int32, (size, members), 1)
-    expand = (row // ROWS == col).astype(jnp.bfloat16)
-    wide = jnp.dot(expand, gain_tr, preferred_element_type=jnp.float32).astype(jnp.bfloat16)
-    wide = lax.dot_general(
-        wide, expand, (((1,), (1,)), ((), ())), preferred_element_type=jnp.float32
-    ).astype(jnp.bfloat16)
-    at_row = lax.broadcasted_iota(jnp.int32, (size, size), 0) % ROWS
-    at_col = lax.broadcasted_iota(jnp.int32, (size, size), 1) % ROWS
-    return jnp.where(at_row == at_col, wide, jnp.bfloat16(0))
+    vmem, anywhere = pl.BlockSpec(memory_space=pltpu.VMEM), pl.BlockSpec(memory_space=pl.ANY)
+    return pl.pallas_call(
+        solve_kernel,
+        in_specs=[vmem] * len(sums) + [anywhere],
+        out_specs=[vmem, vmem, anywhere],
+        out_shape=[
+            jax.ShapeDtypeStruct((members, members), jnp.bfloat16),
+            jax.ShapeDtypeStruct((size, size), jnp.bfloat16),
+            jax.ShapeDtypeStruct(x.shape, x.dtype),
+        ],
+        scratch_shapes=[
+            pltpu.VMEM(x.shape, x.dtype),
+            pltpu.VMEM(x.shape, x.dtype),
+            pltpu.SemaphoreType.DMA,
+            pltpu.SemaphoreType.DMA((x.shape[1] // ROWS,)),
+        ],
+        compiler_params=pltpu.CompilerParams(vmem_limit_bytes=VMEM),
+        cost_estimate=LIGHT,
+    )(*sums, x)
 
 
 def mix_plain(slab, gain_tr):
@@ -312,18 +341,7 @@
         held[2] = after(held[2], sums)
         held.append(swap(jnp.concatenate(held, axis=0), "member", 2))
         far = [across(sums, i) for i in range(1, planes)]
-        sums, got_second = lax.optimization_barrier(
-            ((sums + far[0]) + (far[1] + far[2]), got_second)
-        )
-        gain, spread = whole_call(
-            solve_kernel,
-            [
-                jax.ShapeDtypeStruct((members, members), jnp.bfloat16),
-                jax.ShapeDtypeStruct((members * ROWS, members * ROWS), jnp.bfloat16),
-            ],
-            sums,
-        )
-        mixed_second = blocked(mix_kernel, got_second, spread)
+        gain, spread, mixed_second = solve([sums] + far, got_second)
         mixed_second, got_first, held[3] = lax.optimization_barrier(
             (mixed_second, got_first, held[3])
         )

time: 271 us -> 269 us (level)
    pallas_call x0 -> x1, Pallas kernels: none -> 6.2 us  [solve(): pl.pallas_call(solve_kernel, in_specs=[vmem] * len(sums) + [anywhere], ou...]
    pallas_call x3 -> x2, Pallas kernels: 11.7 us -> 6.64 us  [blocked(): pl.pallas_call(kernel, grid=(total // rows,), in_specs=[pl.BlockSpec(w.sh...]
    pallas_call x2 -> x1, Pallas kernels: 4.77 us -> 1.76 us  [whole_call(): pl.pallas_call(kernel, out_shape=out_shape, cost_estimate=LIGHT)(*args)]
  transfers between devices with their start and end apart: 28 -> 28, of which waited for: 18 -> 18; matrix products, arithmetic and copies ran while one was open for 4% -> 4% of each run, Pallas kernels for 10% -> 9%
where the time goes in v3:
time: 269 us
  waiting for transfers between devices  170 us (63%)
  starting transfers between devices  57.2 us (21%)
  Pallas kernels  24.9 us (9%)
  local copies, waits for them, and re-layouts  10.7 us (4%)
  other arithmetic  4.69 us (2%)
    ppermute x25, waiting for transfers between devices, swap(): return lax.ppermute(x, axis, [(i, i ^ bit) for i in range(count)])  149 us
    ppermute x25, starting transfers between devices, swap(): return lax.ppermute(x, axis, [(i, i ^ bit) for i in range(count)])  36.1 us
    all_to_all x3, starting transfers between devices, exchange(): return lax.all_to_all(x, 'member', split_axis=0, concat_axis=0, tiled=True)  21.1 us
    all_to_all x3, waiting for transfers between devices, exchange(): return lax.all_to_all(x, 'member', split_axis=0, concat_axis=0, tiled=True)  20.2 us
    pallas_call x2, Pallas kernels, blocked(): pl.pallas_call(kernel, grid=(total // rows,), in_specs=[pl.BlockSpec(w.sh...  6.64 us
    pallas_call x1, Pallas kernels, solve(): pl.pallas_call(solve_kernel, in_specs=[vmem] * len(sums) + [anywhere], ou...  6.2 us
  transfers between devices with their start and end apart: 28, of which 18 were waited for; matrix products, arithmetic and copies ran while one was open for 4% of the time, Pallas kernels for 9%

profile of v3, /device:TPU:12, one launch (start us, length us, event | category | flops | bytes accessed | tf_op | source)
XLA Modules:
  0.0 268.7 jit_solution(7978278986963236277)
XLA Ops:
  0.7 7.3 %all-to-all-start = ((bf16[16,32,1024]{2,1,0:T(8,128)(2,1)}), bf16[16,32,1024]{2,1,0:T(8,128)(2,1)}, u32[]{:S(2)}, u32[]{:S(2)}) async-start(bf16[16,32,1024]{2,1,0:T(8,128)(2,1)} %bitcast.117), calls=%async_computation | async-start | bytes 2097152 | tf_op jit(solution)/shard_map/all_to_all | solution.py:259
  12.0 2.2 copy-done
  14.2 4.8 %shard_map.130 = f32[64,512]{1,0:T(8,128)S(1)} custom-call(s32[1]{0:T(128)} %bitcast.1.side_ref, bf16[512,512]{1,0:T(8,128)(2,1)S(1)} %shard_map.128.refs_0_, bf16[512,512]{1,0:T(8,128)(2,1)S(1)} %shard_map.129.refs_1_, bf16[512,512]{1,0:T(8,128)(2,1)S(1)} %collective-permute-done.refs_2_, bf16[512,512]{1,0:T(8,128)(2,1)S(1)} %collective-permute-done.1.refs_3_, ...), custom_call_target="tpu_custom_call" | custom-call | flops 1 | bytes 1 | tf_op jit(solution)/shard_map/pallas_call | solution.py:236
  21.5 2.4 collective-permute-start.4
  24.5 3.3 %collective-permute-start.6 = (bf16[1,72,1024]{2,1,0:T(8,128)(2,1)S(1)}, bf16[1,72,1024]{2,1,0:T(8,128)(2,1)S(1)}, u32[]{:S(2)}, u32[]{:S(2)}) collective-permute-start(bf16[1,72,1024]{2,1,0:T(8,128)(2,1)S(1)} %maximum_bitcast_fusion.refs_0_), channel_id=1, source_target_pairs={{0,16},{2,18},{4,20},{6,22},{8,24},{10,26},{12,28},{14,30},{16,0},... | collective-permute-start | bytes 442376 | tf_op jit(solution)/shard_map/ppermute | solution.py:264
  27.9 8.6 %collective-permute-done.4 = f32[4,2,1024]{2,1,0:T(2,128)S(1)} collective-permute-done((f32[4,2,1024]{2,1,0:T(2,128)S(1)}, f32[4,2,1024]{2,1,0:T(2,128)S(1)}, u32[]{:S(2)}, u32[]{:S(2)}) %collective-permute-start.4) | collective-permute-done | bytes 32800 | tf_op jit(solution)/shard_map/ppermute | solution.py:264
  36.4 3.0 %collective-permute-done.5 = f32[4,2,1024]{2,1,0:T(2,128)S(1)} collective-permute-done((f32[4,2,1024]{2,1,0:T(2,128)S(1)}, f32[4,2,1024]{2,1,0:T(2,128)S(1)}, u32[]{:S(2)}, u32[]{:S(2)}) %collective-permute-start.5) | collective-permute-done | bytes 32800 | tf_op jit(solution)/shard_map/ppermute | solution.py:264
  39.5 7.8 %all-to-all-start.1 = ((bf16[16,128,1024]{2,1,0:T(8,128)(2,1)}), bf16[16,128,1024]{2,1,0:T(8,128)(2,1)}, u32[]{:S(2)}, u32[]{:S(2)}) async-start(bf16[16,128,1024]{2,1,0:T(8,128)(2,1)} %bitcast.112), calls=%async_computation.1 | async-start | bytes 8388608 | tf_op jit(solution)/shard_map/all_to_all | solution.py:259
  48.2 1.5 collective-permute-start.9
  52.4 9.3 %collective-permute-done.9 = f32[4,2,1024]{2,1,0:T(2,128)S(1)} collective-permute-done((f32[4,2,1024]{2,1,0:T(2,128)S(1)}, f32[4,2,1024]{2,1,0:T(2,128)S(1)}, u32[]{:S(2)}, u32[]{:S(2)}) %collective-permute-start.9) | collective-permute-done | bytes 32800 | tf_op jit(solution)/shard_map/ppermute | solution.py:264
  61.7 5.7 %collective-permute-done.8 = f32[4,2,1024]{2,1,0:T(2,128)S(1)} collective-permute-done((f32[4,2,1024]{2,1,0:T(2,128)S(1)}, f32[4,2,1024]{2,1,0:T(2,128)S(1)}, u32[]{:S(2)}, u32[]{:S(2)}) %collective-permute-start.8) | collective-permute-done | bytes 32800 | tf_op jit(solution)/shard_map/ppermute | solution.py:264
  68.2 1.8 shard_map.131
  73.0 2.7 %collective-permute-done.11 = f32[16,32]{1,0:T(8,128)S(1)} collective-permute-done((f32[16,32]{1,0:T(8,128)S(1)}, f32[16,32]{1,0:T(8,128)S(1)}, u32[]{:S(2)}, u32[]{:S(2)}) %collective-permute-start.11) | collective-permute-done | bytes 2080 | tf_op jit(solution)/shard_map/ppermute | solution.py:264
  75.7 3.6 %collective-permute-done.12 = f32[16,32]{1,0:T(8,128)S(1)} collective-permute-done((f32[16,32]{1,0:T(8,128)S(1)}, f32[16,32]{1,0:T(8,128)S(1)}, u32[]{:S(2)}, u32[]{:S(2)}) %collective-permute-start.12) | collective-permute-done | bytes 2080 | tf_op jit(solution)/shard_map/ppermute | solution.py:264
  79.3 43.2 %collective-permute-done.16.refs_2_ = bf16[2,72,1024]{2,1,0:T(8,128)(2,1)S(1)} collective-permute-done((bf16[2,72,1024]{2,1,0:T(8,128)(2,1)S(1)}, bf16[2,72,1024]{2,1,0:T(8,128)(2,1)S(1)}, u32[]{:S(2)}, u32[]{:S(2)}) %collective-permute-start.16) | collective-permute-done | bytes 294944 | tf_op jit(solution)/shard_map/ppermute | solution.py:264
  123.2 2.6 collective-permute-start.15
  125.8 1.5 collective-permute-start.13
  127.3 13.5 %collective-permute-done.15.far3_ref = f32[16,32]{1,0:T(8,128)S(1)} collective-permute-done((f32[16,32]{1,0:T(8,128)S(1)}, f32[16,32]{1,0:T(8,128)S(1)}, u32[]{:S(2)}, u32[]{:S(2)}) %collective-permute-start.15) | collective-permute-done | bytes 2080 | tf_op jit(solution)/shard_map/ppermute | solution.py:264
  141.4 6.2 %shard_map.132 = (bf16[16,16]{1,0:T(8,128)(2,1)}, bf16[256,256]{1,0:T(8,128)(2,1)}, bf16[16,128,1024]{2,1,0:T(8,128)(2,1)}) custom-call(f32[16,32]{1,0:T(8,128)} %copy-done.13, f32[16,32]{1,0:T(8,128)} %copy-done.18, f32[16,32]{1,0:T(8,128)} %copy-done.17, f32[16,32]{1,0:T(8,128)} %copy-done.16, bf16[16,128,1024]{2,1,0:T(8,128)(2,1)} %all-to-all-done.1.x_ref), custom_call_target="tpu_custom_call" | custom-call | flops 1 | bytes 1 | tf_op jit(solution)/shard_map/pallas_call | solution.py:126
  147.6 5.9 %all-to-all-start.2 = ((bf16[16,128,1024]{2,1,0:T(8,128)(2,1)}), bf16[16,128,1024]{2,1,0:T(8,128)(2,1)}, u32[]{:S(2)}, u32[]{:S(2)}) async-start(bf16[16,128,1024]{2,1,0:T(8,128)(2,1)} %get-tuple-element.35), calls=%async_computation.2 | async-start | bytes 8388608 | tf_op jit(solution)/shard_map/all_to_all | solution.py:259
  153.5 2.9 %shard_map.133 = bf16[16,32,1024]{2,1,0:T(8,128)(2,1)} custom-call(bf16[256,256]{1,0:T(8,128)(2,1)} %get-tuple-element.29.spread_ref, bf16[16,32,1024]{2,1,0:T(8,128)(2,1)} %all-to-all-done.x_ref), custom_call_target="tpu_custom_call" | custom-call | flops 1 | bytes 1 | tf_op jit(solution)/shard_map/pallas_call | solution.py:52
  161.3 13.0 %collective-permute-done.20 = bf16[4,32,1024]{2,1,0:T(8,128)(2,1)S(1)} collective-permute-done((bf16[4,32,1024]{2,1,0:T(8,128)(2,1)S(1)}, bf16[4,32,1024]{2,1,0:T(8,128)(2,1)S(1)}, u32[]{:S(2)}, u32[]{:S(2)}) %collective-permute-start.20) | collective-permute-done | bytes 262176 | tf_op jit(solution)/shard_map/ppermute | solution.py:264
  174.3 12.2 %collective-permute-done.19 = bf16[4,32,1024]{2,1,0:T(8,128)(2,1)S(1)} collective-permute-done((bf16[4,32,1024]{2,1,0:T(8,128)(2,1)S(1)}, bf16[4,32,1024]{2,1,0:T(8,128)(2,1)S(1)}, u32[]{:S(2)}, u32[]{:S(2)}) %collective-permute-start.19) | collective-permute-done | bytes 262176 | tf_op jit(solution)/shard_map/ppermute | solution.py:264
  186.8 1.5 collective-permute-start.24
  190.3 7.7 %collective-permute-start.21 = (bf16[4,32,1024]{2,1,0:T(8,128)(2,1)}, bf16[4,32,1024]{2,1,0:T(8,128)(2,1)S(1)}, u32[]{:S(2)}, u32[]{:S(2)}) collective-permute-start(bf16[4,32,1024]{2,1,0:T(8,128)(2,1)} %pad_maximum_fusion.5), channel_id=1, source_target_pairs={{0,8},{2,10},{4,12},{6,14},{8,0},{10,2},{12,4},{14,6},{16,24},{18,... | collective-permute-start | bytes 786440 | tf_op jit(solution)/shard_map/ppermute | solution.py:264
  198.8 5.0 %collective-permute-start.22 = (bf16[4,32,1024]{2,1,0:T(8,128)(2,1)}, bf16[4,32,1024]{2,1,0:T(8,128)(2,1)S(1)}, u32[]{:S(2)}, u32[]{:S(2)}) collective-permute-start(bf16[4,32,1024]{2,1,0:T(8,128)(2,1)} %pad_maximum_fusion.6), channel_id=1, source_target_pairs={{0,16},{2,18},{4,20},{6,22},{8,24},{10,26},{12,28},{14,30},{16,0},... | collective-permute-start | bytes 786440 | tf_op jit(solution)/shard_map/ppermute | solution.py:264
  205.0 24.5 %collective-permute-done.24.refs_4_ = bf16[8,72,1024]{2,1,0:T(8,128)(2,1)S(1)} collective-permute-done((bf16[8,72,1024]{2,1,0:T(8,128)(2,1)S(1)}, bf16[8,72,1024]{2,1,0:T(8,128)(2,1)S(1)}, u32[]{:S(2)}, u32[]{:S(2)}) %collective-permute-start.24) | collective-permute-done | bytes 1179680 | tf_op jit(solution)/shard_map/ppermute | solution.py:264
  230.5 3.6 %shard_map.135 = bf16[72,1024]{1,0:T(8,128)(2,1)} custom-call(f32[16]{0:T(128)} %fusion.1.column_ref, bf16[1,72,1024]{2,1,0:T(8,128)(2,1)} %copy-done.6, bf16[1,72,1024]{2,1,0:T(8,128)(2,1)} %copy-done.8, bf16[2,72,1024]{2,1,0:T(8,128)(2,1)} %copy-done.7, bf16[4,72,1024]{2,1,0:T(8,128)(2,1)} %copy-done.9, bf16[8,72,1024]{2,1,0:T(8,128)(2,1)} %copy-done.10), custom_call_target="tpu_custom_call" | custom-call | flops 1 | bytes 1 | tf_op jit(solution)/shard_map/pallas_call | solution.py:172
  235.6 1.6 slice_bitcast_fusion
  237.1 20.2 %all-to-all-done.2.x_ref = bf16[16,128,1024]{2,1,0:T(8,128)(2,1)} async-done(((bf16[16,128,1024]{2,1,0:T(8,128)(2,1)}), bf16[16,128,1024]{2,1,0:T(8,128)(2,1)}, u32[]{:S(2)}, u32[]{:S(2)}) %all-to-all-start.2) | async-done | bytes 4194336 | tf_op jit(solution)/shard_map/all_to_all | solution.py:259
  257.4 3.7 %shard_map.134 = bf16[16,128,1024]{2,1,0:T(8,128)(2,1)} custom-call(bf16[16,128,1024]{2,1,0:T(8,128)(2,1)} %all-to-all-done.2.x_ref), custom_call_target="tpu_custom_call" | custom-call | flops 1 | bytes 1 | tf_op jit(solution)/shard_map/pallas_call | solution.py:52
  262.4 5.1 %collective-permute-done.23 = bf16[4,32,1024]{2,1,0:T(8,128)(2,1)S(1)} collective-permute-done((bf16[4,32,1024]{2,1,0:T(8,128)(2,1)}, bf16[4,32,1024]{2,1,0:T(8,128)(2,1)S(1)}, u32[]{:S(2)}, u32[]{:S(2)}) %collective-permute-start.23) | collective-permute-done | bytes 262176 | tf_op jit(solution)/shard_map/ppermute | solution.py:264
  (118 shorter events, 29.7 us)
Async XLA Ops:
  0.7 38.9 %all-to-all-start = ((bf16[16,32,1024]{2,1,0:T(8,128)(2,1)}), bf16[16,32,1024]{2,1,0:T(8,128)(2,1)}, u32[]{:S(2)}, u32[]{:S(2)}) async-start(bf16[16,32,1024]{2,1,0:T(8,128)(2,1)} %bitcast.117), calls=%async_computation | async-start | bytes 2097152 | tf_op jit(solution)/shard_map/all_to_all | solution.py:259
  8.9 2.0 collective-permute-start
  9.9 2.1 collective-permute-start.1
  19.1 1.3 collective-permute-start.2
  20.9 7.0 %collective-permute-start.3 = (f32[4,2,1024]{2,1,0:T(2,128)S(1)}, f32[4,2,1024]{2,1,0:T(2,128)S(1)}, u32[]{:S(2)}, u32[]{:S(2)}) collective-permute-start(f32[4,2,1024]{2,1,0:T(2,128)S(1)} %get-tuple-element.84), channel_id=1, source_target_pairs={{0,8},{2,10},{4,12},{6,14},{8,0},{10,2},{12,4},{14,6},{16,24},{18,... | collective-permute-start | bytes 98312 | tf_op jit(solution)/shard_map/ppermute | solution.py:264
  21.5 14.9 %collective-permute-start.4 = (f32[4,2,1024]{2,1,0:T(2,128)S(1)}, f32[4,2,1024]{2,1,0:T(2,128)S(1)}, u32[]{:S(2)}, u32[]{:S(2)}) collective-permute-start(f32[4,2,1024]{2,1,0:T(2,128)S(1)} %get-tuple-element.85), channel_id=1, source_target_pairs={{0,16},{2,18},{4,20},{6,22},{8,24},{10,26},{12,28},{14,30},{16,0},... | collective-permute-start | bytes 98312 | tf_op jit(solution)/shard_map/ppermute | solution.py:264
  23.9 15.6 %collective-permute-start.5 = (f32[4,2,1024]{2,1,0:T(2,128)S(1)}, f32[4,2,1024]{2,1,0:T(2,128)S(1)}, u32[]{:S(2)}, u32[]{:S(2)}) collective-permute-start(f32[4,2,1024]{2,1,0:T(2,128)S(1)} %get-tuple-element.86), channel_id=1, source_target_pairs={{0,24},{2,26},{4,28},{6,30},{8,16},{10,18},{12,20},{14,22},{16,8},... | collective-permute-start | bytes 98312 | tf_op jit(solution)/shard_map/ppermute | solution.py:264
  24.5 162.1 %copy-start.6 = (bf16[1,72,1024]{2,1,0:T(8,128)(2,1)}, bf16[1,72,1024]{2,1,0:T(8,128)(2,1)S(1)}, u32[]{:S(2)}) copy-start(bf16[1,72,1024]{2,1,0:T(8,128)(2,1)S(1)} %maximum_bitcast_fusion.refs_0_) | copy-start | bytes 442372
  24.5 15.0 %collective-permute-start.6 = (bf16[1,72,1024]{2,1,0:T(8,128)(2,1)S(1)}, bf16[1,72,1024]{2,1,0:T(8,128)(2,1)S(1)}, u32[]{:S(2)}, u32[]{:S(2)}) collective-permute-start(bf16[1,72,1024]{2,1,0:T(8,128)(2,1)S(1)} %maximum_bitcast_fusion.refs_0_), channel_id=1, source_target_pairs={{0,16},{2,18},{4,20},{6,22},{8,24},{10,26},{12,28},{14,30},{16,0},... | collective-permute-start | bytes 442376 | tf_op jit(solution)/shard_map/ppermute | solution.py:264
  39.5 147.1 %copy-start.8 = (bf16[1,72,1024]{2,1,0:T(8,128)(2,1)}, bf16[1,72,1024]{2,1,0:T(8,128)(2,1)S(1)}, u32[]{:S(2)}) copy-start(bf16[1,72,1024]{2,1,0:T(8,128)(2,1)S(1)} %collective-permute-done.6.refs_1_) | copy-start | bytes 442372
  39.5 101.3 %all-to-all-start.1 = ((bf16[16,128,1024]{2,1,0:T(8,128)(2,1)}), bf16[16,128,1024]{2,1,0:T(8,128)(2,1)}, u32[]{:S(2)}, u32[]{:S(2)}) async-start(bf16[16,128,1024]{2,1,0:T(8,128)(2,1)} %bitcast.112), calls=%async_computation.1 | async-start | bytes 8388608 | tf_op jit(solution)/shard_map/all_to_all | solution.py:259
  48.2 13.5 %collective-permute-start.9 = (f32[4,2,1024]{2,1,0:T(2,128)S(1)}, f32[4,2,1024]{2,1,0:T(2,128)S(1)}, u32[]{:S(2)}, u32[]{:S(2)}) collective-permute-start(f32[4,2,1024]{2,1,0:T(2,128)S(1)} %get-tuple-element.76), channel_id=1, source_target_pairs={{0,6},{2,4},{4,2},{6,0},{8,14},{10,12},{12,10},{14,8},{16,22},{18,... | collective-permute-start | bytes 98312 | tf_op jit(solution)/shard_map/ppermute | solution.py:264
  49.7 17.7 %collective-permute-start.8 = (f32[4,2,1024]{2,1,0:T(2,128)S(1)}, f32[4,2,1024]{2,1,0:T(2,128)S(1)}, u32[]{:S(2)}, u32[]{:S(2)}) collective-permute-start(f32[4,2,1024]{2,1,0:T(2,128)S(1)} %get-tuple-element.77), channel_id=1, source_target_pairs={{0,4},{2,6},{4,0},{6,2},{8,12},{10,14},{12,8},{14,10},{16,20},{18,... | collective-permute-start | bytes 98312 | tf_op jit(solution)/shard_map/ppermute | solution.py:264
  51.1 16.2 %collective-permute-start.7 = (f32[4,2,1024]{2,1,0:T(2,128)S(1)}, f32[4,2,1024]{2,1,0:T(2,128)S(1)}, u32[]{:S(2)}, u32[]{:S(2)}) collective-permute-start(f32[4,2,1024]{2,1,0:T(2,128)S(1)} %get-tuple-element.78), channel_id=1, source_target_pairs={{0,2},{2,0},{4,6},{6,4},{8,10},{10,8},{12,14},{14,12},{16,18},{18,... | collective-permute-start | bytes 98312 | tf_op jit(solution)/shard_map/ppermute | solution.py:264
  51.7 70.8 %collective-permute-start.16 = (bf16[2,72,1024]{2,1,0:T(8,128)(2,1)S(1)}, bf16[2,72,1024]{2,1,0:T(8,128)(2,1)S(1)}, u32[]{:S(2)}, u32[]{:S(2)}) collective-permute-start(bf16[2,72,1024]{2,1,0:T(8,128)(2,1)S(1)} %pad_maximum_fusion.3), channel_id=1, source_target_pairs={{0,8},{2,10},{4,12},{6,14},{8,0},{10,2},{12,4},{14,6},{16,24},{18,... | collective-permute-start | bytes 884744 | tf_op jit(solution)/shard_map/ppermute | solution.py:264
  69.9 1.4 collective-permute-start.10
  72.0 3.7 %collective-permute-start.11 = (f32[16,32]{1,0:T(8,128)S(1)}, f32[16,32]{1,0:T(8,128)S(1)}, u32[]{:S(2)}, u32[]{:S(2)}) collective-permute-start(f32[16,32]{1,0:T(8,128)S(1)} %add.198), channel_id=1, source_target_pairs={{0,2},{2,0},{4,6},{6,4},{8,10},{10,8},{12,14},{14,12},{16,18},{18,... | collective-permute-start | bytes 6152 | tf_op jit(solution)/shard_map/ppermute | solution.py:264
  75.7 3.7 %collective-permute-start.12 = (f32[16,32]{1,0:T(8,128)S(1)}, f32[16,32]{1,0:T(8,128)S(1)}, u32[]{:S(2)}, u32[]{:S(2)}) collective-permute-start(f32[16,32]{1,0:T(8,128)S(1)} %add.199), channel_id=1, source_target_pairs={{0,4},{2,6},{4,0},{6,2},{8,12},{10,14},{12,8},{14,10},{16,20},{18,... | collective-permute-start | bytes 6152 | tf_op jit(solution)/shard_map/ppermute | solution.py:264
  79.3 61.5 %copy-start.13 = (f32[16,32]{1,0:T(8,128)}, f32[16,32]{1,0:T(8,128)S(1)}, u32[]{:S(2)}) copy-start(f32[16,32]{1,0:T(8,128)S(1)} %add.200.own_ref) | copy-start | bytes 6148
  122.5 64.1 %copy-start.7 = (bf16[2,72,1024]{2,1,0:T(8,128)(2,1)}, bf16[2,72,1024]{2,1,0:T(8,128)(2,1)S(1)}, u32[]{:S(2)}) copy-start(bf16[2,72,1024]{2,1,0:T(8,128)(2,1)S(1)} %collective-permute-done.16.refs_2_) | copy-start | bytes 884740
  122.6 25.0 %collective-permute-start.17 = (bf16[4,72,1024]{2,1,0:T(8,128)(2,1)S(1)}, bf16[4,72,1024]{2,1,0:T(8,128)(2,1)S(1)}, u32[]{:S(2)}, u32[]{:S(2)}) collective-permute-start(bf16[4,72,1024]{2,1,0:T(8,128)(2,1)S(1)} %pad_maximum_fusion.2), channel_id=1, source_target_pairs={{0,4},{2,6},{4,0},{6,2},{8,12},{10,14},{12,8},{14,10},{16,20},{18,... | collective-permute-start | bytes 1769480 | tf_op jit(solution)/shard_map/ppermute | solution.py:264
  123.2 17.6 %collective-permute-start.15 = (f32[16,32]{1,0:T(8,128)S(1)}, f32[16,32]{1,0:T(8,128)S(1)}, u32[]{:S(2)}, u32[]{:S(2)}) collective-permute-start(f32[16,32]{1,0:T(8,128)S(1)} %add.200.own_ref), channel_id=1, source_target_pairs={{0,24},{2,26},{4,28},{6,30},{8,16},{10,18},{12,20},{14,22},{16,8},... | collective-permute-start | bytes 6152 | tf_op jit(solution)/shard_map/ppermute | solution.py:264
  125.8 15.0 %collective-permute-start.14 = (f32[16,32]{1,0:T(8,128)S(1)}, f32[16,32]{1,0:T(8,128)S(1)}, u32[]{:S(2)}, u32[]{:S(2)}) collective-permute-start(f32[16,32]{1,0:T(8,128)S(1)} %add.200.own_ref), channel_id=1, source_target_pairs={{0,16},{2,18},{4,20},{6,22},{8,24},{10,26},{12,28},{14,30},{16,0},... | collective-permute-start | bytes 6152 | tf_op jit(solution)/shard_map/ppermute | solution.py:264
  125.8 15.0 %collective-permute-start.13 = (f32[16,32]{1,0:T(8,128)S(1)}, f32[16,32]{1,0:T(8,128)S(1)}, u32[]{:S(2)}, u32[]{:S(2)}) collective-permute-start(f32[16,32]{1,0:T(8,128)S(1)} %add.200.own_ref), channel_id=1, source_target_pairs={{0,8},{2,10},{4,12},{6,14},{8,0},{10,2},{12,4},{14,6},{16,24},{18,... | collective-permute-start | bytes 6152 | tf_op jit(solution)/shard_map/ppermute | solution.py:264
  147.6 109.7 %all-to-all-start.2 = ((bf16[16,128,1024]{2,1,0:T(8,128)(2,1)}), bf16[16,128,1024]{2,1,0:T(8,128)(2,1)}, u32[]{:S(2)}, u32[]{:S(2)}) async-start(bf16[16,128,1024]{2,1,0:T(8,128)(2,1)} %get-tuple-element.35), calls=%async_computation.2 | async-start | bytes 8388608 | tf_op jit(solution)/shard_map/all_to_all | solution.py:259
  157.7 16.5 %collective-permute-start.20 = (bf16[4,32,1024]{2,1,0:T(8,128)(2,1)S(1)}, bf16[4,32,1024]{2,1,0:T(8,128)(2,1)S(1)}, u32[]{:S(2)}, u32[]{:S(2)}) collective-permute-start(bf16[4,32,1024]{2,1,0:T(8,128)(2,1)S(1)} %get-tuple-element.66), channel_id=1, source_target_pairs={{0,6},{2,4},{4,2},{6,0},{8,14},{10,12},{12,10},{14,8},{16,22},{18,... | collective-permute-start | bytes 786440 | tf_op jit(solution)/shard_map/ppermute | solution.py:264
  159.2 27.2 %collective-permute-start.19 = (bf16[4,32,1024]{2,1,0:T(8,128)(2,1)S(1)}, bf16[4,32,1024]{2,1,0:T(8,128)(2,1)S(1)}, u32[]{:S(2)}, u32[]{:S(2)}) collective-permute-start(bf16[4,32,1024]{2,1,0:T(8,128)(2,1)S(1)} %get-tuple-element.67), channel_id=1, source_target_pairs={{0,4},{2,6},{4,0},{6,2},{8,12},{10,14},{12,8},{14,10},{16,20},{18,... | collective-permute-start | bytes 786440 | tf_op jit(solution)/shard_map/ppermute | solution.py:264
  160.7 25.8 %collective-permute-start.18 = (bf16[4,32,1024]{2,1,0:T(8,128)(2,1)S(1)}, bf16[4,32,1024]{2,1,0:T(8,128)(2,1)S(1)}, u32[]{:S(2)}, u32[]{:S(2)}) collective-permute-start(bf16[4,32,1024]{2,1,0:T(8,128)(2,1)S(1)} %get-tuple-element.68), channel_id=1, source_target_pairs={{0,2},{2,0},{4,6},{6,4},{8,10},{10,8},{12,14},{14,12},{16,18},{18,... | collective-permute-start | bytes 786440 | tf_op jit(solution)/shard_map/ppermute | solution.py:264
  186.8 42.7 %collective-permute-start.24 = (bf16[8,72,1024]{2,1,0:T(8,128)(2,1)S(1)}, bf16[8,72,1024]{2,1,0:T(8,128)(2,1)S(1)}, u32[]{:S(2)}, u32[]{:S(2)}) collective-permute-start(bf16[8,72,1024]{2,1,0:T(8,128)(2,1)S(1)} %pad_maximum_fusion), channel_id=1, source_target_pairs={{0,2},{2,0},{4,6},{6,4},{8,10},{10,8},{12,14},{14,12},{16,18},{18,... | collective-permute-start | bytes 3538952 | tf_op jit(solution)/shard_map/ppermute | solution.py:264
  190.3 70.8 %collective-permute-start.21 = (bf16[4,32,1024]{2,1,0:T(8,128)(2,1)}, bf16[4,32,1024]{2,1,0:T(8,128)(2,1)S(1)}, u32[]{:S(2)}, u32[]{:S(2)}) collective-permute-start(bf16[4,32,1024]{2,1,0:T(8,128)(2,1)} %pad_maximum_fusion.5), channel_id=1, source_target_pairs={{0,8},{2,10},{4,12},{6,14},{8,0},{10,2},{12,4},{14,6},{16,24},{18,... | collective-permute-start | bytes 786440 | tf_op jit(solution)/shard_map/ppermute | solution.py:264
  198.8 63.6 %collective-permute-start.22 = (bf16[4,32,1024]{2,1,0:T(8,128)(2,1)}, bf16[4,32,1024]{2,1,0:T(8,128)(2,1)S(1)}, u32[]{:S(2)}, u32[]{:S(2)}) collective-permute-start(bf16[4,32,1024]{2,1,0:T(8,128)(2,1)} %pad_maximum_fusion.6), channel_id=1, source_target_pairs={{0,16},{2,18},{4,20},{6,22},{8,24},{10,26},{12,28},{14,30},{16,0},... | collective-permute-start | bytes 786440 | tf_op jit(solution)/shard_map/ppermute | solution.py:264
  204.4 63.0 %collective-permute-start.23 = (bf16[4,32,1024]{2,1,0:T(8,128)(2,1)}, bf16[4,32,1024]{2,1,0:T(8,128)(2,1)S(1)}, u32[]{:S(2)}, u32[]{:S(2)}) collective-permute-start(bf16[4,32,1024]{2,1,0:T(8,128)(2,1)} %pad_maximum_fusion.7), channel_id=1, source_target_pairs={{0,24},{2,26},{4,28},{6,30},{8,16},{10,18},{12,20},{14,22},{16,8},... | collective-permute-start | bytes 786440 | tf_op jit(solution)/shard_map/ppermute | solution.py:264
  (16 other events, 93.8 us)

commit v4 on v3

--- a/solution.py
+++ b/solution.py
@@ -151,34 +151,17 @@
     ).astype(jnp.bfloat16)
 
 
-def mix_one_kernel(column_ref, *refs):
-    y_ref = refs[-1]
-    blocks = [ref[...].astype(jnp.float32) for ref in refs[:-1]]
-    members = column_ref.shape[0]
-    mean = sum(jnp.sum(block, axis=0) for block in blocks) * (1.0 / members)
+def mix_one(column, blocks):
+    full = [block.astype(jnp.float32) for block in blocks]
+    mean = sum(jnp.sum(block, axis=0) for block in full) * (1.0 / column.shape[0])
     total = jnp.zeros_like(mean)
     at = 0
-    for block in blocks:
-        for i in range(block.shape[0]):
-            center = (block[i] - mean).astype(jnp.bfloat16).astype(jnp.float32)
-            total = total + center * column_ref[at]
-            at += 1
-    y_ref[...] = total.astype(jnp.bfloat16)
-
-
-def mix_one(column, blocks):
-    rows, width = blocks[0].shape[1:]
-    step = rows if rows % ROWS else ROWS
-    return pl.pallas_call(
-        mix_one_kernel,
-        grid=(rows // step,),
-        in_specs=[pl.BlockSpec(memory_space=pltpu.SMEM)]
-        + [pl.BlockSpec((x.shape[0], step, width), lambda i: (0, i, 0)) for x in blocks],
-        out_specs=pl.BlockSpec((step, width), lambda i: (i, 0)),
-        out_shape=jax.ShapeDtypeStruct((rows, width), jnp.bfloat16),
-        compiler_params=pltpu.CompilerParams(vmem_limit_bytes=VMEM),
-        cost_estimate=LIGHT,
-    )(column, *blocks)
+    for block in full:
+        count = block.shape[0]
+        center = (block - mean).astype(jnp.bfloat16).astype(jnp.float32)
+        total = total + jnp.sum(center * column[at : at + count, None, None], axis=0)
+        at += count
+    return total.astype(jnp.bfloat16)
 
 
 def first_kernel(scale, x_ref, w_ref, b_ref, y_ref):
@@ -316,8 +299,7 @@
         both = both.reshape((planes, PLANE) + both.shape[1:])
         parts = [pick(both, plane ^ i) for i in range(planes)]
         parts = jnp.stack([parts[0]] + [across(parts[i], i) for i in range(1, planes)])
-        pad = jnp.zeros((-(outs + 2) % 8, width), jnp.bfloat16)
-        small = jnp.concatenate([third_w.T, b_first, b_second, pad], axis=0)[None]
+        small = jnp.concatenate([third_w.T, b_first, b_second], axis=0)[None]
         held = [small, swap(after(small, both), "member", 8)]
         slabs_second, parts, held[1], got_first = lax.optimization_barrier(
             (slabs_second, parts, held[1], got_first)

time: 269 us -> 270 us (level); the launches traced: 269 us -> 266 us
  waiting for transfers between devices: 170 us -> 166 us
  other arithmetic: 4.69 us -> 8.48 us
  Pallas kernels: 24.9 us -> 21.2 us
    ppermute x25, waiting for transfers between devices: 149 us -> 142 us  [swap(): return lax.ppermute(x, axis, [(i, i ^ bit) for i in range(count)])]
    all_to_all x3, waiting for transfers between devices: 20.2 us -> 24.4 us  [exchange(): return lax.all_to_all(x, 'member', split_axis=0, concat_axis=0, tiled=True)]
    pallas_call x1 -> x0, Pallas kernels: 3.64 us -> none  [mix_one(): pl.pallas_call(mix_one_kernel, grid=(rows // step,), in_specs=[pl.BlockSp...]
    reduce_sum x0 -> x6, other arithmetic: none -> 3.23 us  [the longest x3 1.77 us: mix_one(): total = total + jnp.sum(center * column[at:at + count, None, None], axis=0)]
  transfers between devices with their start and end apart: 28 -> 28, of which waited for: 18 -> 19; matrix products, arithmetic and copies ran while one was open for 4% -> 5% of each run, Pallas kernels for 9% -> 8%
where the time goes in v4:
time: 270 us; the launch traced here: 266 us
  waiting for transfers between devices  166 us (61%)
  starting transfers between devices  58.2 us (22%)
  Pallas kernels  21.2 us (8%)
  local copies, waits for them, and re-layouts  10.5 us (4%)
  other arithmetic  8.48 us (3%)
    ppermute x25, waiting for transfers between devices, swap(): return lax.ppermute(x, axis, [(i, i ^ bit) for i in range(count)])  142 us
    ppermute x25, starting transfers between devices, swap(): return lax.ppermute(x, axis, [(i, i ^ bit) for i in range(count)])  37.3 us
    all_to_all x3, waiting for transfers between devices, exchange(): return lax.all_to_all(x, 'member', split_axis=0, concat_axis=0, tiled=True)  24.4 us
    all_to_all x3, starting transfers between devices, exchange(): return lax.all_to_all(x, 'member', split_axis=0, concat_axis=0, tiled=True)  20.9 us
    pallas_call x2, Pallas kernels, blocked(): pl.pallas_call(kernel, grid=(total // rows,), in_specs=[pl.BlockSpec(w.sh...  6.63 us
    pallas_call x1, Pallas kernels, solve(): pl.pallas_call(solve_kernel, in_specs=[vmem] * len(sums) + [anywhere], ou...  6.2 us
  transfers between devices with their start and end apart: 28, of which 19 were waited for; matrix products, arithmetic and copies ran while one was open for 5% of the time, Pallas kernels for 8%

profile of v4, /device:TPU:12, one launch (start us, length us, event | category | flops | bytes accessed | tf_op | source)
XLA Modules:
  0.0 265.6 jit_solution(17961729080536989708)
XLA Ops:
  0.7 7.3 %all-to-all-start = ((bf16[16,32,1024]{2,1,0:T(8,128)(2,1)}), bf16[16,32,1024]{2,1,0:T(8,128)(2,1)}, u32[]{:S(2)}, u32[]{:S(2)}) async-start(bf16[16,32,1024]{2,1,0:T(8,128)(2,1)} %bitcast.151), calls=%async_computation | async-start | bytes 2097152 | tf_op jit(solution)/shard_map/all_to_all | solution.py:242
  12.7 2.2 copy-done
  14.9 4.8 %shard_map.130 = f32[64,512]{1,0:T(8,128)S(1)} custom-call(s32[1]{0:T(128)} %bitcast.1.side_ref, bf16[512,512]{1,0:T(8,128)(2,1)S(1)} %shard_map.128.refs_0_, bf16[512,512]{1,0:T(8,128)(2,1)S(1)} %shard_map.129.refs_1_, bf16[512,512]{1,0:T(8,128)(2,1)S(1)} %collective-permute-done.refs_2_, bf16[512,512]{1,0:T(8,128)(2,1)S(1)} %collective-permute-done.1.refs_3_, ...), custom_call_target="tpu_custom_call" | custom-call | flops 1 | bytes 1 | tf_op jit(solution)/shard_map/pallas_call | solution.py:219
  22.2 2.4 collective-permute-start.4
  25.1 3.3 %collective-permute-start.6 = (bf16[1,66,1024]{2,1,0:T(8,128)(2,1)S(1)}, bf16[1,66,1024]{2,1,0:T(8,128)(2,1)S(1)}, u32[]{:S(2)}, u32[]{:S(2)}) collective-permute-start(bf16[1,66,1024]{2,1,0:T(8,128)(2,1)S(1)} %maximum_bitcast_fusion), channel_id=1, source_target_pairs={{0,16},{2,18},{4,20},{6,22},{8,24},{10,26},{12,28},{14,30},{16,0},... | collective-permute-start | bytes 405512 | tf_op jit(solution)/shard_map/ppermute | solution.py:247
  28.5 8.0 %collective-permute-done.4 = f32[4,2,1024]{2,1,0:T(2,128)S(1)} collective-permute-done((f32[4,2,1024]{2,1,0:T(2,128)S(1)}, f32[4,2,1024]{2,1,0:T(2,128)S(1)}, u32[]{:S(2)}, u32[]{:S(2)}) %collective-permute-start.4) | collective-permute-done | bytes 32800 | tf_op jit(solution)/shard_map/ppermute | solution.py:247
  36.4 3.0 %collective-permute-done.5 = f32[4,2,1024]{2,1,0:T(2,128)S(1)} collective-permute-done((f32[4,2,1024]{2,1,0:T(2,128)S(1)}, f32[4,2,1024]{2,1,0:T(2,128)S(1)}, u32[]{:S(2)}, u32[]{:S(2)}) %collective-permute-start.5) | collective-permute-done | bytes 32800 | tf_op jit(solution)/shard_map/ppermute | solution.py:247
  39.5 7.9 %all-to-all-start.1 = ((bf16[16,128,1024]{2,1,0:T(8,128)(2,1)}), bf16[16,128,1024]{2,1,0:T(8,128)(2,1)}, u32[]{:S(2)}, u32[]{:S(2)}) async-start(bf16[16,128,1024]{2,1,0:T(8,128)(2,1)} %bitcast.146), calls=%async_computation.1 | async-start | bytes 8388608 | tf_op jit(solution)/shard_map/all_to_all | solution.py:242
  48.2 1.5 collective-permute-start.7
  52.4 9.1 %collective-permute-done.7 = f32[4,2,1024]{2,1,0:T(2,128)S(1)} collective-permute-done((f32[4,2,1024]{2,1,0:T(2,128)S(1)}, f32[4,2,1024]{2,1,0:T(2,128)S(1)}, u32[]{:S(2)}, u32[]{:S(2)}) %collective-permute-start.7) | collective-permute-done | bytes 32800 | tf_op jit(solution)/shard_map/ppermute | solution.py:247
  61.4 5.9 %collective-permute-done.8 = f32[4,2,1024]{2,1,0:T(2,128)S(1)} collective-permute-done((f32[4,2,1024]{2,1,0:T(2,128)S(1)}, f32[4,2,1024]{2,1,0:T(2,128)S(1)}, u32[]{:S(2)}, u32[]{:S(2)}) %collective-permute-start.8) | collective-permute-done | bytes 32800 | tf_op jit(solution)/shard_map/ppermute | solution.py:247
  68.2 1.8 shard_map.131
  73.0 2.7 %collective-permute-done.11 = f32[16,32]{1,0:T(8,128)S(1)} collective-permute-done((f32[16,32]{1,0:T(8,128)S(1)}, f32[16,32]{1,0:T(8,128)S(1)}, u32[]{:S(2)}, u32[]{:S(2)}) %collective-permute-start.11) | collective-permute-done | bytes 2080 | tf_op jit(solution)/shard_map/ppermute | solution.py:247
  75.7 3.6 %collective-permute-done.12 = f32[16,32]{1,0:T(8,128)S(1)} collective-permute-done((f32[16,32]{1,0:T(8,128)S(1)}, f32[16,32]{1,0:T(8,128)S(1)}, u32[]{:S(2)}, u32[]{:S(2)}) %collective-permute-start.12) | collective-permute-done | bytes 2080 | tf_op jit(solution)/shard_map/ppermute | solution.py:247
  79.3 43.1 %collective-permute-done.16 = bf16[2,66,1024]{2,1,0:T(8,128)(2,1)S(1)} collective-permute-done((bf16[2,66,1024]{2,1,0:T(8,128)(2,1)S(1)}, bf16[2,66,1024]{2,1,0:T(8,128)(2,1)S(1)}, u32[]{:S(2)}, u32[]{:S(2)}) %collective-permute-start.16) | collective-permute-done | bytes 270368 | tf_op jit(solution)/shard_map/ppermute | solution.py:247
  123.6 4.0 %collective-permute-start.14 = (f32[16,32]{1,0:T(8,128)S(1)}, f32[16,32]{1,0:T(8,128)S(1)}, u32[]{:S(2)}, u32[]{:S(2)}) collective-permute-start(f32[16,32]{1,0:T(8,128)S(1)} %add.235.own_ref), channel_id=1, source_target_pairs={{0,16},{2,18},{4,20},{6,22},{8,24},{10,26},{12,28},{14,30},{16,0},... | collective-permute-start | bytes 6152 | tf_op jit(solution)/shard_map/ppermute | solution.py:247
  127.7 10.4 %collective-permute-done.14.far2_ref = f32[16,32]{1,0:T(8,128)S(1)} collective-permute-done((f32[16,32]{1,0:T(8,128)S(1)}, f32[16,32]{1,0:T(8,128)S(1)}, u32[]{:S(2)}, u32[]{:S(2)}) %collective-permute-start.14) | collective-permute-done | bytes 2080 | tf_op jit(solution)/shard_map/ppermute | solution.py:247
  138.1 2.8 %collective-permute-done.15.far3_ref = f32[16,32]{1,0:T(8,128)S(1)} collective-permute-done((f32[16,32]{1,0:T(8,128)S(1)}, f32[16,32]{1,0:T(8,128)S(1)}, u32[]{:S(2)}, u32[]{:S(2)}) %collective-permute-start.15) | collective-permute-done | bytes 2080 | tf_op jit(solution)/shard_map/ppermute | solution.py:247
  141.5 6.2 %shard_map.132 = (bf16[16,16]{1,0:T(8,128)(2,1)}, bf16[256,256]{1,0:T(8,128)(2,1)}, bf16[16,128,1024]{2,1,0:T(8,128)(2,1)}) custom-call(f32[16,32]{1,0:T(8,128)} %copy-done.9, f32[16,32]{1,0:T(8,128)} %copy-done.12, f32[16,32]{1,0:T(8,128)} %copy-done.13, f32[16,32]{1,0:T(8,128)} %copy-done.14, bf16[16,128,1024]{2,1,0:T(8,128)(2,1)} %all-to-all-done.1.x_ref), custom_call_target="tpu_custom_call" | custom-call | flops 1 | bytes 1 | tf_op jit(solution)/shard_map/pallas_call | solution.py:126
  147.7 5.7 %all-to-all-start.2 = ((bf16[16,128,1024]{2,1,0:T(8,128)(2,1)}), bf16[16,128,1024]{2,1,0:T(8,128)(2,1)}, u32[]{:S(2)}, u32[]{:S(2)}) async-start(bf16[16,128,1024]{2,1,0:T(8,128)(2,1)} %get-tuple-element.35), calls=%async_computation.2 | async-start | bytes 8388608 | tf_op jit(solution)/shard_map/all_to_all | solution.py:242
  153.5 2.9 %shard_map.133 = bf16[16,32,1024]{2,1,0:T(8,128)(2,1)} custom-call(bf16[256,256]{1,0:T(8,128)(2,1)} %get-tuple-element.29.spread_ref, bf16[16,32,1024]{2,1,0:T(8,128)(2,1)} %all-to-all-done.x_ref), custom_call_target="tpu_custom_call" | custom-call | flops 1 | bytes 1 | tf_op jit(solution)/shard_map/pallas_call | solution.py:52
  157.7 1.5 collective-permute-start.18
  162.5 10.7 %collective-permute-done.18 = bf16[4,32,1024]{2,1,0:T(8,128)(2,1)S(1)} collective-permute-done((bf16[4,32,1024]{2,1,0:T(8,128)(2,1)S(1)}, bf16[4,32,1024]{2,1,0:T(8,128)(2,1)S(1)}, u32[]{:S(2)}, u32[]{:S(2)}) %collective-permute-start.18) | collective-permute-done | bytes 262176 | tf_op jit(solution)/shard_map/ppermute | solution.py:247
  173.2 13.1 %collective-permute-done.19 = bf16[4,32,1024]{2,1,0:T(8,128)(2,1)S(1)} collective-permute-done((bf16[4,32,1024]{2,1,0:T(8,128)(2,1)S(1)}, bf16[4,32,1024]{2,1,0:T(8,128)(2,1)S(1)}, u32[]{:S(2)}, u32[]{:S(2)}) %collective-permute-start.19) | collective-permute-done | bytes 262176 | tf_op jit(solution)/shard_map/ppermute | solution.py:247
  187.7 1.5 collective-permute-start.24
  190.3 7.1 %collective-permute-start.23 = (bf16[4,32,1024]{2,1,0:T(8,128)(2,1)S(1)}, bf16[4,32,1024]{2,1,0:T(8,128)(2,1)S(1)}, u32[]{:S(2)}, u32[]{:S(2)}) collective-permute-start(bf16[4,32,1024]{2,1,0:T(8,128)(2,1)S(1)} %pad_maximum_fusion.7), channel_id=1, source_target_pairs={{0,24},{2,26},{4,28},{6,30},{8,16},{10,18},{12,20},{14,22},{16,8},... | collective-permute-start | bytes 786440 | tf_op jit(solution)/shard_map/ppermute | solution.py:247
  197.5 5.6 %collective-permute-start.22 = (bf16[4,32,1024]{2,1,0:T(8,128)(2,1)S(1)}, bf16[4,32,1024]{2,1,0:T(8,128)(2,1)S(1)}, u32[]{:S(2)}, u32[]{:S(2)}) collective-permute-start(bf16[4,32,1024]{2,1,0:T(8,128)(2,1)S(1)} %pad_maximum_fusion.6), channel_id=1, source_target_pairs={{0,16},{2,18},{4,20},{6,22},{8,24},{10,26},{12,28},{14,30},{16,0},... | collective-permute-start | bytes 786440 | tf_op jit(solution)/shard_map/ppermute | solution.py:247
  205.4 21.8 %collective-permute-done.24 = bf16[8,66,1024]{2,0,1:T(8,128)(2,1)S(1)} collective-permute-done((bf16[8,66,1024]{2,0,1:T(8,128)(2,1)S(1)}, bf16[8,66,1024]{2,0,1:T(8,128)(2,1)S(1)}, u32[]{:S(2)}, u32[]{:S(2)}) %collective-permute-start.24) | collective-permute-done | bytes 1081376 | tf_op jit(solution)/shard_map/ppermute | solution.py:247
  232.6 24.4 %all-to-all-done.2.x_ref = bf16[16,128,1024]{2,1,0:T(8,128)(2,1)} async-done(((bf16[16,128,1024]{2,1,0:T(8,128)(2,1)}), bf16[16,128,1024]{2,1,0:T(8,128)(2,1)}, u32[]{:S(2)}, u32[]{:S(2)}) %all-to-all-start.2) | async-done | bytes 4194336 | tf_op jit(solution)/shard_map/all_to_all | solution.py:242
  257.0 3.7 %shard_map.134 = bf16[16,128,1024]{2,1,0:T(8,128)(2,1)} custom-call(bf16[16,128,1024]{2,1,0:T(8,128)(2,1)} %all-to-all-done.2.x_ref), custom_call_target="tpu_custom_call" | custom-call | flops 1 | bytes 1 | tf_op jit(solution)/shard_map/pallas_call | solution.py:52
  260.8 1.8 collective-permute-done.23
  262.5 1.8 collective-permute-done.22
  (123 shorter events, 32.8 us)
Async XLA Ops:
  0.6 7.4 %copy-start.1 = (bf16[1,512,1024]{2,1,0:T(8,128)(2,1)S(1)}, bf16[1,512,1024]{2,1,0:T(8,128)(2,1)}, u32[]{:S(2)}) copy-start(bf16[1,512,1024]{2,1,0:T(8,128)(2,1)} %param.10) | copy-start | bytes 3145732
  0.6 9.1 %copy-start.5 = (bf16[1,1024]{1,0:T(2,128)(2,1)S(1)}, bf16[1,1024]{1,0:T(2,128)(2,1)}, u32[]{:S(2)}) copy-start(bf16[1,1024]{1,0:T(2,128)(2,1)} %b_ref.3) | copy-start | bytes 6148
  0.7 38.8 %all-to-all-start = ((bf16[16,32,1024]{2,1,0:T(8,128)(2,1)}), bf16[16,32,1024]{2,1,0:T(8,128)(2,1)}, u32[]{:S(2)}, u32[]{:S(2)}) async-start(bf16[16,32,1024]{2,1,0:T(8,128)(2,1)} %bitcast.151), calls=%async_computation | async-start | bytes 2097152 | tf_op jit(solution)/shard_map/all_to_all | solution.py:242
  9.6 2.0 collective-permute-start
  10.7 2.1 collective-permute-start.1
  19.8 1.3 collective-permute-start.2
  21.5 6.9 %collective-permute-start.3 = (f32[4,2,1024]{2,1,0:T(2,128)S(1)}, f32[4,2,1024]{2,1,0:T(2,128)S(1)}, u32[]{:S(2)}, u32[]{:S(2)}) collective-permute-start(f32[4,2,1024]{2,1,0:T(2,128)S(1)} %get-tuple-element.84), channel_id=1, source_target_pairs={{0,8},{2,10},{4,12},{6,14},{8,0},{10,2},{12,4},{14,6},{16,24},{18,... | collective-permute-start | bytes 98312 | tf_op jit(solution)/shard_map/ppermute | solution.py:247
  22.2 14.2 %collective-permute-start.4 = (f32[4,2,1024]{2,1,0:T(2,128)S(1)}, f32[4,2,1024]{2,1,0:T(2,128)S(1)}, u32[]{:S(2)}, u32[]{:S(2)}) collective-permute-start(f32[4,2,1024]{2,1,0:T(2,128)S(1)} %get-tuple-element.85), channel_id=1, source_target_pairs={{0,16},{2,18},{4,20},{6,22},{8,24},{10,26},{12,28},{14,30},{16,0},... | collective-permute-start | bytes 98312 | tf_op jit(solution)/shard_map/ppermute | solution.py:247
  24.6 14.9 %collective-permute-start.5 = (f32[4,2,1024]{2,1,0:T(2,128)S(1)}, f32[4,2,1024]{2,1,0:T(2,128)S(1)}, u32[]{:S(2)}, u32[]{:S(2)}) collective-permute-start(f32[4,2,1024]{2,1,0:T(2,128)S(1)} %get-tuple-element.86), channel_id=1, source_target_pairs={{0,24},{2,26},{4,28},{6,30},{8,16},{10,18},{12,20},{14,22},{16,8},... | collective-permute-start | bytes 98312 | tf_op jit(solution)/shard_map/ppermute | solution.py:247
  25.1 14.4 %collective-permute-start.6 = (bf16[1,66,1024]{2,1,0:T(8,128)(2,1)S(1)}, bf16[1,66,1024]{2,1,0:T(8,128)(2,1)S(1)}, u32[]{:S(2)}, u32[]{:S(2)}) collective-permute-start(bf16[1,66,1024]{2,1,0:T(8,128)(2,1)S(1)} %maximum_bitcast_fusion), channel_id=1, source_target_pairs={{0,16},{2,18},{4,20},{6,22},{8,24},{10,26},{12,28},{14,30},{16,0},... | collective-permute-start | bytes 405512 | tf_op jit(solution)/shard_map/ppermute | solution.py:247
  39.5 101.4 %all-to-all-start.1 = ((bf16[16,128,1024]{2,1,0:T(8,128)(2,1)}), bf16[16,128,1024]{2,1,0:T(8,128)(2,1)}, u32[]{:S(2)}, u32[]{:S(2)}) async-start(bf16[16,128,1024]{2,1,0:T(8,128)(2,1)} %bitcast.146), calls=%async_computation.1 | async-start | bytes 8388608 | tf_op jit(solution)/shard_map/all_to_all | solution.py:242
  48.2 13.3 %collective-permute-start.7 = (f32[4,2,1024]{2,1,0:T(2,128)S(1)}, f32[4,2,1024]{2,1,0:T(2,128)S(1)}, u32[]{:S(2)}, u32[]{:S(2)}) collective-permute-start(f32[4,2,1024]{2,1,0:T(2,128)S(1)} %get-tuple-element.78), channel_id=1, source_target_pairs={{0,2},{2,0},{4,6},{6,4},{8,10},{10,8},{12,14},{14,12},{16,18},{18,... | collective-permute-start | bytes 98312 | tf_op jit(solution)/shard_map/ppermute | solution.py:247
  49.7 17.7 %collective-permute-start.8 = (f32[4,2,1024]{2,1,0:T(2,128)S(1)}, f32[4,2,1024]{2,1,0:T(2,128)S(1)}, u32[]{:S(2)}, u32[]{:S(2)}) collective-permute-start(f32[4,2,1024]{2,1,0:T(2,128)S(1)} %get-tuple-element.77), channel_id=1, source_target_pairs={{0,4},{2,6},{4,0},{6,2},{8,12},{10,14},{12,8},{14,10},{16,20},{18,... | collective-permute-start | bytes 98312 | tf_op jit(solution)/shard_map/ppermute | solution.py:247
  50.2 17.1 %collective-permute-start.9 = (f32[4,2,1024]{2,1,0:T(2,128)S(1)}, f32[4,2,1024]{2,1,0:T(2,128)S(1)}, u32[]{:S(2)}, u32[]{:S(2)}) collective-permute-start(f32[4,2,1024]{2,1,0:T(2,128)S(1)} %get-tuple-element.76), channel_id=1, source_target_pairs={{0,6},{2,4},{4,2},{6,0},{8,14},{10,12},{12,10},{14,8},{16,22},{18,... | collective-permute-start | bytes 98312 | tf_op jit(solution)/shard_map/ppermute | solution.py:247
  51.7 70.7 %collective-permute-start.16 = (bf16[2,66,1024]{2,1,0:T(8,128)(2,1)S(1)}, bf16[2,66,1024]{2,1,0:T(8,128)(2,1)S(1)}, u32[]{:S(2)}, u32[]{:S(2)}) collective-permute-start(bf16[2,66,1024]{2,1,0:T(8,128)(2,1)S(1)} %pad_maximum_fusion.3), channel_id=1, source_target_pairs={{0,8},{2,10},{4,12},{6,14},{8,0},{10,2},{12,4},{14,6},{16,24},{18,... | collective-permute-start | bytes 811016 | tf_op jit(solution)/shard_map/ppermute | solution.py:247
  69.9 1.4 collective-permute-start.10
  72.0 3.7 %collective-permute-start.11 = (f32[16,32]{1,0:T(8,128)S(1)}, f32[16,32]{1,0:T(8,128)S(1)}, u32[]{:S(2)}, u32[]{:S(2)}) collective-permute-start(f32[16,32]{1,0:T(8,128)S(1)} %add.233), channel_id=1, source_target_pairs={{0,2},{2,0},{4,6},{6,4},{8,10},{10,8},{12,14},{14,12},{16,18},{18,... | collective-permute-start | bytes 6152 | tf_op jit(solution)/shard_map/ppermute | solution.py:247
  75.7 3.7 %collective-permute-start.12 = (f32[16,32]{1,0:T(8,128)S(1)}, f32[16,32]{1,0:T(8,128)S(1)}, u32[]{:S(2)}, u32[]{:S(2)}) collective-permute-start(f32[16,32]{1,0:T(8,128)S(1)} %add.234), channel_id=1, source_target_pairs={{0,4},{2,6},{4,0},{6,2},{8,12},{10,14},{12,8},{14,10},{16,20},{18,... | collective-permute-start | bytes 6152 | tf_op jit(solution)/shard_map/ppermute | solution.py:247
  79.3 61.6 %copy-start.9 = (f32[16,32]{1,0:T(8,128)}, f32[16,32]{1,0:T(8,128)S(1)}, u32[]{:S(2)}) copy-start(f32[16,32]{1,0:T(8,128)S(1)} %add.235.own_ref) | copy-start | bytes 6148
  122.9 24.8 %collective-permute-start.17 = (bf16[4,66,1024]{2,0,1:T(4,128)(2,1)S(1)}, bf16[4,66,1024]{2,0,1:T(4,128)(2,1)S(1)}, u32[]{:S(2)}, u32[]{:S(2)}) collective-permute-start(bf16[4,66,1024]{2,0,1:T(4,128)(2,1)S(1)} %copy.18), channel_id=1, source_target_pairs={{0,4},{2,6},{4,0},{6,2},{8,12},{10,14},{12,8},{14,10},{16,20},{18,... | collective-permute-start | bytes 1622024 | tf_op jit(solution)/shard_map/ppermute | solution.py:247
  123.6 4.1 %collective-permute-start.13 = (f32[16,32]{1,0:T(8,128)S(1)}, f32[16,32]{1,0:T(8,128)S(1)}, u32[]{:S(2)}, u32[]{:S(2)}) collective-permute-start(f32[16,32]{1,0:T(8,128)S(1)} %add.235.own_ref), channel_id=1, source_target_pairs={{0,8},{2,10},{4,12},{6,14},{8,0},{10,2},{12,4},{14,6},{16,24},{18,... | collective-permute-start | bytes 6152 | tf_op jit(solution)/shard_map/ppermute | solution.py:247
  123.6 14.5 %collective-permute-start.14 = (f32[16,32]{1,0:T(8,128)S(1)}, f32[16,32]{1,0:T(8,128)S(1)}, u32[]{:S(2)}, u32[]{:S(2)}) collective-permute-start(f32[16,32]{1,0:T(8,128)S(1)} %add.235.own_ref), channel_id=1, source_target_pairs={{0,16},{2,18},{4,20},{6,22},{8,24},{10,26},{12,28},{14,30},{16,0},... | collective-permute-start | bytes 6152 | tf_op jit(solution)/shard_map/ppermute | solution.py:247
  127.7 13.2 %collective-permute-start.15 = (f32[16,32]{1,0:T(8,128)S(1)}, f32[16,32]{1,0:T(8,128)S(1)}, u32[]{:S(2)}, u32[]{:S(2)}) collective-permute-start(f32[16,32]{1,0:T(8,128)S(1)} %add.235.own_ref), channel_id=1, source_target_pairs={{0,24},{2,26},{4,28},{6,30},{8,16},{10,18},{12,20},{14,22},{16,8},... | collective-permute-start | bytes 6152 | tf_op jit(solution)/shard_map/ppermute | solution.py:247
  127.7 13.2 %copy-start.12 = (f32[16,32]{1,0:T(8,128)}, f32[16,32]{1,0:T(8,128)S(1)}, u32[]{:S(2)}) copy-start(f32[16,32]{1,0:T(8,128)S(1)} %collective-permute-done.13.far1_ref) | copy-start | bytes 6148
  147.7 109.3 %all-to-all-start.2 = ((bf16[16,128,1024]{2,1,0:T(8,128)(2,1)}), bf16[16,128,1024]{2,1,0:T(8,128)(2,1)}, u32[]{:S(2)}, u32[]{:S(2)}) async-start(bf16[16,128,1024]{2,1,0:T(8,128)(2,1)} %get-tuple-element.35), calls=%async_computation.2 | async-start | bytes 8388608 | tf_op jit(solution)/shard_map/all_to_all | solution.py:242
  157.7 15.5 %collective-permute-start.18 = (bf16[4,32,1024]{2,1,0:T(8,128)(2,1)S(1)}, bf16[4,32,1024]{2,1,0:T(8,128)(2,1)S(1)}, u32[]{:S(2)}, u32[]{:S(2)}) collective-permute-start(bf16[4,32,1024]{2,1,0:T(8,128)(2,1)S(1)} %get-tuple-element.68), channel_id=1, source_target_pairs={{0,2},{2,0},{4,6},{6,4},{8,10},{10,8},{12,14},{14,12},{16,18},{18,... | collective-permute-start | bytes 786440 | tf_op jit(solution)/shard_map/ppermute | solution.py:247
  159.2 27.1 %collective-permute-start.19 = (bf16[4,32,1024]{2,1,0:T(8,128)(2,1)S(1)}, bf16[4,32,1024]{2,1,0:T(8,128)(2,1)S(1)}, u32[]{:S(2)}, u32[]{:S(2)}) collective-permute-start(bf16[4,32,1024]{2,1,0:T(8,128)(2,1)S(1)} %get-tuple-element.67), channel_id=1, source_target_pairs={{0,4},{2,6},{4,0},{6,2},{8,12},{10,14},{12,8},{14,10},{16,20},{18,... | collective-permute-start | bytes 786440 | tf_op jit(solution)/shard_map/ppermute | solution.py:247
  159.8 26.5 %collective-permute-start.20 = (bf16[4,32,1024]{2,1,0:T(8,128)(2,1)S(1)}, bf16[4,32,1024]{2,1,0:T(8,128)(2,1)S(1)}, u32[]{:S(2)}, u32[]{:S(2)}) collective-permute-start(bf16[4,32,1024]{2,1,0:T(8,128)(2,1)S(1)} %get-tuple-element.66), channel_id=1, source_target_pairs={{0,6},{2,4},{4,2},{6,0},{8,14},{10,12},{12,10},{14,8},{16,22},{18,... | collective-permute-start | bytes 786440 | tf_op jit(solution)/shard_map/ppermute | solution.py:247
  187.7 39.5 %collective-permute-start.24 = (bf16[8,66,1024]{2,0,1:T(8,128)(2,1)S(1)}, bf16[8,66,1024]{2,0,1:T(8,128)(2,1)S(1)}, u32[]{:S(2)}, u32[]{:S(2)}) collective-permute-start(bf16[8,66,1024]{2,0,1:T(8,128)(2,1)S(1)} %pad_maximum_fusion), channel_id=1, source_target_pairs={{0,2},{2,0},{4,6},{6,4},{8,10},{10,8},{12,14},{14,12},{16,18},{18,... | collective-permute-start | bytes 3244040 | tf_op jit(solution)/shard_map/ppermute | solution.py:247
  190.3 72.2 %collective-permute-start.23 = (bf16[4,32,1024]{2,1,0:T(8,128)(2,1)S(1)}, bf16[4,32,1024]{2,1,0:T(8,128)(2,1)S(1)}, u32[]{:S(2)}, u32[]{:S(2)}) collective-permute-start(bf16[4,32,1024]{2,1,0:T(8,128)(2,1)S(1)} %pad_maximum_fusion.7), channel_id=1, source_target_pairs={{0,24},{2,26},{4,28},{6,30},{8,16},{10,18},{12,20},{14,22},{16,8},... | collective-permute-start | bytes 786440 | tf_op jit(solution)/shard_map/ppermute | solution.py:247
  197.5 66.9 %collective-permute-start.22 = (bf16[4,32,1024]{2,1,0:T(8,128)(2,1)S(1)}, bf16[4,32,1024]{2,1,0:T(8,128)(2,1)S(1)}, u32[]{:S(2)}, u32[]{:S(2)}) collective-permute-start(bf16[4,32,1024]{2,1,0:T(8,128)(2,1)S(1)} %pad_maximum_fusion.6), channel_id=1, source_target_pairs={{0,16},{2,18},{4,20},{6,22},{8,24},{10,26},{12,28},{14,30},{16,0},... | collective-permute-start | bytes 786440 | tf_op jit(solution)/shard_map/ppermute | solution.py:247
  203.1 61.2 %collective-permute-start.21 = (bf16[4,32,1024]{2,1,0:T(8,128)(2,1)S(1)}, bf16[4,32,1024]{2,1,0:T(8,128)(2,1)S(1)}, u32[]{:S(2)}, u32[]{:S(2)}) collective-permute-start(bf16[4,32,1024]{2,1,0:T(8,128)(2,1)S(1)} %pad_maximum_fusion.5), channel_id=1, source_target_pairs={{0,8},{2,10},{4,12},{6,14},{8,0},{10,2},{12,4},{14,6},{16,24},{18,... | collective-permute-start | bytes 786440 | tf_op jit(solution)/shard_map/ppermute | solution.py:247
  (12 other events, 47.9 us)

commit v5 on v4

--- a/solution.py
+++ b/solution.py
@@ -34,6 +34,24 @@
         center = (full - mean).astype(jnp.bfloat16).reshape(members * ROWS, TILE)
         mixed = jnp.dot(spread_ref[...], center, preferred_element_type=jnp.float32)
         y_ref[piece] = mixed.astype(jnp.bfloat16).reshape(members, ROWS, TILE)
+
+
+def center_kernel(x_ref, y_ref):
+    members, rows, width = x_ref.shape
+    for at in range(0, rows, ROWS):
+        for left in range(0, width, TILE):
+            piece = (slice(None), pl.ds(at, ROWS), pl.ds(left, TILE))
+            full = x_ref[piece].astype(jnp.float32)
+            mean = jnp.sum(full, axis=0, keepdims=True) * (1.0 / members)
+            y_ref[piece] = (full - mean).astype(jnp.bfloat16)
+
+
+def apply_rows(spread_ref, x_ref, y_ref, at):
+    members, _, width = x_ref.shape
+    rows = (slice(None), pl.ds(at, ROWS), slice(None))
+    center = x_ref[rows].reshape(members * ROWS, width)
+    mixed = jnp.dot(spread_ref[...], center, preferred_element_type=jnp.float32)
+    y_ref[rows] = mixed.astype(jnp.bfloat16).reshape(members, ROWS, width)
 
 
 def mix_kernel(spread_ref, x_ref, y_ref):
@@ -112,7 +130,7 @@
     stores = []
     for i in range(x_ref.shape[1] // ROWS):
         rows = (slice(None), pl.ds(i * ROWS, ROWS), slice(None))
-        mix_rows(spread_ref, x_buf, y_buf, i * ROWS)
+        apply_rows(spread_ref, x_buf, y_buf, i * ROWS)
         stores.append(pltpu.make_async_copy(y_buf.at[rows], y_ref.at[rows], y_sems.at[i]))
         stores[-1].start()
     for store in stores:
@@ -162,6 +180,35 @@
         total = total + jnp.sum(center * column[at : at + count, None, None], axis=0)
         at += count
     return total.astype(jnp.bfloat16)
+
+
+def place_kernel(at_ref, *refs):
+    parts, out_ref, sems = refs[:-2], refs[-2], refs[-1]
+    size = parts[0].shape[0]
+    copies = [
+        pltpu.make_async_copy(
+            part, out_ref.at[pl.ds((at_ref[0] ^ flip) * size, size)], sems.at[flip]
+        )
+        for flip, part in enumerate(parts)
+    ]
+    for copy in copies:
+        copy.start()
+    for copy in copies:
+        copy.wait()
+
+
+def place_parts(at, parts):
+    count, shape = len(parts), parts[0].shape
+    return pl.pallas_call(
+        place_kernel,
+        in_specs=[pl.BlockSpec(memory_space=pltpu.SMEM)]
+        + [pl.BlockSpec(memory_space=pltpu.VMEM)] * count,
+        out_specs=pl.BlockSpec(memory_space=pl.ANY),
+        out_shape=jax.ShapeDtypeStruct((count * shape[0],) + shape[1:], parts[0].dtype),
+        scratch_shapes=[pltpu.SemaphoreType.DMA((count,))],
+        compiler_params=pltpu.CompilerParams(vmem_limit_bytes=32 << 20),
+        cost_estimate=LIGHT,
+    )(at[None], *parts)
 
 
 def first_kernel(scale, x_ref, w_ref, b_ref, y_ref):
@@ -293,24 +340,27 @@
     both = jnp.concatenate(
         [pred.reshape(members, 1, count), resid.reshape(members, 1, count)], axis=1
     )
-    got_first = exchange(slabs_first)
+    got_second = exchange(slabs_second)
     var_part = lax.dynamic_index_in_dim(variance_half.reshape(members, count), me, 0)
     if fast:
-        both = both.reshape((planes, PLANE) + both.shape[1:])
-        parts = [pick(both, plane ^ i) for i in range(planes)]
-        parts = jnp.stack([parts[0]] + [across(parts[i], i) for i in range(1, planes)])
-        small = jnp.concatenate([third_w.T, b_first, b_second], axis=0)[None]
-        held = [small, swap(after(small, both), "member", 8)]
-        slabs_second, parts, held[1], got_first = lax.optimization_barrier(
-            (slabs_second, parts, held[1], got_first)
-        )
-        got_second = exchange(slabs_second)
-        held.append(swap(jnp.concatenate(held, axis=0), "member", 4))
-        both = jnp.stack([pick(parts, plane ^ i) for i in range(planes)])
-        parts = [pick(both, place ^ i, 1) for i in range(PLANE)]
-        parts = jnp.stack([parts[0]] + [swap(parts[i], "member", i) for i in range(1, PLANE)])
-        both = jnp.stack([pick(parts, place ^ i) for i in range(PLANE)], axis=1)
-        both = both.reshape((members,) + both.shape[2:])
+        def by_plane(parts):
+            parts = jnp.stack(parts)
+            return jnp.stack([pick(parts, plane ^ i) for i in range(planes)])
+
+        def within(x):
+            parts = [pick(x, place ^ i, 1) for i in range(PLANE)]
+            parts = jnp.stack([parts[0]] + [swap(parts[i], "member", i) for i in range(1, PLANE)])
+            return jnp.stack([pick(parts, place ^ i) for i in range(PLANE)])
+
+        slabs = within(slabs_first.reshape((planes, PLANE) + slabs_first.shape[1:]))
+        both, slabs = lax.optimization_barrier((both, slabs))
+        both = within(both.reshape((planes, PLANE) + both.shape[1:]))
+        parts = [pick(both, plane ^ i, 1) for i in range(planes)]
+        parts = [parts[0]] + [across(parts[i], i) for i in range(1, planes)]
+        parts, slabs = lax.optimization_barrier((parts, slabs))
+        both = jnp.concatenate(by_plane(parts), axis=0)
+        parts = [pick(slabs, plane ^ i, 1) for i in range(planes)]
+        parts = [parts[0]] + [across(parts[i], i) for i in range(1, planes)]
         sums = whole_call(
             moments_kernel,
             jax.ShapeDtypeStruct((members, 2 * members), jnp.float32),
@@ -320,25 +370,25 @@
         sums = sums + swap(sums, "pair", 1)
         sums = sums + swap(sums, "member", 1)
         sums = sums + swap(sums, "member", 2)
-        held[2] = after(held[2], sums)
+        small = jnp.concatenate([third_w.T, b_first, b_second], axis=0)[None]
+        center = blocked(center_kernel, got_second)
+        sums, small, parts[1], center = lax.optimization_barrier((sums, small, parts[1], center))
+        held = [small, swap(small, "member", 8)]
+        far = [across(sums, i) for i in range(1, planes)]
+        far, held[1], parts = lax.optimization_barrier((far, held[1], parts))
+        held.append(swap(jnp.concatenate(held, axis=0), "member", 4))
+        gain, spread, mixed_second = solve([sums] + far, center)
+        mixed_second, parts, held[2] = lax.optimization_barrier((mixed_second, parts, held[2]))
+        new_second = exchange(mixed_second)
+
         held.append(swap(jnp.concatenate(held, axis=0), "member", 2))
-        far = [across(sums, i) for i in range(1, planes)]
-        gain, spread, mixed_second = solve([sums] + far, got_second)
-        mixed_second, got_first, held[3] = lax.optimization_barrier(
-            (mixed_second, got_first, held[3])
-        )
-        new_second = exchange(mixed_second)
-
+        got_first = by_plane(parts).reshape(slabs_first.shape)
         mixed_first = blocked(mix_kernel, got_first, spread)
         mixed_first = mixed_first.reshape((planes, PLANE) + mixed_first.shape[1:])
-        parts = [pick(mixed_first, place ^ i, 1) for i in range(PLANE)]
-        parts = jnp.stack([parts[0]] + [swap(parts[i], "member", i) for i in range(1, PLANE)])
-        held[3] = after(held[3], parts)
+        back, held[3] = lax.optimization_barrier((within(mixed_first), held[3]))
         held.append(swap(jnp.concatenate(held, axis=0), "member", 1))
-        homes = []
-        for flip in range(planes):
-            block = jnp.stack([pick(pick(parts, place ^ i), plane ^ flip) for i in range(PLANE)])
-            homes.append(across(block, flip) if flip else block)
+        homes = [pick(back, plane ^ i, 1) for i in range(planes)]
+        homes = [homes[0]] + [across(homes[i], i) for i in range(1, planes)]
 
         order = me[None]
         for bit in (8, 4, 2, 1):
@@ -352,11 +402,7 @@
         homes, new_second, new_third, new_bfirst, new_bsecond = lax.optimization_barrier(
             (homes, new_second, new_third, new_bfirst, new_bsecond)
         )
-        new_first = jnp.zeros(slabs_first.shape, jnp.bfloat16)
-        for flip, part in enumerate(homes):
-            new_first = lax.dynamic_update_slice_in_dim(
-                new_first, part, (plane ^ flip) * PLANE, 0
-            )
+        new_first = place_parts(plane, homes)
     else:
         both = exchange(both)
         allpred, allres = both[:, 0], both[:, 1]
@@ -368,8 +414,8 @@
         sums = lax.psum(sums, ("member", "pair"))
         gain = solve_gain(sums[:, :members], sums[:, members:])
         gain_tr = gain.astype(jnp.bfloat16).T
-        new_second = exchange(mix_plain(exchange(slabs_second), gain_tr))
-        new_first = exchange(mix_plain(got_first, gain_tr))
+        new_second = exchange(mix_plain(got_second, gain_tr))
+        new_first = exchange(mix_plain(exchange(slabs_first), gain_tr))
         small = jnp.concatenate([third_w.T, b_first, b_second], axis=0)
         full = lax.all_gather(small, "member", axis=0)
         new_small = mix_plain(full, lax.dynamic_index_in_dim(gain_tr, me, 0))[0]

time: 270 us -> 268 us (level); the launches traced: 266 us -> 267 us
  waiting for transfers between devices: 166 us -> 148 us
  starting transfers between devices: 58.2 us -> 69.9 us
  other arithmetic: 8.48 us -> 14.5 us
  Pallas kernels: 21.2 us -> 26.3 us
  local copies, waits for them, and re-layouts: 10.5 us -> 7.21 us
    ppermute x25 -> x31, starting transfers between devices: 37.3 us -> 56.2 us  [swap(): return lax.ppermute(x, axis, [(i, i ^ bit) for i in range(count)])]
    ppermute x25 -> x31, waiting for transfers between devices: 142 us -> 131 us  [swap(): return lax.ppermute(x, axis, [(i, i ^ bit) for i in range(count)])]
    all_to_all x3 -> x2, waiting for transfers between devices: 24.4 us -> 17.2 us  [exchange(): return lax.all_to_all(x, 'member', split_axis=0, concat_axis=0, tiled=True)]
    all_to_all x3 -> x2, starting transfers between devices: 20.9 us -> 13.8 us  [exchange(): return lax.all_to_all(x, 'member', split_axis=0, concat_axis=0, tiled=True)]
    unnamed x32 -> x28, local copies, waits for them, and re-layouts: 4.48 us -> 0.07 us
    pallas_call x2 -> x3, Pallas kernels: 6.63 us -> 10.9 us  [blocked(): pl.pallas_call(kernel, grid=(total // rows,), in_specs=[pl.BlockSpec(w.sh...]
  transfers between devices with their start and end apart: 28 -> 33, of which waited for: 19 -> 19; matrix products, arithmetic and copies ran while one was open for 5% -> 8% of each run, Pallas kernels for 8% -> 9%
where the time goes in v5:
time: 268 us; the launch traced here: 267 us
  waiting for transfers between devices  148 us (55%)
  starting transfers between devices  69.9 us (26%)
  Pallas kernels  26.3 us (10%)
  other arithmetic  14.5 us (5%)
  local copies, waits for them, and re-layouts  7.21 us (3%)
    ppermute x31, waiting for transfers between devices, swap(): return lax.ppermute(x, axis, [(i, i ^ bit) for i in range(count)])  131 us
    ppermute x31, starting transfers between devices, swap(): return lax.ppermute(x, axis, [(i, i ^ bit) for i in range(count)])  56.2 us
    all_to_all x2, waiting for transfers between devices, exchange(): return lax.all_to_all(x, 'member', split_axis=0, concat_axis=0, tiled=True)  17.2 us
    all_to_all x2, starting transfers between devices, exchange(): return lax.all_to_all(x, 'member', split_axis=0, concat_axis=0, tiled=True)  13.8 us
    pallas_call x3, Pallas kernels, blocked(): pl.pallas_call(kernel, grid=(total // rows,), in_specs=[pl.BlockSpec(w.sh...  10.9 us
    pallas_call x1, Pallas kernels, solve(): pl.pallas_call(solve_kernel, in_specs=[vmem] * len(sums) + [anywhere], ou...  5.96 us
  transfers between devices with their start and end apart: 33, of which 19 were waited for; matrix products, arithmetic and copies ran while one was open for 8% of the time, Pallas kernels for 9%

profile of v5, /device:TPU:12, one launch (start us, length us, event | category | flops | bytes accessed | tf_op | source)
XLA Modules:
  0.0 267.3 jit_solution(9824934087919016405)
XLA Ops:
  0.6 7.3 %all-to-all-start = ((bf16[16,128,1024]{2,1,0:T(8,128)(2,1)}), bf16[16,128,1024]{2,1,0:T(8,128)(2,1)}, u32[]{:S(2)}, u32[]{:S(2)}) async-start(bf16[16,128,1024]{2,1,0:T(8,128)(2,1)} %bitcast.144), calls=%async_computation | async-start | bytes 8388608 | tf_op jit(solution)/shard_map/all_to_all | solution.py:289
  14.9 13.3 %collective-permute-done.3 = bf16[4,32,1024]{2,1,0:T(8,128)(2,1)} collective-permute-done((bf16[4,32,1024]{2,1,0:T(8,128)(2,1)}, bf16[4,32,1024]{2,1,0:T(8,128)(2,1)}, u32[]{:S(2)}, u32[]{:S(2)}) %collective-permute-start.3) | collective-permute-done | bytes 262176 | tf_op jit(solution)/shard_map/ppermute | solution.py:294
  28.2 14.5 %collective-permute-done.4 = bf16[4,32,1024]{2,1,0:T(8,128)(2,1)} collective-permute-done((bf16[4,32,1024]{2,1,0:T(8,128)(2,1)}, bf16[4,32,1024]{2,1,0:T(8,128)(2,1)}, u32[]{:S(2)}, u32[]{:S(2)}) %collective-permute-start.4) | collective-permute-done | bytes 262176 | tf_op jit(solution)/shard_map/ppermute | solution.py:294
  44.1 4.8 %shard_map.130 = f32[64,512]{1,0:T(8,128)S(1)} custom-call(s32[1]{0:T(128)} %bitcast.1.side_ref, bf16[512,512]{1,0:T(8,128)(2,1)S(1)} %shard_map.128.refs_0_, bf16[512,512]{1,0:T(8,128)(2,1)S(1)} %shard_map.129.refs_1_, bf16[512,512]{1,0:T(8,128)(2,1)S(1)} %collective-permute-done.refs_2_, bf16[512,512]{1,0:T(8,128)(2,1)S(1)} %collective-permute-done.1.refs_3_, ...), custom_call_target="tpu_custom_call" | custom-call | flops 1 | bytes 1 | tf_op jit(solution)/shard_map/pallas_call | solution.py:266
  52.2 5.9 %collective-permute-start.7 = (f32[4,2,1024]{2,1,0:T(2,128)S(1)}, f32[4,2,1024]{2,1,0:T(2,128)S(1)}, u32[]{:S(2)}, u32[]{:S(2)}) collective-permute-start(f32[4,2,1024]{2,1,0:T(2,128)S(1)} %bitcast.170), channel_id=1, source_target_pairs={{0,4},{2,6},{4,0},{6,2},{8,12},{10,14},{12,8},{14,10},{16,20},{18,... | collective-permute-start | bytes 98312 | tf_op jit(solution)/shard_map/ppermute | solution.py:294
  58.4 2.0 collective-permute-done.7
  60.4 11.2 %collective-permute-done.8 = f32[4,2,1024]{2,1,0:T(2,128)S(1)} collective-permute-done((f32[4,2,1024]{2,1,0:T(2,128)S(1)}, f32[4,2,1024]{2,1,0:T(2,128)S(1)}, u32[]{:S(2)}, u32[]{:S(2)}) %collective-permute-start.8) | collective-permute-done | bytes 32800 | tf_op jit(solution)/shard_map/ppermute | solution.py:294
  71.8 12.2 %collective-permute-start.11 = (f32[4,2,1024]{2,1,0:T(2,128)S(1)}, f32[4,2,1024]{2,1,0:T(2,128)S(1)}, u32[]{:S(2)}, u32[]{:S(2)}) collective-permute-start(f32[4,2,1024]{2,1,0:T(2,128)S(1)} %get-tuple-element.117), channel_id=1, source_target_pairs={{0,24},{2,26},{4,28},{6,30},{8,16},{10,18},{12,20},{14,22},{16,8},... | collective-permute-start | bytes 98312 | tf_op jit(solution)/shard_map/ppermute | solution.py:294
  86.0 17.6 %collective-permute-done.10 = f32[4,2,1024]{2,1,0:T(2,128)S(1)} collective-permute-done((f32[4,2,1024]{2,1,0:T(2,128)S(1)}, f32[4,2,1024]{2,1,0:T(2,128)S(1)}, u32[]{:S(2)}, u32[]{:S(2)}) %collective-permute-start.10) | collective-permute-done | bytes 32800 | tf_op jit(solution)/shard_map/ppermute | solution.py:294
  103.6 2.5 collective-permute-done.11
  110.5 1.8 shard_map.131
  115.2 2.9 %collective-permute-done.13 = f32[16,32]{1,0:T(8,128)S(1)} collective-permute-done((f32[16,32]{1,0:T(8,128)S(1)}, f32[16,32]{1,0:T(8,128)S(1)}, u32[]{:S(2)}, u32[]{:S(2)}) %collective-permute-start.13) | collective-permute-done | bytes 2080 | tf_op jit(solution)/shard_map/ppermute | solution.py:294
  119.1 2.6 collective-permute-done.14
  121.7 4.3 %shard_map.132.x_ref = bf16[16,128,1024]{2,1,0:T(8,128)(2,1)} custom-call(bf16[16,128,1024]{2,1,0:T(8,128)(2,1)} %all-to-all-done.x_ref), custom_call_target="tpu_custom_call" | custom-call | flops 1 | bytes 1 | tf_op jit(solution)/shard_map/pallas_call | solution.py:70
  126.0 2.5 collective-permute-start.19
  128.4 2.5 collective-permute-start.17
  131.9 4.7 %collective-permute-done.21 = bf16[4,32,1024]{2,1,0:T(8,128)(2,1)S(1)} collective-permute-done((bf16[4,32,1024]{2,1,0:T(8,128)(2,1)S(1)}, bf16[4,32,1024]{2,1,0:T(8,128)(2,1)S(1)}, u32[]{:S(2)}, u32[]{:S(2)}) %collective-permute-start.21) | collective-permute-done | bytes 262176 | tf_op jit(solution)/shard_map/ppermute | solution.py:294
  139.9 6.0 %shard_map.133 = (bf16[16,16]{1,0:T(8,128)(2,1)}, bf16[256,256]{1,0:T(8,128)(2,1)}, bf16[16,128,1024]{2,1,0:T(8,128)(2,1)}) custom-call(f32[16,32]{1,0:T(8,128)} %copy-done.7, f32[16,32]{1,0:T(8,128)} %copy-done.10, f32[16,32]{1,0:T(8,128)} %copy-done.11, f32[16,32]{1,0:T(8,128)} %copy-done.12, bf16[16,128,1024]{2,1,0:T(8,128)(2,1)} %shard_map.132.x_ref), custom_call_target="tpu_custom_call" | custom-call | flops 1 | bytes 1 | tf_op jit(solution)/shard_map/pallas_call | solution.py:144
  145.9 6.4 %all-to-all-start.1 = ((bf16[16,128,1024]{2,1,0:T(8,128)(2,1)}), bf16[16,128,1024]{2,1,0:T(8,128)(2,1)}, u32[]{:S(2)}, u32[]{:S(2)}) async-start(bf16[16,128,1024]{2,1,0:T(8,128)(2,1)} %get-tuple-element.70), calls=%async_computation.1 | async-start | bytes 8388608 | tf_op jit(solution)/shard_map/all_to_all | solution.py:289
  153.7 2.9 %shard_map.134 = bf16[16,32,1024]{2,1,0:T(8,128)(2,1)} custom-call(bf16[256,256]{1,0:T(8,128)(2,1)} %get-tuple-element.57.spread_ref, bf16[16,32,1024]{2,1,0:T(8,128)(2,1)} %bitcast.156), custom_call_target="tpu_custom_call" | custom-call | flops 1 | bytes 1 | tf_op jit(solution)/shard_map/pallas_call | solution.py:70
  163.2 8.5 %collective-permute-done.23 = bf16[4,32,1024]{2,1,0:T(8,128)(2,1)S(1)} collective-permute-done((bf16[4,32,1024]{2,1,0:T(8,128)(2,1)S(1)}, bf16[4,32,1024]{2,1,0:T(8,128)(2,1)S(1)}, u32[]{:S(2)}, u32[]{:S(2)}) %collective-permute-start.23) | collective-permute-done | bytes 262176 | tf_op jit(solution)/shard_map/ppermute | solution.py:294
  171.7 14.2 %collective-permute-done.24 = bf16[4,32,1024]{2,1,0:T(8,128)(2,1)S(1)} collective-permute-done((bf16[4,32,1024]{2,1,0:T(8,128)(2,1)S(1)}, bf16[4,32,1024]{2,1,0:T(8,128)(2,1)S(1)}, u32[]{:S(2)}, u32[]{:S(2)}) %collective-permute-start.24) | collective-permute-done | bytes 262176 | tf_op jit(solution)/shard_map/ppermute | solution.py:294
  186.2 16.7 %collective-permute-done.26 = bf16[4,66,1024]{2,0,1:T(4,128)(2,1)S(1)} collective-permute-done((bf16[4,66,1024]{2,0,1:T(4,128)(2,1)S(1)}, bf16[4,66,1024]{2,0,1:T(4,128)(2,1)S(1)}, u32[]{:S(2)}, u32[]{:S(2)}) %collective-permute-start.26) | collective-permute-done | bytes 540704 | tf_op jit(solution)/shard_map/ppermute | solution.py:294
  203.0 2.2 pad_maximum_fusion
  205.2 3.0 %collective-permute-start.30 = (bf16[8,66,1024]{2,0,1:T(8,128)(2,1)}, bf16[8,66,1024]{2,0,1:T(8,128)(2,1)}, u32[]{:S(2)}, u32[]{:S(2)}) collective-permute-start(bf16[8,66,1024]{2,0,1:T(8,128)(2,1)} %pad_maximum_fusion), channel_id=1, source_target_pairs={{0,2},{2,0},{4,6},{6,4},{8,10},{10,8},{12,14},{14,12},{16,18},{18,... | collective-permute-start | bytes 3244040 | tf_op jit(solution)/shard_map/ppermute | solution.py:294
  209.8 9.3 %collective-permute-start.27 = (bf16[4,32,1024]{2,1,0:T(8,128)(2,1)S(1)}, bf16[4,32,1024]{2,1,0:T(8,128)(2,1)S(1)}, u32[]{:S(2)}, u32[]{:S(2)}) collective-permute-start(bf16[4,32,1024]{2,1,0:T(8,128)(2,1)S(1)} %get-tuple-element.85), channel_id=1, source_target_pairs={{0,8},{2,10},{4,12},{6,14},{8,0},{10,2},{12,4},{14,6},{16,24},{18,... | collective-permute-start | bytes 786440 | tf_op jit(solution)/shard_map/ppermute | solution.py:294
  221.4 8.9 %collective-permute-done.30 = bf16[8,66,1024]{2,0,1:T(8,128)(2,1)} collective-permute-done((bf16[8,66,1024]{2,0,1:T(8,128)(2,1)}, bf16[8,66,1024]{2,0,1:T(8,128)(2,1)}, u32[]{:S(2)}, u32[]{:S(2)}) %collective-permute-start.30) | collective-permute-done | bytes 1081376 | tf_op jit(solution)/shard_map/ppermute | solution.py:294
  230.3 2.0 convert_reduce_fusion
  233.4 2.1 multiply_reduce_fusion
  238.2 17.2 %all-to-all-done.1.x_ref = bf16[16,128,1024]{2,1,0:T(8,128)(2,1)} async-done(((bf16[16,128,1024]{2,1,0:T(8,128)(2,1)}), bf16[16,128,1024]{2,1,0:T(8,128)(2,1)}, u32[]{:S(2)}, u32[]{:S(2)}) %all-to-all-start.1) | async-done | bytes 4194336 | tf_op jit(solution)/shard_map/all_to_all | solution.py:289
  255.4 3.7 %shard_map.135 = bf16[16,128,1024]{2,1,0:T(8,128)(2,1)} custom-call(bf16[16,128,1024]{2,1,0:T(8,128)(2,1)} %all-to-all-done.1.x_ref), custom_call_target="tpu_custom_call" | custom-call | flops 1 | bytes 1 | tf_op jit(solution)/shard_map/pallas_call | solution.py:70
  260.8 5.4 %collective-permute-done.29.refs_3_ = bf16[4,32,1024]{2,1,0:T(8,128)(2,1)S(1)} collective-permute-done((bf16[4,32,1024]{2,1,0:T(8,128)(2,1)S(1)}, bf16[4,32,1024]{2,1,0:T(8,128)(2,1)S(1)}, u32[]{:S(2)}, u32[]{:S(2)}) %collective-permute-start.29) | collective-permute-done | bytes 262176 | tf_op jit(solution)/shard_map/ppermute | solution.py:294
  (136 shorter events, 45.0 us)
Async XLA Ops:
  0.6 121.1 %all-to-all-start = ((bf16[16,128,1024]{2,1,0:T(8,128)(2,1)}), bf16[16,128,1024]{2,1,0:T(8,128)(2,1)}, u32[]{:S(2)}, u32[]{:S(2)}) async-start(bf16[16,128,1024]{2,1,0:T(8,128)(2,1)} %bitcast.144), calls=%async_computation | async-start | bytes 8388608 | tf_op jit(solution)/shard_map/all_to_all | solution.py:289
  8.9 19.2 %collective-permute-start.3 = (bf16[4,32,1024]{2,1,0:T(8,128)(2,1)}, bf16[4,32,1024]{2,1,0:T(8,128)(2,1)}, u32[]{:S(2)}, u32[]{:S(2)}) collective-permute-start(bf16[4,32,1024]{2,1,0:T(8,128)(2,1)} %get-tuple-element.110), channel_id=1, source_target_pairs={{0,2},{2,0},{4,6},{6,4},{8,10},{10,8},{12,14},{14,12},{16,18},{18,... | collective-permute-start | bytes 786440 | tf_op jit(solution)/shard_map/ppermute | solution.py:294
  10.4 32.3 %collective-permute-start.4 = (bf16[4,32,1024]{2,1,0:T(8,128)(2,1)}, bf16[4,32,1024]{2,1,0:T(8,128)(2,1)}, u32[]{:S(2)}, u32[]{:S(2)}) collective-permute-start(bf16[4,32,1024]{2,1,0:T(8,128)(2,1)} %get-tuple-element.109), channel_id=1, source_target_pairs={{0,4},{2,6},{4,0},{6,2},{8,12},{10,14},{12,8},{14,10},{16,20},{18,... | collective-permute-start | bytes 786440 | tf_op jit(solution)/shard_map/ppermute | solution.py:294
  11.0 31.7 %collective-permute-start.5 = (bf16[4,32,1024]{2,1,0:T(8,128)(2,1)}, bf16[4,32,1024]{2,1,0:T(8,128)(2,1)}, u32[]{:S(2)}, u32[]{:S(2)}) collective-permute-start(bf16[4,32,1024]{2,1,0:T(8,128)(2,1)} %get-tuple-element.108), channel_id=1, source_target_pairs={{0,6},{2,4},{4,2},{6,0},{8,14},{10,12},{12,10},{14,8},{16,22},{18,... | collective-permute-start | bytes 786440 | tf_op jit(solution)/shard_map/ppermute | solution.py:294
  13.3 30.7 %collective-permute-start = (bf16[512,512]{1,0:T(8,128)(2,1)S(1)}, bf16[512,512]{1,0:T(8,128)(2,1)S(1)}, u32[]{:S(2)}, u32[]{:S(2)}) collective-permute-start(bf16[512,512]{1,0:T(8,128)(2,1)S(1)} %shard_map.128.refs_0_), channel_id=1, source_target_pairs={{0,1},{1,0},{2,3},{3,2},{4,5},{5,4},{6,7},{7,6},{8,9},{9,8},{10,11... | collective-permute-start | bytes 1572872 | tf_op jit(solution)/shard_map/ppermute | solution.py:294
  14.4 29.7 %collective-permute-start.1 = (bf16[512,512]{1,0:T(8,128)(2,1)S(1)}, bf16[512,512]{1,0:T(8,128)(2,1)S(1)}, u32[]{:S(2)}, u32[]{:S(2)}) collective-permute-start(bf16[512,512]{1,0:T(8,128)(2,1)S(1)} %shard_map.129.refs_1_), channel_id=1, source_target_pairs={{0,1},{1,0},{2,3},{3,2},{4,5},{5,4},{6,7},{7,6},{8,9},{9,8},{10,11... | collective-permute-start | bytes 1572872 | tf_op jit(solution)/shard_map/ppermute | solution.py:294
  50.7 7.7 %collective-permute-start.6 = (f32[4,2,1024]{2,1,0:T(2,128)S(1)}, f32[4,2,1024]{2,1,0:T(2,128)S(1)}, u32[]{:S(2)}, u32[]{:S(2)}) collective-permute-start(f32[4,2,1024]{2,1,0:T(2,128)S(1)} %bitcast.169), channel_id=1, source_target_pairs={{0,2},{2,0},{4,6},{6,4},{8,10},{10,8},{12,14},{14,12},{16,18},{18,... | collective-permute-start | bytes 98312 | tf_op jit(solution)/shard_map/ppermute | solution.py:294
  52.2 8.1 %collective-permute-start.7 = (f32[4,2,1024]{2,1,0:T(2,128)S(1)}, f32[4,2,1024]{2,1,0:T(2,128)S(1)}, u32[]{:S(2)}, u32[]{:S(2)}) collective-permute-start(f32[4,2,1024]{2,1,0:T(2,128)S(1)} %bitcast.170), channel_id=1, source_target_pairs={{0,4},{2,6},{4,0},{6,2},{8,12},{10,14},{12,8},{14,10},{16,20},{18,... | collective-permute-start | bytes 98312 | tf_op jit(solution)/shard_map/ppermute | solution.py:294
  58.2 13.4 %collective-permute-start.8 = (f32[4,2,1024]{2,1,0:T(2,128)S(1)}, f32[4,2,1024]{2,1,0:T(2,128)S(1)}, u32[]{:S(2)}, u32[]{:S(2)}) collective-permute-start(f32[4,2,1024]{2,1,0:T(2,128)S(1)} %bitcast.171), channel_id=1, source_target_pairs={{0,6},{2,4},{4,2},{6,0},{8,14},{10,12},{12,10},{14,8},{16,22},{18,... | collective-permute-start | bytes 98312 | tf_op jit(solution)/shard_map/ppermute | solution.py:294
  71.8 31.8 %collective-permute-start.10 = (f32[4,2,1024]{2,1,0:T(2,128)S(1)}, f32[4,2,1024]{2,1,0:T(2,128)S(1)}, u32[]{:S(2)}, u32[]{:S(2)}) collective-permute-start(f32[4,2,1024]{2,1,0:T(2,128)S(1)} %get-tuple-element.118), channel_id=1, source_target_pairs={{0,16},{2,18},{4,20},{6,22},{8,24},{10,26},{12,28},{14,30},{16,0},... | collective-permute-start | bytes 98312 | tf_op jit(solution)/shard_map/ppermute | solution.py:294
  71.8 34.2 %collective-permute-start.11 = (f32[4,2,1024]{2,1,0:T(2,128)S(1)}, f32[4,2,1024]{2,1,0:T(2,128)S(1)}, u32[]{:S(2)}, u32[]{:S(2)}) collective-permute-start(f32[4,2,1024]{2,1,0:T(2,128)S(1)} %get-tuple-element.117), channel_id=1, source_target_pairs={{0,24},{2,26},{4,28},{6,30},{8,16},{10,18},{12,20},{14,22},{16,8},... | collective-permute-start | bytes 98312 | tf_op jit(solution)/shard_map/ppermute | solution.py:294
  84.0 22.0 %collective-permute-start.9 = (f32[4,2,1024]{2,1,0:T(2,128)S(1)}, f32[4,2,1024]{2,1,0:T(2,128)S(1)}, u32[]{:S(2)}, u32[]{:S(2)}) collective-permute-start(f32[4,2,1024]{2,1,0:T(2,128)S(1)} %get-tuple-element.119), channel_id=1, source_target_pairs={{0,8},{2,10},{4,12},{6,14},{8,0},{10,2},{12,4},{14,6},{16,24},{18,... | collective-permute-start | bytes 98312 | tf_op jit(solution)/shard_map/ppermute | solution.py:294
  106.1 19.9 %collective-permute-start.15 = (bf16[4,32,1024]{2,1,0:T(8,128)(2,1)S(1)}, bf16[4,32,1024]{2,1,0:T(8,128)(2,1)S(1)}, u32[]{:S(2)}, u32[]{:S(2)}) collective-permute-start(bf16[4,32,1024]{2,1,0:T(8,128)(2,1)S(1)} %get-tuple-element.102), channel_id=1, source_target_pairs={{0,8},{2,10},{4,12},{6,14},{8,0},{10,2},{12,4},{14,6},{16,24},{18,... | collective-permute-start | bytes 786440 | tf_op jit(solution)/shard_map/ppermute | solution.py:294
  107.4 23.5 %collective-permute-start.20 = (bf16[4,32,1024]{2,1,0:T(8,128)(2,1)S(1)}, bf16[4,32,1024]{2,1,0:T(8,128)(2,1)S(1)}, u32[]{:S(2)}, u32[]{:S(2)}) collective-permute-start(bf16[4,32,1024]{2,1,0:T(8,128)(2,1)S(1)} %get-tuple-element.100), channel_id=1, source_target_pairs={{0,16},{2,18},{4,20},{6,22},{8,24},{10,26},{12,28},{14,30},{16,0},... | collective-permute-start | bytes 786440 | tf_op jit(solution)/shard_map/ppermute | solution.py:294
  108.2 28.5 %collective-permute-start.21 = (bf16[4,32,1024]{2,1,0:T(8,128)(2,1)S(1)}, bf16[4,32,1024]{2,1,0:T(8,128)(2,1)S(1)}, u32[]{:S(2)}, u32[]{:S(2)}) collective-permute-start(bf16[4,32,1024]{2,1,0:T(8,128)(2,1)S(1)} %get-tuple-element.99), channel_id=1, source_target_pairs={{0,24},{2,26},{4,28},{6,30},{8,16},{10,18},{12,20},{14,22},{16,8},... | collective-permute-start | bytes 786440 | tf_op jit(solution)/shard_map/ppermute | solution.py:294
  112.3 1.4 collective-permute-start.12
  114.4 3.7 %collective-permute-start.13 = (f32[16,32]{1,0:T(8,128)S(1)}, f32[16,32]{1,0:T(8,128)S(1)}, u32[]{:S(2)}, u32[]{:S(2)}) collective-permute-start(f32[16,32]{1,0:T(8,128)S(1)} %add.144), channel_id=1, source_target_pairs={{0,2},{2,0},{4,6},{6,4},{8,10},{10,8},{12,14},{14,12},{16,18},{18,... | collective-permute-start | bytes 6152 | tf_op jit(solution)/shard_map/ppermute | solution.py:294
  118.0 3.7 %collective-permute-start.14 = (f32[16,32]{1,0:T(8,128)S(1)}, f32[16,32]{1,0:T(8,128)S(1)}, u32[]{:S(2)}, u32[]{:S(2)}) collective-permute-start(f32[16,32]{1,0:T(8,128)S(1)} %add.145), channel_id=1, source_target_pairs={{0,4},{2,6},{4,0},{6,2},{8,12},{10,14},{12,8},{14,10},{16,20},{18,... | collective-permute-start | bytes 6152 | tf_op jit(solution)/shard_map/ppermute | solution.py:294
  126.0 12.4 %collective-permute-start.19 = (bf16[1,66,1024]{2,1,0:T(8,128)(2,1)S(1)}, bf16[1,66,1024]{2,1,0:T(8,128)(2,1)S(1)}, u32[]{:S(2)}, u32[]{:S(2)}) collective-permute-start(bf16[1,66,1024]{2,1,0:T(8,128)(2,1)S(1)} %maximum_bitcast_fusion), channel_id=1, source_target_pairs={{0,16},{2,18},{4,20},{6,22},{8,24},{10,26},{12,28},{14,30},{16,0},... | collective-permute-start | bytes 405512 | tf_op jit(solution)/shard_map/ppermute | solution.py:294
  128.4 8.2 %collective-permute-start.16 = (f32[16,32]{1,0:T(8,128)S(1)}, f32[16,32]{1,0:T(8,128)S(1)}, u32[]{:S(2)}, u32[]{:S(2)}) collective-permute-start(f32[16,32]{1,0:T(8,128)S(1)} %add.146.own_ref), channel_id=1, source_target_pairs={{0,8},{2,10},{4,12},{6,14},{8,0},{10,2},{12,4},{14,6},{16,24},{18,... | collective-permute-start | bytes 6152 | tf_op jit(solution)/shard_map/ppermute | solution.py:294
  128.4 8.2 %collective-permute-start.17 = (f32[16,32]{1,0:T(8,128)S(1)}, f32[16,32]{1,0:T(8,128)S(1)}, u32[]{:S(2)}, u32[]{:S(2)}) collective-permute-start(f32[16,32]{1,0:T(8,128)S(1)} %add.146.own_ref), channel_id=1, source_target_pairs={{0,16},{2,18},{4,20},{6,22},{8,24},{10,26},{12,28},{14,30},{16,0},... | collective-permute-start | bytes 6152 | tf_op jit(solution)/shard_map/ppermute | solution.py:294
  130.9 7.5 %collective-permute-start.18 = (f32[16,32]{1,0:T(8,128)S(1)}, f32[16,32]{1,0:T(8,128)S(1)}, u32[]{:S(2)}, u32[]{:S(2)}) collective-permute-start(f32[16,32]{1,0:T(8,128)S(1)} %add.146.own_ref), channel_id=1, source_target_pairs={{0,24},{2,26},{4,28},{6,30},{8,16},{10,18},{12,20},{14,22},{16,8},... | collective-permute-start | bytes 6152 | tf_op jit(solution)/shard_map/ppermute | solution.py:294
  138.4 7.4 %collective-permute-start.22 = (bf16[2,66,1024]{2,1,0:T(8,128)(2,1)S(1)}, bf16[2,66,1024]{2,1,0:T(8,128)(2,1)S(1)}, u32[]{:S(2)}, u32[]{:S(2)}) collective-permute-start(bf16[2,66,1024]{2,1,0:T(8,128)(2,1)S(1)} %pad_maximum_fusion.8), channel_id=1, source_target_pairs={{0,8},{2,10},{4,12},{6,14},{8,0},{10,2},{12,4},{14,6},{16,24},{18,... | collective-permute-start | bytes 811016 | tf_op jit(solution)/shard_map/ppermute | solution.py:294
  145.9 109.5 %all-to-all-start.1 = ((bf16[16,128,1024]{2,1,0:T(8,128)(2,1)}), bf16[16,128,1024]{2,1,0:T(8,128)(2,1)}, u32[]{:S(2)}, u32[]{:S(2)}) async-start(bf16[16,128,1024]{2,1,0:T(8,128)(2,1)} %get-tuple-element.70), calls=%async_computation.1 | async-start | bytes 8388608 | tf_op jit(solution)/shard_map/all_to_all | solution.py:289
  157.8 13.9 %collective-permute-start.23 = (bf16[4,32,1024]{2,1,0:T(8,128)(2,1)S(1)}, bf16[4,32,1024]{2,1,0:T(8,128)(2,1)S(1)}, u32[]{:S(2)}, u32[]{:S(2)}) collective-permute-start(bf16[4,32,1024]{2,1,0:T(8,128)(2,1)S(1)} %get-tuple-element.94), channel_id=1, source_target_pairs={{0,2},{2,0},{4,6},{6,4},{8,10},{10,8},{12,14},{14,12},{16,18},{18,... | collective-permute-start | bytes 786440 | tf_op jit(solution)/shard_map/ppermute | solution.py:294
  159.4 26.5 %collective-permute-start.24 = (bf16[4,32,1024]{2,1,0:T(8,128)(2,1)S(1)}, bf16[4,32,1024]{2,1,0:T(8,128)(2,1)S(1)}, u32[]{:S(2)}, u32[]{:S(2)}) collective-permute-start(bf16[4,32,1024]{2,1,0:T(8,128)(2,1)S(1)} %get-tuple-element.93), channel_id=1, source_target_pairs={{0,4},{2,6},{4,0},{6,2},{8,12},{10,14},{12,8},{14,10},{16,20},{18,... | collective-permute-start | bytes 786440 | tf_op jit(solution)/shard_map/ppermute | solution.py:294
  159.9 25.9 %collective-permute-start.25 = (bf16[4,32,1024]{2,1,0:T(8,128)(2,1)S(1)}, bf16[4,32,1024]{2,1,0:T(8,128)(2,1)S(1)}, u32[]{:S(2)}, u32[]{:S(2)}) collective-permute-start(bf16[4,32,1024]{2,1,0:T(8,128)(2,1)S(1)} %get-tuple-element.92), channel_id=1, source_target_pairs={{0,6},{2,4},{4,2},{6,0},{8,14},{10,12},{12,10},{14,8},{16,22},{18,... | collective-permute-start | bytes 786440 | tf_op jit(solution)/shard_map/ppermute | solution.py:294
  161.9 41.1 %collective-permute-start.26 = (bf16[4,66,1024]{2,0,1:T(4,128)(2,1)S(1)}, bf16[4,66,1024]{2,0,1:T(4,128)(2,1)S(1)}, u32[]{:S(2)}, u32[]{:S(2)}) collective-permute-start(bf16[4,66,1024]{2,0,1:T(4,128)(2,1)S(1)} %copy.26), channel_id=1, source_target_pairs={{0,4},{2,6},{4,0},{6,2},{8,12},{10,14},{12,8},{14,10},{16,20},{18,... | collective-permute-start | bytes 1622024 | tf_op jit(solution)/shard_map/ppermute | solution.py:294
  205.2 25.1 %collective-permute-start.30 = (bf16[8,66,1024]{2,0,1:T(8,128)(2,1)}, bf16[8,66,1024]{2,0,1:T(8,128)(2,1)}, u32[]{:S(2)}, u32[]{:S(2)}) collective-permute-start(bf16[8,66,1024]{2,0,1:T(8,128)(2,1)} %pad_maximum_fusion), channel_id=1, source_target_pairs={{0,2},{2,0},{4,6},{6,4},{8,10},{10,8},{12,14},{14,12},{16,18},{18,... | collective-permute-start | bytes 3244040 | tf_op jit(solution)/shard_map/ppermute | solution.py:294
  209.8 49.3 %collective-permute-start.27 = (bf16[4,32,1024]{2,1,0:T(8,128)(2,1)S(1)}, bf16[4,32,1024]{2,1,0:T(8,128)(2,1)S(1)}, u32[]{:S(2)}, u32[]{:S(2)}) collective-permute-start(bf16[4,32,1024]{2,1,0:T(8,128)(2,1)S(1)} %get-tuple-element.85), channel_id=1, source_target_pairs={{0,8},{2,10},{4,12},{6,14},{8,0},{10,2},{12,4},{14,6},{16,24},{18,... | collective-permute-start | bytes 786440 | tf_op jit(solution)/shard_map/ppermute | solution.py:294
  219.2 41.6 %collective-permute-start.28 = (bf16[4,32,1024]{2,1,0:T(8,128)(2,1)S(1)}, bf16[4,32,1024]{2,1,0:T(8,128)(2,1)S(1)}, u32[]{:S(2)}, u32[]{:S(2)}) collective-permute-start(bf16[4,32,1024]{2,1,0:T(8,128)(2,1)S(1)} %get-tuple-element.84), channel_id=1, source_target_pairs={{0,16},{2,18},{4,20},{6,22},{8,24},{10,26},{12,28},{14,30},{16,0},... | collective-permute-start | bytes 786440 | tf_op jit(solution)/shard_map/ppermute | solution.py:294
  220.0 46.1 %collective-permute-start.29 = (bf16[4,32,1024]{2,1,0:T(8,128)(2,1)S(1)}, bf16[4,32,1024]{2,1,0:T(8,128)(2,1)S(1)}, u32[]{:S(2)}, u32[]{:S(2)}) collective-permute-start(bf16[4,32,1024]{2,1,0:T(8,128)(2,1)S(1)} %get-tuple-element.83), channel_id=1, source_target_pairs={{0,24},{2,26},{4,28},{6,30},{8,16},{10,18},{12,20},{14,22},{16,8},... | collective-permute-start | bytes 786440 | tf_op jit(solution)/shard_map/ppermute | solution.py:294
  (15 other events, 150.9 us)

commit v6 on v5

--- a/solution.py
+++ b/solution.py
@@ -11,6 +11,7 @@
 ROWS = 1 << ROW_BITS
 PLANE = 4
 TILE = 256
+LOADS = 4
 VMEM = 56 << 20
 LIGHT = pl.CostEstimate(flops=1, bytes_accessed=1, transcendentals=0)
 
@@ -96,10 +97,17 @@
 
 
 def solve_kernel(
-    own_ref, far1_ref, far2_ref, far3_ref, x_ref, gain_ref, spread_ref, y_ref, x_buf, y_buf, x_sem, y_sems
+    own_ref, far1_ref, far2_ref, far3_ref, x_ref, gain_ref, spread_ref, y_ref, x_buf, y_buf, x_sems, y_sems
 ):
-    load = pltpu.make_async_copy(x_ref, x_buf, x_sem)
-    load.start()
+    size = x_ref.shape[0] // LOADS
+    loads = [
+        pltpu.make_async_copy(
+            x_ref.at[pl.ds(i * size, size)], x_buf.at[pl.ds(i * size, size)], x_sems.at[i]
+        )
+        for i in range(LOADS)
+    ]
+    for load in loads:
+        load.start()
     total = (own_ref[...] + far1_ref[...]) + (far2_ref[...] + far3_ref[...])
     count = total.shape[0]
     row = lax.broadcasted_iota(jnp.int32, total.shape, 0)
@@ -107,8 +115,7 @@
     total = total + jnp.where(row == col, float(count), 0.0)
     for k in range(count):
         pivot = total[k : k + 1, :] / total[k : k + 1, k : k + 1]
-        factor = jnp.where(row == k, total - 1.0, total)[:, k : k + 1]
-        total = total - factor * pivot
+        total = jnp.where(row == k, pivot, total - total[:, k : k + 1] * pivot)
     gain = total[:, count:].astype(jnp.bfloat16)
     gain_ref[...] = gain
     size = count * ROWS
@@ -126,7 +133,8 @@
     same = ((at_row ^ at_col) & (ROWS - 1)) == 0
     spread_ref[...] = jnp.where(same, wide, 0.0).astype(jnp.bfloat16)
 
-    load.wait()
+    for load in loads:
+        load.wait()
     stores = []
     for i in range(x_ref.shape[1] // ROWS):
         rows = (slice(None), pl.ds(i * ROWS, ROWS), slice(None))
@@ -153,7 +161,7 @@
         scratch_shapes=[
             pltpu.VMEM(x.shape, x.dtype),
             pltpu.VMEM(x.shape, x.dtype),
-            pltpu.SemaphoreType.DMA,
+            pltpu.SemaphoreType.DMA((LOADS,)),
             pltpu.SemaphoreType.DMA((x.shape[1] // ROWS,)),
         ],
         compiler_params=pltpu.CompilerParams(vmem_limit_bytes=VMEM),
@@ -357,10 +365,20 @@
         both = within(both.reshape((planes, PLANE) + both.shape[1:]))
         parts = [pick(both, plane ^ i, 1) for i in range(planes)]
         parts = [parts[0]] + [across(parts[i], i) for i in range(1, planes)]
-        parts, slabs = lax.optimization_barrier((parts, slabs))
+        small = jnp.concatenate([third_w.T, b_first, b_second], axis=0)
+        slabs = [pick(slabs, plane ^ i, 1) for i in range(planes)]
+        joined = jnp.concatenate([slabs[2].reshape(-1, width), small], axis=0)
+        parts, slabs, joined = lax.optimization_barrier((parts, slabs, joined))
         both = jnp.concatenate(by_plane(parts), axis=0)
-        parts = [pick(slabs, plane ^ i, 1) for i in range(planes)]
-        parts = [parts[0]] + [across(parts[i], i) for i in range(1, planes)]
+        joined = across(joined, 2)
+        size = joined.shape[0] - small.shape[0]
+        held = [small[None], joined[None, size:]]
+        parts = [
+            slabs[0],
+            across(slabs[1], 1),
+            joined[:size].reshape(slabs[2].shape),
+            across(slabs[3], 3),
+        ]
         sums = whole_call(
             moments_kernel,
             jax.ShapeDtypeStruct((members, 2 * members), jnp.float32),
@@ -370,10 +388,8 @@
         sums = sums + swap(sums, "pair", 1)
         sums = sums + swap(sums, "member", 1)
         sums = sums + swap(sums, "member", 2)
-        small = jnp.concatenate([third_w.T, b_first, b_second], axis=0)[None]
         center = blocked(center_kernel, got_second)
-        sums, small, parts[1], center = lax.optimization_barrier((sums, small, parts[1], center))
-        held = [small, swap(small, "member", 8)]
+        sums, parts[1], parts[3], center = lax.optimization_barrier((sums, parts[1], parts[3], center))
         far = [across(sums, i) for i in range(1, planes)]
         far, held[1], parts = lax.optimization_barrier((far, held[1], parts))
         held.append(swap(jnp.concatenate(held, axis=0), "member", 4))

time: 268 us -> 266 us (level)
  starting transfers between devices: 69.9 us -> 66.5 us
    ppermute x31 -> x30, starting transfers between devices: 56.2 us -> 53.1 us  [swap(): return lax.ppermute(x, axis, [(i, i ^ bit) for i in range(count)])]
    ppermute x31 -> x30, waiting for transfers between devices: 131 us -> 132 us  [swap(): return lax.ppermute(x, axis, [(i, i ^ bit) for i in range(count)])]
  transfers between devices with their start and end apart: 33 -> 32, of which waited for: 19 -> 21; matrix products, arithmetic and copies ran while one was open for 8% -> 8% of each run, Pallas kernels for 9% -> 10%
where the time goes in v6:
time: 266 us; the launch traced here: 265 us
  waiting for transfers between devices  149 us (56%)
  starting transfers between devices  66.5 us (25%)
  Pallas kernels  26.3 us (10%)
  other arithmetic  13.5 us (5%)
  local copies, waits for them, and re-layouts  8.14 us (3%)
    ppermute x30, waiting for transfers between devices, swap(): return lax.ppermute(x, axis, [(i, i ^ bit) for i in range(count)])  132 us
    ppermute x30, starting transfers between devices, swap(): return lax.ppermute(x, axis, [(i, i ^ bit) for i in range(count)])  53.1 us
    all_to_all x2, waiting for transfers between devices, exchange(): return lax.all_to_all(x, 'member', split_axis=0, concat_axis=0, tiled=True)  17.6 us
    all_to_all x2, starting transfers between devices, exchange(): return lax.all_to_all(x, 'member', split_axis=0, concat_axis=0, tiled=True)  13.5 us
    pallas_call x3, Pallas kernels, blocked(): pl.pallas_call(kernel, grid=(total // rows,), in_specs=[pl.BlockSpec(w.sh...  10.9 us
    pallas_call x1, Pallas kernels, solve(): pl.pallas_call(solve_kernel, in_specs=[vmem] * len(sums) + [anywhere], ou...  6.02 us
  transfers between devices with their start and end apart: 32, of which 21 were waited for; matrix products, arithmetic and copies ran while one was open for 8% of the time, Pallas kernels for 10%

profile of v6, /device:TPU:12, one launch (start us, length us, event | category | flops | bytes accessed | tf_op | source)
XLA Modules:
  0.0 265.3 jit_solution(15774063090965182637)
XLA Ops:
  0.6 7.3 %all-to-all-start = ((bf16[16,128,1024]{2,1,0:T(8,128)(2,1)}), bf16[16,128,1024]{2,1,0:T(8,128)(2,1)}, u32[]{:S(2)}, u32[]{:S(2)}) async-start(bf16[16,128,1024]{2,1,0:T(8,128)(2,1)} %bitcast.150), calls=%async_computation | async-start | bytes 8388608 | tf_op jit(solution)/shard_map/all_to_all | solution.py:297
  15.6 12.6 %collective-permute-done.3 = bf16[4,32,1024]{2,1,0:T(8,128)(2,1)} collective-permute-done((bf16[4,32,1024]{2,1,0:T(8,128)(2,1)}, bf16[4,32,1024]{2,1,0:T(8,128)(2,1)}, u32[]{:S(2)}, u32[]{:S(2)}) %collective-permute-start.3) | collective-permute-done | bytes 262176 | tf_op jit(solution)/shard_map/ppermute | solution.py:302
  28.2 14.5 %collective-permute-done.4 = bf16[4,32,1024]{2,1,0:T(8,128)(2,1)} collective-permute-done((bf16[4,32,1024]{2,1,0:T(8,128)(2,1)}, bf16[4,32,1024]{2,1,0:T(8,128)(2,1)}, u32[]{:S(2)}, u32[]{:S(2)}) %collective-permute-start.4) | collective-permute-done | bytes 262176 | tf_op jit(solution)/shard_map/ppermute | solution.py:302
  44.1 4.9 %shard_map.130 = f32[64,512]{1,0:T(8,128)S(1)} custom-call(s32[1]{0:T(128)} %bitcast.1.side_ref, bf16[512,512]{1,0:T(8,128)(2,1)S(1)} %shard_map.128.refs_0_, bf16[512,512]{1,0:T(8,128)(2,1)S(1)} %shard_map.129.refs_1_, bf16[512,512]{1,0:T(8,128)(2,1)S(1)} %collective-permute-done.refs_2_, bf16[512,512]{1,0:T(8,128)(2,1)S(1)} %collective-permute-done.1.refs_3_, ...), custom_call_target="tpu_custom_call" | custom-call | flops 1 | bytes 1 | tf_op jit(solution)/shard_map/pallas_call | solution.py:274
  52.2 5.9 %collective-permute-start.7 = (f32[4,2,1024]{2,1,0:T(2,128)S(1)}, f32[4,2,1024]{2,1,0:T(2,128)S(1)}, u32[]{:S(2)}, u32[]{:S(2)}) collective-permute-start(f32[4,2,1024]{2,1,0:T(2,128)S(1)} %bitcast.184), channel_id=1, source_target_pairs={{0,4},{2,6},{4,0},{6,2},{8,12},{10,14},{12,8},{14,10},{16,20},{18,... | collective-permute-start | bytes 98312 | tf_op jit(solution)/shard_map/ppermute | solution.py:302
  58.4 2.0 collective-permute-done.7
  60.4 11.2 %collective-permute-done.8 = f32[4,2,1024]{2,1,0:T(2,128)S(1)} collective-permute-done((f32[4,2,1024]{2,1,0:T(2,128)S(1)}, f32[4,2,1024]{2,1,0:T(2,128)S(1)}, u32[]{:S(2)}, u32[]{:S(2)}) %collective-permute-start.8) | collective-permute-done | bytes 32800 | tf_op jit(solution)/shard_map/ppermute | solution.py:302
  71.8 12.2 %collective-permute-start.11 = (f32[4,2,1024]{2,1,0:T(2,128)S(1)}, f32[4,2,1024]{2,1,0:T(2,128)S(1)}, u32[]{:S(2)}, u32[]{:S(2)}) collective-permute-start(f32[4,2,1024]{2,1,0:T(2,128)S(1)} %get-tuple-element.123), channel_id=1, source_target_pairs={{0,24},{2,26},{4,28},{6,30},{8,16},{10,18},{12,20},{14,22},{16,8},... | collective-permute-start | bytes 98312 | tf_op jit(solution)/shard_map/ppermute | solution.py:302
  85.4 18.1 %collective-permute-done.10 = f32[4,2,1024]{2,1,0:T(2,128)S(1)} collective-permute-done((f32[4,2,1024]{2,1,0:T(2,128)S(1)}, f32[4,2,1024]{2,1,0:T(2,128)S(1)}, u32[]{:S(2)}, u32[]{:S(2)}) %collective-permute-start.10) | collective-permute-done | bytes 32800 | tf_op jit(solution)/shard_map/ppermute | solution.py:302
  103.6 2.5 collective-permute-done.11
  107.5 2.9 %collective-permute-start.20 = (bf16[194,1024]{1,0:T(8,128)(2,1)S(1)}, bf16[194,1024]{1,0:T(8,128)(2,1)S(1)}, u32[]{:S(2)}, u32[]{:S(2)}) collective-permute-start(bf16[194,1024]{1,0:T(8,128)(2,1)S(1)} %pad_maximum_fusion.8), channel_id=1, source_target_pairs={{0,16},{2,18},{4,20},{6,22},{8,24},{10,26},{12,28},{14,30},{16,0},... | collective-permute-start | bytes 1191944 | tf_op jit(solution)/shard_map/ppermute | solution.py:302
  111.2 1.8 shard_map.131
  115.4 3.3 %collective-permute-done.13 = f32[16,32]{1,0:T(8,128)S(1)} collective-permute-done((f32[16,32]{1,0:T(8,128)S(1)}, f32[16,32]{1,0:T(8,128)S(1)}, u32[]{:S(2)}, u32[]{:S(2)}) %collective-permute-start.13) | collective-permute-done | bytes 2080 | tf_op jit(solution)/shard_map/ppermute | solution.py:302
  119.3 3.1 %collective-permute-done.14 = f32[16,32]{1,0:T(8,128)S(1)} collective-permute-done((f32[16,32]{1,0:T(8,128)S(1)}, f32[16,32]{1,0:T(8,128)S(1)}, u32[]{:S(2)}, u32[]{:S(2)}) %collective-permute-start.14) | collective-permute-done | bytes 2080 | tf_op jit(solution)/shard_map/ppermute | solution.py:302
  122.4 4.3 %shard_map.132.x_ref = bf16[16,128,1024]{2,1,0:T(8,128)(2,1)} custom-call(bf16[16,128,1024]{2,1,0:T(8,128)(2,1)} %all-to-all-done.x_ref), custom_call_target="tpu_custom_call" | custom-call | flops 1 | bytes 1 | tf_op jit(solution)/shard_map/pallas_call | solution.py:71
  126.6 3.7 %collective-permute-done.16 = bf16[4,32,1024]{2,1,0:T(8,128)(2,1)S(1)} collective-permute-done((bf16[4,32,1024]{2,1,0:T(8,128)(2,1)S(1)}, bf16[4,32,1024]{2,1,0:T(8,128)(2,1)S(1)}, u32[]{:S(2)}, u32[]{:S(2)}) %collective-permute-start.16) | collective-permute-done | bytes 262176 | tf_op jit(solution)/shard_map/ppermute | solution.py:302
  130.4 2.1 collective-permute-start.18
  135.1 2.3 collective-permute-done.19.far3_ref
  138.9 6.0 %shard_map.133 = (bf16[16,16]{1,0:T(8,128)(2,1)}, bf16[256,256]{1,0:T(8,128)(2,1)}, bf16[16,128,1024]{2,1,0:T(8,128)(2,1)}) custom-call(f32[16,32]{1,0:T(8,128)} %copy-done.9, f32[16,32]{1,0:T(8,128)} %copy-done.12, f32[16,32]{1,0:T(8,128)} %copy-done.13, f32[16,32]{1,0:T(8,128)} %copy-done.14, bf16[16,128,1024]{2,1,0:T(8,128)(2,1)} %shard_map.132.x_ref), custom_call_target="tpu_custom_call" | custom-call | flops 1 | bytes 1 | tf_op jit(solution)/shard_map/pallas_call | solution.py:152
  144.9 6.2 %all-to-all-start.1 = ((bf16[16,128,1024]{2,1,0:T(8,128)(2,1)}), bf16[16,128,1024]{2,1,0:T(8,128)(2,1)}, u32[]{:S(2)}, u32[]{:S(2)}) async-start(bf16[16,128,1024]{2,1,0:T(8,128)(2,1)} %get-tuple-element.76), calls=%async_computation.1 | async-start | bytes 8388608 | tf_op jit(solution)/shard_map/all_to_all | solution.py:297
  152.5 2.9 %shard_map.134 = bf16[16,32,1024]{2,1,0:T(8,128)(2,1)} custom-call(bf16[256,256]{1,0:T(8,128)(2,1)} %get-tuple-element.63.spread_ref, bf16[16,32,1024]{2,1,0:T(8,128)(2,1)} %bitcast.169), custom_call_target="tpu_custom_call" | custom-call | flops 1 | bytes 1 | tf_op jit(solution)/shard_map/pallas_call | solution.py:71
  162.0 8.1 %collective-permute-done.22 = bf16[4,32,1024]{2,1,0:T(8,128)(2,1)S(1)} collective-permute-done((bf16[4,32,1024]{2,1,0:T(8,128)(2,1)S(1)}, bf16[4,32,1024]{2,1,0:T(8,128)(2,1)S(1)}, u32[]{:S(2)}, u32[]{:S(2)}) %collective-permute-start.22) | collective-permute-done | bytes 262176 | tf_op jit(solution)/shard_map/ppermute | solution.py:302
  170.1 14.2 %collective-permute-done.23 = bf16[4,32,1024]{2,1,0:T(8,128)(2,1)S(1)} collective-permute-done((bf16[4,32,1024]{2,1,0:T(8,128)(2,1)S(1)}, bf16[4,32,1024]{2,1,0:T(8,128)(2,1)S(1)}, u32[]{:S(2)}, u32[]{:S(2)}) %collective-permute-start.23) | collective-permute-done | bytes 262176 | tf_op jit(solution)/shard_map/ppermute | solution.py:302
  184.7 17.1 %collective-permute-done.25 = bf16[4,66,1024]{2,0,1:T(4,128)(2,1)S(1)} collective-permute-done((bf16[4,66,1024]{2,0,1:T(4,128)(2,1)S(1)}, bf16[4,66,1024]{2,0,1:T(4,128)(2,1)S(1)}, u32[]{:S(2)}, u32[]{:S(2)}) %collective-permute-start.25) | collective-permute-done | bytes 540704 | tf_op jit(solution)/shard_map/ppermute | solution.py:302
  203.0 3.6 %collective-permute-start.29 = (bf16[8,66,1024]{2,0,1:T(8,128)(2,1)S(1)}, bf16[8,66,1024]{2,0,1:T(8,128)(2,1)}, u32[]{:S(2)}, u32[]{:S(2)}) collective-permute-start(bf16[8,66,1024]{2,0,1:T(8,128)(2,1)S(1)} %pad_maximum_fusion), channel_id=1, source_target_pairs={{0,2},{2,0},{4,6},{6,4},{8,10},{10,8},{12,14},{14,12},{16,18},{18,... | collective-permute-start | bytes 3244040 | tf_op jit(solution)/shard_map/ppermute | solution.py:302
  209.0 8.4 %collective-permute-start.26 = (bf16[4,32,1024]{2,1,0:T(8,128)(2,1)}, bf16[4,32,1024]{2,1,0:T(8,128)(2,1)S(1)}, u32[]{:S(2)}, u32[]{:S(2)}) collective-permute-start(bf16[4,32,1024]{2,1,0:T(8,128)(2,1)} %get-tuple-element.91), channel_id=1, source_target_pairs={{0,8},{2,10},{4,12},{6,14},{8,0},{10,2},{12,4},{14,6},{16,24},{18,... | collective-permute-start | bytes 786440 | tf_op jit(solution)/shard_map/ppermute | solution.py:302
  219.6 8.9 %collective-permute-done.29 = bf16[8,66,1024]{2,0,1:T(8,128)(2,1)} collective-permute-done((bf16[8,66,1024]{2,0,1:T(8,128)(2,1)S(1)}, bf16[8,66,1024]{2,0,1:T(8,128)(2,1)}, u32[]{:S(2)}, u32[]{:S(2)}) %collective-permute-start.29) | collective-permute-done | bytes 1081376 | tf_op jit(solution)/shard_map/ppermute | solution.py:302
  228.4 2.0 convert_reduce_fusion
  231.5 2.1 multiply_reduce_fusion
  236.4 17.6 %all-to-all-done.1.x_ref = bf16[16,128,1024]{2,1,0:T(8,128)(2,1)} async-done(((bf16[16,128,1024]{2,1,0:T(8,128)(2,1)}), bf16[16,128,1024]{2,1,0:T(8,128)(2,1)}, u32[]{:S(2)}, u32[]{:S(2)}) %all-to-all-start.1) | async-done | bytes 4194336 | tf_op jit(solution)/shard_map/all_to_all | solution.py:297
  253.9 3.7 %shard_map.135 = bf16[16,128,1024]{2,1,0:T(8,128)(2,1)} custom-call(bf16[16,128,1024]{2,1,0:T(8,128)(2,1)} %all-to-all-done.1.x_ref), custom_call_target="tpu_custom_call" | custom-call | flops 1 | bytes 1 | tf_op jit(solution)/shard_map/pallas_call | solution.py:71
  259.4 4.8 %collective-permute-done.28.refs_3_ = bf16[4,32,1024]{2,1,0:T(8,128)(2,1)S(1)} collective-permute-done((bf16[4,32,1024]{2,1,0:T(8,128)(2,1)}, bf16[4,32,1024]{2,1,0:T(8,128)(2,1)S(1)}, u32[]{:S(2)}, u32[]{:S(2)}) %collective-permute-start.28) | collective-permute-done | bytes 262176 | tf_op jit(solution)/shard_map/ppermute | solution.py:302
  (142 shorter events, 44.0 us)
Async XLA Ops:
  0.6 121.7 %all-to-all-start = ((bf16[16,128,1024]{2,1,0:T(8,128)(2,1)}), bf16[16,128,1024]{2,1,0:T(8,128)(2,1)}, u32[]{:S(2)}, u32[]{:S(2)}) async-start(bf16[16,128,1024]{2,1,0:T(8,128)(2,1)} %bitcast.150), calls=%async_computation | async-start | bytes 8388608 | tf_op jit(solution)/shard_map/all_to_all | solution.py:297
  8.9 19.2 %collective-permute-start.3 = (bf16[4,32,1024]{2,1,0:T(8,128)(2,1)}, bf16[4,32,1024]{2,1,0:T(8,128)(2,1)}, u32[]{:S(2)}, u32[]{:S(2)}) collective-permute-start(bf16[4,32,1024]{2,1,0:T(8,128)(2,1)} %get-tuple-element.116), channel_id=1, source_target_pairs={{0,2},{2,0},{4,6},{6,4},{8,10},{10,8},{12,14},{14,12},{16,18},{18,... | collective-permute-start | bytes 786440 | tf_op jit(solution)/shard_map/ppermute | solution.py:302
  10.4 32.3 %collective-permute-start.4 = (bf16[4,32,1024]{2,1,0:T(8,128)(2,1)}, bf16[4,32,1024]{2,1,0:T(8,128)(2,1)}, u32[]{:S(2)}, u32[]{:S(2)}) collective-permute-start(bf16[4,32,1024]{2,1,0:T(8,128)(2,1)} %get-tuple-element.115), channel_id=1, source_target_pairs={{0,4},{2,6},{4,0},{6,2},{8,12},{10,14},{12,8},{14,10},{16,20},{18,... | collective-permute-start | bytes 786440 | tf_op jit(solution)/shard_map/ppermute | solution.py:302
  11.0 31.7 %collective-permute-start.5 = (bf16[4,32,1024]{2,1,0:T(8,128)(2,1)}, bf16[4,32,1024]{2,1,0:T(8,128)(2,1)}, u32[]{:S(2)}, u32[]{:S(2)}) collective-permute-start(bf16[4,32,1024]{2,1,0:T(8,128)(2,1)} %get-tuple-element.114), channel_id=1, source_target_pairs={{0,6},{2,4},{4,2},{6,0},{8,14},{10,12},{12,10},{14,8},{16,22},{18,... | collective-permute-start | bytes 786440 | tf_op jit(solution)/shard_map/ppermute | solution.py:302
  13.3 30.7 %collective-permute-start = (bf16[512,512]{1,0:T(8,128)(2,1)S(1)}, bf16[512,512]{1,0:T(8,128)(2,1)S(1)}, u32[]{:S(2)}, u32[]{:S(2)}) collective-permute-start(bf16[512,512]{1,0:T(8,128)(2,1)S(1)} %shard_map.128.refs_0_), channel_id=1, source_target_pairs={{0,1},{1,0},{2,3},{3,2},{4,5},{5,4},{6,7},{7,6},{8,9},{9,8},{10,11... | collective-permute-start | bytes 1572872 | tf_op jit(solution)/shard_map/ppermute | solution.py:302
  14.3 29.7 %collective-permute-start.1 = (bf16[512,512]{1,0:T(8,128)(2,1)S(1)}, bf16[512,512]{1,0:T(8,128)(2,1)S(1)}, u32[]{:S(2)}, u32[]{:S(2)}) collective-permute-start(bf16[512,512]{1,0:T(8,128)(2,1)S(1)} %shard_map.129.refs_1_), channel_id=1, source_target_pairs={{0,1},{1,0},{2,3},{3,2},{4,5},{5,4},{6,7},{7,6},{8,9},{9,8},{10,11... | collective-permute-start | bytes 1572872 | tf_op jit(solution)/shard_map/ppermute | solution.py:302
  49.0 1.3 collective-permute-start.2
  50.7 7.7 %collective-permute-start.6 = (f32[4,2,1024]{2,1,0:T(2,128)S(1)}, f32[4,2,1024]{2,1,0:T(2,128)S(1)}, u32[]{:S(2)}, u32[]{:S(2)}) collective-permute-start(f32[4,2,1024]{2,1,0:T(2,128)S(1)} %bitcast.183), channel_id=1, source_target_pairs={{0,2},{2,0},{4,6},{6,4},{8,10},{10,8},{12,14},{14,12},{16,18},{18,... | collective-permute-start | bytes 98312 | tf_op jit(solution)/shard_map/ppermute | solution.py:302
  52.2 8.2 %collective-permute-start.7 = (f32[4,2,1024]{2,1,0:T(2,128)S(1)}, f32[4,2,1024]{2,1,0:T(2,128)S(1)}, u32[]{:S(2)}, u32[]{:S(2)}) collective-permute-start(f32[4,2,1024]{2,1,0:T(2,128)S(1)} %bitcast.184), channel_id=1, source_target_pairs={{0,4},{2,6},{4,0},{6,2},{8,12},{10,14},{12,8},{14,10},{16,20},{18,... | collective-permute-start | bytes 98312 | tf_op jit(solution)/shard_map/ppermute | solution.py:302
  58.1 13.4 %collective-permute-start.8 = (f32[4,2,1024]{2,1,0:T(2,128)S(1)}, f32[4,2,1024]{2,1,0:T(2,128)S(1)}, u32[]{:S(2)}, u32[]{:S(2)}) collective-permute-start(f32[4,2,1024]{2,1,0:T(2,128)S(1)} %bitcast.185), channel_id=1, source_target_pairs={{0,6},{2,4},{4,2},{6,0},{8,14},{10,12},{12,10},{14,8},{16,22},{18,... | collective-permute-start | bytes 98312 | tf_op jit(solution)/shard_map/ppermute | solution.py:302
  71.8 31.8 %collective-permute-start.10 = (f32[4,2,1024]{2,1,0:T(2,128)S(1)}, f32[4,2,1024]{2,1,0:T(2,128)S(1)}, u32[]{:S(2)}, u32[]{:S(2)}) collective-permute-start(f32[4,2,1024]{2,1,0:T(2,128)S(1)} %get-tuple-element.124), channel_id=1, source_target_pairs={{0,16},{2,18},{4,20},{6,22},{8,24},{10,26},{12,28},{14,30},{16,0},... | collective-permute-start | bytes 98312 | tf_op jit(solution)/shard_map/ppermute | solution.py:302
  71.8 34.2 %collective-permute-start.11 = (f32[4,2,1024]{2,1,0:T(2,128)S(1)}, f32[4,2,1024]{2,1,0:T(2,128)S(1)}, u32[]{:S(2)}, u32[]{:S(2)}) collective-permute-start(f32[4,2,1024]{2,1,0:T(2,128)S(1)} %get-tuple-element.123), channel_id=1, source_target_pairs={{0,24},{2,26},{4,28},{6,30},{8,16},{10,18},{12,20},{14,22},{16,8},... | collective-permute-start | bytes 98312 | tf_op jit(solution)/shard_map/ppermute | solution.py:302
  84.0 22.0 %collective-permute-start.9 = (f32[4,2,1024]{2,1,0:T(2,128)S(1)}, f32[4,2,1024]{2,1,0:T(2,128)S(1)}, u32[]{:S(2)}, u32[]{:S(2)}) collective-permute-start(f32[4,2,1024]{2,1,0:T(2,128)S(1)} %get-tuple-element.125), channel_id=1, source_target_pairs={{0,8},{2,10},{4,12},{6,14},{8,0},{10,2},{12,4},{14,6},{16,24},{18,... | collective-permute-start | bytes 98312 | tf_op jit(solution)/shard_map/ppermute | solution.py:302
  106.0 20.6 %collective-permute-start.15 = (bf16[4,32,1024]{2,1,0:T(8,128)(2,1)S(1)}, bf16[4,32,1024]{2,1,0:T(8,128)(2,1)S(1)}, u32[]{:S(2)}, u32[]{:S(2)}) collective-permute-start(bf16[4,32,1024]{2,1,0:T(8,128)(2,1)S(1)} %get-tuple-element.52), channel_id=1, source_target_pairs={{0,8},{2,10},{4,12},{6,14},{8,0},{10,2},{12,4},{14,6},{16,24},{18,... | collective-permute-start | bytes 786440 | tf_op jit(solution)/shard_map/ppermute | solution.py:302
  107.1 23.2 %collective-permute-start.16 = (bf16[4,32,1024]{2,1,0:T(8,128)(2,1)S(1)}, bf16[4,32,1024]{2,1,0:T(8,128)(2,1)S(1)}, u32[]{:S(2)}, u32[]{:S(2)}) collective-permute-start(bf16[4,32,1024]{2,1,0:T(8,128)(2,1)S(1)} %get-tuple-element.53), channel_id=1, source_target_pairs={{0,24},{2,26},{4,28},{6,30},{8,16},{10,18},{12,20},{14,22},{16,8},... | collective-permute-start | bytes 786440 | tf_op jit(solution)/shard_map/ppermute | solution.py:302
  107.5 27.5 %collective-permute-start.20 = (bf16[194,1024]{1,0:T(8,128)(2,1)S(1)}, bf16[194,1024]{1,0:T(8,128)(2,1)S(1)}, u32[]{:S(2)}, u32[]{:S(2)}) collective-permute-start(bf16[194,1024]{1,0:T(8,128)(2,1)S(1)} %pad_maximum_fusion.8), channel_id=1, source_target_pairs={{0,16},{2,18},{4,20},{6,22},{8,24},{10,26},{12,28},{14,30},{16,0},... | collective-permute-start | bytes 1191944 | tf_op jit(solution)/shard_map/ppermute | solution.py:302
  113.0 1.4 collective-permute-start.12
  115.1 3.7 %collective-permute-start.13 = (f32[16,32]{1,0:T(8,128)S(1)}, f32[16,32]{1,0:T(8,128)S(1)}, u32[]{:S(2)}, u32[]{:S(2)}) collective-permute-start(f32[16,32]{1,0:T(8,128)S(1)} %add.148), channel_id=1, source_target_pairs={{0,2},{2,0},{4,6},{6,4},{8,10},{10,8},{12,14},{14,12},{16,18},{18,... | collective-permute-start | bytes 6152 | tf_op jit(solution)/shard_map/ppermute | solution.py:302
  118.7 3.7 %collective-permute-start.14 = (f32[16,32]{1,0:T(8,128)S(1)}, f32[16,32]{1,0:T(8,128)S(1)}, u32[]{:S(2)}, u32[]{:S(2)}) collective-permute-start(f32[16,32]{1,0:T(8,128)S(1)} %add.149), channel_id=1, source_target_pairs={{0,4},{2,6},{4,0},{6,2},{8,12},{10,14},{12,8},{14,10},{16,20},{18,... | collective-permute-start | bytes 6152 | tf_op jit(solution)/shard_map/ppermute | solution.py:302
  130.4 4.7 %collective-permute-start.17 = (f32[16,32]{1,0:T(8,128)S(1)}, f32[16,32]{1,0:T(8,128)S(1)}, u32[]{:S(2)}, u32[]{:S(2)}) collective-permute-start(f32[16,32]{1,0:T(8,128)S(1)} %add.150.own_ref), channel_id=1, source_target_pairs={{0,8},{2,10},{4,12},{6,14},{8,0},{10,2},{12,4},{14,6},{16,24},{18,... | collective-permute-start | bytes 6152 | tf_op jit(solution)/shard_map/ppermute | solution.py:302
  130.4 4.7 %collective-permute-start.18 = (f32[16,32]{1,0:T(8,128)S(1)}, f32[16,32]{1,0:T(8,128)S(1)}, u32[]{:S(2)}, u32[]{:S(2)}) collective-permute-start(f32[16,32]{1,0:T(8,128)S(1)} %add.150.own_ref), channel_id=1, source_target_pairs={{0,16},{2,18},{4,20},{6,22},{8,24},{10,26},{12,28},{14,30},{16,0},... | collective-permute-start | bytes 6152 | tf_op jit(solution)/shard_map/ppermute | solution.py:302
  132.5 4.9 %collective-permute-start.19 = (f32[16,32]{1,0:T(8,128)S(1)}, f32[16,32]{1,0:T(8,128)S(1)}, u32[]{:S(2)}, u32[]{:S(2)}) collective-permute-start(f32[16,32]{1,0:T(8,128)S(1)} %add.150.own_ref), channel_id=1, source_target_pairs={{0,24},{2,26},{4,28},{6,30},{8,16},{10,18},{12,20},{14,22},{16,8},... | collective-permute-start | bytes 6152 | tf_op jit(solution)/shard_map/ppermute | solution.py:302
  137.4 7.5 %collective-permute-start.21 = (bf16[2,66,1024]{2,1,0:T(8,128)(2,1)S(1)}, bf16[2,66,1024]{2,1,0:T(8,128)(2,1)S(1)}, u32[]{:S(2)}, u32[]{:S(2)}) collective-permute-start(bf16[2,66,1024]{2,1,0:T(8,128)(2,1)S(1)} %pad_maximum_fusion.9), channel_id=1, source_target_pairs={{0,8},{2,10},{4,12},{6,14},{8,0},{10,2},{12,4},{14,6},{16,24},{18,... | collective-permute-start | bytes 811016 | tf_op jit(solution)/shard_map/ppermute | solution.py:302
  144.9 109.0 %all-to-all-start.1 = ((bf16[16,128,1024]{2,1,0:T(8,128)(2,1)}), bf16[16,128,1024]{2,1,0:T(8,128)(2,1)}, u32[]{:S(2)}, u32[]{:S(2)}) async-start(bf16[16,128,1024]{2,1,0:T(8,128)(2,1)} %get-tuple-element.76), calls=%async_computation.1 | async-start | bytes 8388608 | tf_op jit(solution)/shard_map/all_to_all | solution.py:297
  156.6 13.5 %collective-permute-start.22 = (bf16[4,32,1024]{2,1,0:T(8,128)(2,1)S(1)}, bf16[4,32,1024]{2,1,0:T(8,128)(2,1)S(1)}, u32[]{:S(2)}, u32[]{:S(2)}) collective-permute-start(bf16[4,32,1024]{2,1,0:T(8,128)(2,1)S(1)} %get-tuple-element.100), channel_id=1, source_target_pairs={{0,2},{2,0},{4,6},{6,4},{8,10},{10,8},{12,14},{14,12},{16,18},{18,... | collective-permute-start | bytes 786440 | tf_op jit(solution)/shard_map/ppermute | solution.py:302
  158.2 26.1 %collective-permute-start.23 = (bf16[4,32,1024]{2,1,0:T(8,128)(2,1)S(1)}, bf16[4,32,1024]{2,1,0:T(8,128)(2,1)S(1)}, u32[]{:S(2)}, u32[]{:S(2)}) collective-permute-start(bf16[4,32,1024]{2,1,0:T(8,128)(2,1)S(1)} %get-tuple-element.99), channel_id=1, source_target_pairs={{0,4},{2,6},{4,0},{6,2},{8,12},{10,14},{12,8},{14,10},{16,20},{18,... | collective-permute-start | bytes 786440 | tf_op jit(solution)/shard_map/ppermute | solution.py:302
  158.7 25.5 %collective-permute-start.24 = (bf16[4,32,1024]{2,1,0:T(8,128)(2,1)S(1)}, bf16[4,32,1024]{2,1,0:T(8,128)(2,1)S(1)}, u32[]{:S(2)}, u32[]{:S(2)}) collective-permute-start(bf16[4,32,1024]{2,1,0:T(8,128)(2,1)S(1)} %get-tuple-element.98), channel_id=1, source_target_pairs={{0,6},{2,4},{4,2},{6,0},{8,14},{10,12},{12,10},{14,8},{16,22},{18,... | collective-permute-start | bytes 786440 | tf_op jit(solution)/shard_map/ppermute | solution.py:302
  160.7 41.1 %collective-permute-start.25 = (bf16[4,66,1024]{2,0,1:T(4,128)(2,1)S(1)}, bf16[4,66,1024]{2,0,1:T(4,128)(2,1)S(1)}, u32[]{:S(2)}, u32[]{:S(2)}) collective-permute-start(bf16[4,66,1024]{2,0,1:T(4,128)(2,1)S(1)} %copy.26), channel_id=1, source_target_pairs={{0,4},{2,6},{4,0},{6,2},{8,12},{10,14},{12,8},{14,10},{16,20},{18,... | collective-permute-start | bytes 1622024 | tf_op jit(solution)/shard_map/ppermute | solution.py:302
  203.0 25.4 %collective-permute-start.29 = (bf16[8,66,1024]{2,0,1:T(8,128)(2,1)S(1)}, bf16[8,66,1024]{2,0,1:T(8,128)(2,1)}, u32[]{:S(2)}, u32[]{:S(2)}) collective-permute-start(bf16[8,66,1024]{2,0,1:T(8,128)(2,1)S(1)} %pad_maximum_fusion), channel_id=1, source_target_pairs={{0,2},{2,0},{4,6},{6,4},{8,10},{10,8},{12,14},{14,12},{16,18},{18,... | collective-permute-start | bytes 3244040 | tf_op jit(solution)/shard_map/ppermute | solution.py:302
  209.0 48.7 %collective-permute-start.26 = (bf16[4,32,1024]{2,1,0:T(8,128)(2,1)}, bf16[4,32,1024]{2,1,0:T(8,128)(2,1)S(1)}, u32[]{:S(2)}, u32[]{:S(2)}) collective-permute-start(bf16[4,32,1024]{2,1,0:T(8,128)(2,1)} %get-tuple-element.91), channel_id=1, source_target_pairs={{0,8},{2,10},{4,12},{6,14},{8,0},{10,2},{12,4},{14,6},{16,24},{18,... | collective-permute-start | bytes 786440 | tf_op jit(solution)/shard_map/ppermute | solution.py:302
  217.4 42.0 %collective-permute-start.27 = (bf16[4,32,1024]{2,1,0:T(8,128)(2,1)}, bf16[4,32,1024]{2,1,0:T(8,128)(2,1)S(1)}, u32[]{:S(2)}, u32[]{:S(2)}) collective-permute-start(bf16[4,32,1024]{2,1,0:T(8,128)(2,1)} %get-tuple-element.90), channel_id=1, source_target_pairs={{0,16},{2,18},{4,20},{6,22},{8,24},{10,26},{12,28},{14,30},{16,0},... | collective-permute-start | bytes 786440 | tf_op jit(solution)/shard_map/ppermute | solution.py:302
  218.2 46.0 %collective-permute-start.28 = (bf16[4,32,1024]{2,1,0:T(8,128)(2,1)}, bf16[4,32,1024]{2,1,0:T(8,128)(2,1)S(1)}, u32[]{:S(2)}, u32[]{:S(2)}) collective-permute-start(bf16[4,32,1024]{2,1,0:T(8,128)(2,1)} %get-tuple-element.89), channel_id=1, source_target_pairs={{0,24},{2,26},{4,28},{6,30},{8,16},{10,18},{12,20},{14,22},{16,8},... | collective-permute-start | bytes 786440 | tf_op jit(solution)/shard_map/ppermute | solution.py:302
  (17 other events, 171.3 us)

commit v7 on v6

--- a/solution.py
+++ b/solution.py
@@ -360,8 +360,8 @@
             parts = jnp.stack([parts[0]] + [swap(parts[i], "member", i) for i in range(1, PLANE)])
             return jnp.stack([pick(parts, place ^ i) for i in range(PLANE)])
 
-        slabs = within(slabs_first.reshape((planes, PLANE) + slabs_first.shape[1:]))
-        both, slabs = lax.optimization_barrier((both, slabs))
+        slabs = after(slabs_first, partial_out)
+        slabs = within(slabs.reshape((planes, PLANE) + slabs.shape[1:]))
         both = within(both.reshape((planes, PLANE) + both.shape[1:]))
         parts = [pick(both, plane ^ i, 1) for i in range(planes)]
         parts = [parts[0]] + [across(parts[i], i) for i in range(1, planes)]

time: 266 us -> 263 us (0.989)
  starting transfers between devices: 66.5 us -> 57.1 us
  waiting for transfers between devices: 149 us -> 155 us
  local copies, waits for them, and re-layouts: 8.14 us -> 10.9 us
    ppermute x30, starting transfers between devices: 53.1 us -> 44.7 us  [swap(): return lax.ppermute(x, axis, [(i, i ^ bit) for i in range(count)])]
    ppermute x30, waiting for transfers between devices: 132 us -> 136 us  [swap(): return lax.ppermute(x, axis, [(i, i ^ bit) for i in range(count)])]
  transfers between devices with their start and end apart: 32 -> 32, of which waited for: 21 -> 22; matrix products, arithmetic and copies ran while one was open for 8% -> 8% of each run, Pallas kernels for 10% -> 10%
where the time goes in v7:
time: 263 us
  waiting for transfers between devices  155 us (59%)
  starting transfers between devices  57.1 us (22%)
  Pallas kernels  26.3 us (10%)
  other arithmetic  12 us (5%)
  local copies, waits for them, and re-layouts  10.9 us (4%)
    ppermute x30, waiting for transfers between devices, swap(): return lax.ppermute(x, axis, [(i, i ^ bit) for i in range(count)])  136 us
    ppermute x30, starting transfers between devices, swap(): return lax.ppermute(x, axis, [(i, i ^ bit) for i in range(count)])  44.7 us
    all_to_all x2, waiting for transfers between devices, exchange(): return lax.all_to_all(x, 'member', split_axis=0, concat_axis=0, tiled=True)  19.3 us
    all_to_all x2, starting transfers between devices, exchange(): return lax.all_to_all(x, 'member', split_axis=0, concat_axis=0, tiled=True)  12.4 us
    pallas_call x3, Pallas kernels, blocked(): pl.pallas_call(kernel, grid=(total // rows,), in_specs=[pl.BlockSpec(w.sh...  10.9 us
    pallas_call x1, Pallas kernels, solve(): pl.pallas_call(solve_kernel, in_specs=[vmem] * len(sums) + [anywhere], ou...  6.04 us
  transfers between devices with their start and end apart: 32, of which 22 were waited for; matrix products, arithmetic and copies ran while one was open for 8% of the time, Pallas kernels for 10%

profile of v7, /device:TPU:12, one launch (start us, length us, event | category | flops | bytes accessed | tf_op | source)
XLA Modules:
  0.0 262.6 jit_solution(1651509867668492895)
XLA Ops:
  0.7 7.3 %all-to-all-start = ((bf16[16,128,1024]{2,1,0:T(8,128)(2,1)}), bf16[16,128,1024]{2,1,0:T(8,128)(2,1)}, u32[]{:S(2)}, u32[]{:S(2)}) async-start(bf16[16,128,1024]{2,1,0:T(8,128)(2,1)} %bitcast.153), calls=%async_computation | async-start | bytes 8388608 | tf_op jit(solution)/shard_map/all_to_all | solution.py:297
  12.1 2.2 copy-done
  14.3 4.8 %shard_map.130 = f32[64,512]{1,0:T(8,128)S(1)} custom-call(s32[1]{0:T(128)} %bitcast.1.side_ref, bf16[512,512]{1,0:T(8,128)(2,1)S(1)} %shard_map.128.refs_0_, bf16[512,512]{1,0:T(8,128)(2,1)S(1)} %shard_map.129.refs_1_, bf16[512,512]{1,0:T(8,128)(2,1)S(1)} %collective-permute-done.refs_2_, bf16[512,512]{1,0:T(8,128)(2,1)S(1)} %collective-permute-done.1.refs_3_, ...), custom_call_target="tpu_custom_call" | custom-call | flops 1 | bytes 1 | tf_op jit(solution)/shard_map/pallas_call | solution.py:274
  24.5 1.5 collective-permute-start.9
  29.0 8.9 %collective-permute-start.7 = (f32[4,2,1024]{2,1,0:T(2,128)S(1)}, f32[4,2,1024]{2,1,0:T(2,128)S(1)}, u32[]{:S(2)}, u32[]{:S(2)}) collective-permute-start(f32[4,2,1024]{2,1,0:T(2,128)S(1)} %get-tuple-element.122), channel_id=1, source_target_pairs={{0,16},{2,18},{4,20},{6,22},{8,24},{10,26},{12,28},{14,30},{16,0},... | collective-permute-start | bytes 98312 | tf_op jit(solution)/shard_map/ppermute | solution.py:302
  38.3 5.7 %collective-permute-done.10 = bf16[4,32,1024]{2,1,0:T(8,128)(2,1)S(1)} collective-permute-done((bf16[4,32,1024]{2,1,0:T(8,128)(2,1)S(1)}, bf16[4,32,1024]{2,1,0:T(8,128)(2,1)S(1)}, u32[]{:S(2)}, u32[]{:S(2)}) %collective-permute-start.10) | collective-permute-done | bytes 262176 | tf_op jit(solution)/shard_map/ppermute | solution.py:302
  44.1 17.7 %collective-permute-done.11 = bf16[4,32,1024]{2,1,0:T(8,128)(2,1)S(1)} collective-permute-done((bf16[4,32,1024]{2,1,0:T(8,128)(2,1)S(1)}, bf16[4,32,1024]{2,1,0:T(8,128)(2,1)S(1)}, u32[]{:S(2)}, u32[]{:S(2)}) %collective-permute-start.11) | collective-permute-done | bytes 262176 | tf_op jit(solution)/shard_map/ppermute | solution.py:302
  62.3 18.5 %collective-permute-done.6 = f32[4,2,1024]{2,1,0:T(2,128)S(1)} collective-permute-done((f32[4,2,1024]{2,1,0:T(2,128)S(1)}, f32[4,2,1024]{2,1,0:T(2,128)S(1)}, u32[]{:S(2)}, u32[]{:S(2)}) %collective-permute-start.6) | collective-permute-done | bytes 32800 | tf_op jit(solution)/shard_map/ppermute | solution.py:302
  80.8 20.0 %collective-permute-done.7 = f32[4,2,1024]{2,1,0:T(2,128)S(1)} collective-permute-done((f32[4,2,1024]{2,1,0:T(2,128)S(1)}, f32[4,2,1024]{2,1,0:T(2,128)S(1)}, u32[]{:S(2)}, u32[]{:S(2)}) %collective-permute-start.7) | collective-permute-done | bytes 32800 | tf_op jit(solution)/shard_map/ppermute | solution.py:302
  100.8 4.4 %collective-permute-done.8 = f32[4,2,1024]{2,1,0:T(2,128)S(1)} collective-permute-done((f32[4,2,1024]{2,1,0:T(2,128)S(1)}, f32[4,2,1024]{2,1,0:T(2,128)S(1)}, u32[]{:S(2)}, u32[]{:S(2)}) %collective-permute-start.8) | collective-permute-done | bytes 32800 | tf_op jit(solution)/shard_map/ppermute | solution.py:302
  106.4 3.3 %collective-permute-start.20 = (bf16[194,1024]{1,0:T(8,128)(2,1)S(1)}, bf16[194,1024]{1,0:T(8,128)(2,1)S(1)}, u32[]{:S(2)}, u32[]{:S(2)}) collective-permute-start(bf16[194,1024]{1,0:T(8,128)(2,1)S(1)} %pad_maximum_fusion.8), channel_id=1, source_target_pairs={{0,16},{2,18},{4,20},{6,22},{8,24},{10,26},{12,28},{14,30},{16,0},... | collective-permute-start | bytes 1191944 | tf_op jit(solution)/shard_map/ppermute | solution.py:302
  110.5 1.8 shard_map.131
  114.3 3.6 %collective-permute-done.13 = f32[16,32]{1,0:T(8,128)S(1)} collective-permute-done((f32[16,32]{1,0:T(8,128)S(1)}, f32[16,32]{1,0:T(8,128)S(1)}, u32[]{:S(2)}, u32[]{:S(2)}) %collective-permute-start.13) | collective-permute-done | bytes 2080 | tf_op jit(solution)/shard_map/ppermute | solution.py:302
  118.0 3.6 %collective-permute-done.14 = f32[16,32]{1,0:T(8,128)S(1)} collective-permute-done((f32[16,32]{1,0:T(8,128)S(1)}, f32[16,32]{1,0:T(8,128)S(1)}, u32[]{:S(2)}, u32[]{:S(2)}) %collective-permute-start.14) | collective-permute-done | bytes 2080 | tf_op jit(solution)/shard_map/ppermute | solution.py:302
  121.6 4.3 %shard_map.132.x_ref = bf16[16,128,1024]{2,1,0:T(8,128)(2,1)} custom-call(bf16[16,128,1024]{2,1,0:T(8,128)(2,1)} %all-to-all-done.x_ref), custom_call_target="tpu_custom_call" | custom-call | flops 1 | bytes 1 | tf_op jit(solution)/shard_map/pallas_call | solution.py:71
  125.9 4.1 %collective-permute-done.16 = bf16[4,32,1024]{2,1,0:T(8,128)(2,1)S(1)} collective-permute-done((bf16[4,32,1024]{2,1,0:T(8,128)(2,1)S(1)}, bf16[4,32,1024]{2,1,0:T(8,128)(2,1)S(1)}, u32[]{:S(2)}, u32[]{:S(2)}) %collective-permute-start.16) | collective-permute-done | bytes 262176 | tf_op jit(solution)/shard_map/ppermute | solution.py:302
  131.2 2.3 collective-permute-start.19
  134.6 1.9 collective-permute-done.19.far3_ref
  138.1 6.0 %shard_map.133 = (bf16[16,16]{1,0:T(8,128)(2,1)}, bf16[256,256]{1,0:T(8,128)(2,1)}, bf16[16,128,1024]{2,1,0:T(8,128)(2,1)}) custom-call(f32[16,32]{1,0:T(8,128)} %copy-done.10, f32[16,32]{1,0:T(8,128)} %copy-done.13, f32[16,32]{1,0:T(8,128)} %copy-done.14, f32[16,32]{1,0:T(8,128)} %copy-done.15, bf16[16,128,1024]{2,1,0:T(8,128)(2,1)} %shard_map.132.x_ref), custom_call_target="tpu_custom_call" | custom-call | flops 1 | bytes 1 | tf_op jit(solution)/shard_map/pallas_call | solution.py:152
  144.2 5.1 %all-to-all-start.1 = ((bf16[16,128,1024]{2,1,0:T(8,128)(2,1)}), bf16[16,128,1024]{2,1,0:T(8,128)(2,1)}, u32[]{:S(2)}, u32[]{:S(2)}) async-start(bf16[16,128,1024]{2,1,0:T(8,128)(2,1)} %get-tuple-element.74), calls=%async_computation.1 | async-start | bytes 8388608 | tf_op jit(solution)/shard_map/all_to_all | solution.py:297
  150.6 2.9 %shard_map.134 = bf16[16,32,1024]{2,1,0:T(8,128)(2,1)} custom-call(bf16[256,256]{1,0:T(8,128)(2,1)} %get-tuple-element.61.spread_ref, bf16[16,32,1024]{2,1,0:T(8,128)(2,1)} %bitcast.172), custom_call_target="tpu_custom_call" | custom-call | flops 1 | bytes 1 | tf_op jit(solution)/shard_map/pallas_call | solution.py:71
  160.2 7.6 %collective-permute-done.22 = bf16[4,32,1024]{2,1,0:T(8,128)(2,1)S(1)} collective-permute-done((bf16[4,32,1024]{2,1,0:T(8,128)(2,1)S(1)}, bf16[4,32,1024]{2,1,0:T(8,128)(2,1)S(1)}, u32[]{:S(2)}, u32[]{:S(2)}) %collective-permute-start.22) | collective-permute-done | bytes 262176 | tf_op jit(solution)/shard_map/ppermute | solution.py:302
  167.8 14.2 %collective-permute-done.23 = bf16[4,32,1024]{2,1,0:T(8,128)(2,1)S(1)} collective-permute-done((bf16[4,32,1024]{2,1,0:T(8,128)(2,1)S(1)}, bf16[4,32,1024]{2,1,0:T(8,128)(2,1)S(1)}, u32[]{:S(2)}, u32[]{:S(2)}) %collective-permute-start.23) | collective-permute-done | bytes 262176 | tf_op jit(solution)/shard_map/ppermute | solution.py:302
  183.3 16.8 %collective-permute-done.25 = bf16[4,66,1024]{2,0,1:T(4,128)(2,1)S(1)} collective-permute-done((bf16[4,66,1024]{2,0,1:T(4,128)(2,1)S(1)}, bf16[4,66,1024]{2,0,1:T(4,128)(2,1)S(1)}, u32[]{:S(2)}, u32[]{:S(2)}) %collective-permute-start.25) | collective-permute-done | bytes 540704 | tf_op jit(solution)/shard_map/ppermute | solution.py:302
  200.1 2.2 pad_maximum_fusion
  202.3 3.5 %collective-permute-start.29 = (bf16[8,66,1024]{2,0,1:T(8,128)(2,1)}, bf16[8,66,1024]{2,0,1:T(8,128)(2,1)S(1)}, u32[]{:S(2)}, u32[]{:S(2)}) collective-permute-start(bf16[8,66,1024]{2,0,1:T(8,128)(2,1)} %pad_maximum_fusion), channel_id=1, source_target_pairs={{0,2},{2,0},{4,6},{6,4},{8,10},{10,8},{12,14},{14,12},{16,18},{18,... | collective-permute-start | bytes 3244040 | tf_op jit(solution)/shard_map/ppermute | solution.py:302
  207.3 2.1 dynamic-slice_bitcast_fusion
  209.4 8.1 %collective-permute-start.26 = (bf16[4,32,1024]{2,1,0:T(8,128)(2,1)}, bf16[4,32,1024]{2,1,0:T(8,128)(2,1)S(1)}, u32[]{:S(2)}, u32[]{:S(2)}) collective-permute-start(bf16[4,32,1024]{2,1,0:T(8,128)(2,1)} %get-tuple-element.89), channel_id=1, source_target_pairs={{0,8},{2,10},{4,12},{6,14},{8,0},{10,2},{12,4},{14,6},{16,24},{18,... | collective-permute-start | bytes 786440 | tf_op jit(solution)/shard_map/ppermute | solution.py:302
  219.6 7.2 %collective-permute-done.29 = bf16[8,66,1024]{2,0,1:T(8,128)(2,1)S(1)} collective-permute-done((bf16[8,66,1024]{2,0,1:T(8,128)(2,1)}, bf16[8,66,1024]{2,0,1:T(8,128)(2,1)S(1)}, u32[]{:S(2)}, u32[]{:S(2)}) %collective-permute-start.29) | collective-permute-done | bytes 1081376 | tf_op jit(solution)/shard_map/ppermute | solution.py:302
  232.6 19.3 %all-to-all-done.1.x_ref = bf16[16,128,1024]{2,1,0:T(8,128)(2,1)} async-done(((bf16[16,128,1024]{2,1,0:T(8,128)(2,1)}), bf16[16,128,1024]{2,1,0:T(8,128)(2,1)}, u32[]{:S(2)}, u32[]{:S(2)}) %all-to-all-start.1) | async-done | bytes 4194336 | tf_op jit(solution)/shard_map/all_to_all | solution.py:297
  251.9 3.7 %shard_map.135 = bf16[16,128,1024]{2,1,0:T(8,128)(2,1)} custom-call(bf16[16,128,1024]{2,1,0:T(8,128)(2,1)} %all-to-all-done.1.x_ref), custom_call_target="tpu_custom_call" | custom-call | flops 1 | bytes 1 | tf_op jit(solution)/shard_map/pallas_call | solution.py:71
  257.1 4.4 %collective-permute-done.28.refs_3_ = bf16[4,32,1024]{2,1,0:T(8,128)(2,1)S(1)} collective-permute-done((bf16[4,32,1024]{2,1,0:T(8,128)(2,1)S(1)}, bf16[4,32,1024]{2,1,0:T(8,128)(2,1)S(1)}, u32[]{:S(2)}, u32[]{:S(2)}) %collective-permute-start.28) | collective-permute-done | bytes 262176 | tf_op jit(solution)/shard_map/ppermute | solution.py:302
  (140 shorter events, 42.3 us)
Async XLA Ops:
  0.7 121.0 %all-to-all-start = ((bf16[16,128,1024]{2,1,0:T(8,128)(2,1)}), bf16[16,128,1024]{2,1,0:T(8,128)(2,1)}, u32[]{:S(2)}, u32[]{:S(2)}) async-start(bf16[16,128,1024]{2,1,0:T(8,128)(2,1)} %bitcast.153), calls=%async_computation | async-start | bytes 8388608 | tf_op jit(solution)/shard_map/all_to_all | solution.py:297
  9.0 2.0 collective-permute-start
  10.0 2.1 collective-permute-start.1
  19.1 1.3 collective-permute-start.2
  20.9 5.7 %collective-permute-start.3 = (f32[4,2,1024]{2,1,0:T(2,128)S(1)}, f32[4,2,1024]{2,1,0:T(2,128)S(1)}, u32[]{:S(2)}, u32[]{:S(2)}) collective-permute-start(f32[4,2,1024]{2,1,0:T(2,128)S(1)} %get-tuple-element.130), channel_id=1, source_target_pairs={{0,2},{2,0},{4,6},{6,4},{8,10},{10,8},{12,14},{14,12},{16,18},{18,... | collective-permute-start | bytes 98312 | tf_op jit(solution)/shard_map/ppermute | solution.py:302
  22.4 5.7 %collective-permute-start.4 = (f32[4,2,1024]{2,1,0:T(2,128)S(1)}, f32[4,2,1024]{2,1,0:T(2,128)S(1)}, u32[]{:S(2)}, u32[]{:S(2)}) collective-permute-start(f32[4,2,1024]{2,1,0:T(2,128)S(1)} %get-tuple-element.131), channel_id=1, source_target_pairs={{0,4},{2,6},{4,0},{6,2},{8,12},{10,14},{12,8},{14,10},{16,20},{18,... | collective-permute-start | bytes 98312 | tf_op jit(solution)/shard_map/ppermute | solution.py:302
  22.9 5.2 %collective-permute-start.5 = (f32[4,2,1024]{2,1,0:T(2,128)S(1)}, f32[4,2,1024]{2,1,0:T(2,128)S(1)}, u32[]{:S(2)}, u32[]{:S(2)}) collective-permute-start(f32[4,2,1024]{2,1,0:T(2,128)S(1)} %get-tuple-element.132), channel_id=1, source_target_pairs={{0,6},{2,4},{4,2},{6,0},{8,14},{10,12},{12,10},{14,8},{16,22},{18,... | collective-permute-start | bytes 98312 | tf_op jit(solution)/shard_map/ppermute | solution.py:302
  24.5 13.3 %collective-permute-start.9 = (bf16[4,32,1024]{2,1,0:T(8,128)(2,1)S(1)}, bf16[4,32,1024]{2,1,0:T(8,128)(2,1)S(1)}, u32[]{:S(2)}, u32[]{:S(2)}) collective-permute-start(bf16[4,32,1024]{2,1,0:T(8,128)(2,1)S(1)} %get-tuple-element.113), channel_id=1, source_target_pairs={{0,2},{2,0},{4,6},{6,4},{8,10},{10,8},{12,14},{14,12},{16,18},{18,... | collective-permute-start | bytes 786440 | tf_op jit(solution)/shard_map/ppermute | solution.py:302
  26.0 18.0 %collective-permute-start.10 = (bf16[4,32,1024]{2,1,0:T(8,128)(2,1)S(1)}, bf16[4,32,1024]{2,1,0:T(8,128)(2,1)S(1)}, u32[]{:S(2)}, u32[]{:S(2)}) collective-permute-start(bf16[4,32,1024]{2,1,0:T(8,128)(2,1)S(1)} %get-tuple-element.112), channel_id=1, source_target_pairs={{0,4},{2,6},{4,0},{6,2},{8,12},{10,14},{12,8},{14,10},{16,20},{18,... | collective-permute-start | bytes 786440 | tf_op jit(solution)/shard_map/ppermute | solution.py:302
  26.6 35.2 %collective-permute-start.11 = (bf16[4,32,1024]{2,1,0:T(8,128)(2,1)S(1)}, bf16[4,32,1024]{2,1,0:T(8,128)(2,1)S(1)}, u32[]{:S(2)}, u32[]{:S(2)}) collective-permute-start(bf16[4,32,1024]{2,1,0:T(8,128)(2,1)S(1)} %get-tuple-element.114), channel_id=1, source_target_pairs={{0,6},{2,4},{4,2},{6,0},{8,14},{10,12},{12,10},{14,8},{16,22},{18,... | collective-permute-start | bytes 786440 | tf_op jit(solution)/shard_map/ppermute | solution.py:302
  28.3 52.5 %collective-permute-start.6 = (f32[4,2,1024]{2,1,0:T(2,128)S(1)}, f32[4,2,1024]{2,1,0:T(2,128)S(1)}, u32[]{:S(2)}, u32[]{:S(2)}) collective-permute-start(f32[4,2,1024]{2,1,0:T(2,128)S(1)} %get-tuple-element.123), channel_id=1, source_target_pairs={{0,8},{2,10},{4,12},{6,14},{8,0},{10,2},{12,4},{14,6},{16,24},{18,... | collective-permute-start | bytes 98312 | tf_op jit(solution)/shard_map/ppermute | solution.py:302
  29.0 71.8 %collective-permute-start.7 = (f32[4,2,1024]{2,1,0:T(2,128)S(1)}, f32[4,2,1024]{2,1,0:T(2,128)S(1)}, u32[]{:S(2)}, u32[]{:S(2)}) collective-permute-start(f32[4,2,1024]{2,1,0:T(2,128)S(1)} %get-tuple-element.122), channel_id=1, source_target_pairs={{0,16},{2,18},{4,20},{6,22},{8,24},{10,26},{12,28},{14,30},{16,0},... | collective-permute-start | bytes 98312 | tf_op jit(solution)/shard_map/ppermute | solution.py:302
  37.9 67.4 %collective-permute-start.8 = (f32[4,2,1024]{2,1,0:T(2,128)S(1)}, f32[4,2,1024]{2,1,0:T(2,128)S(1)}, u32[]{:S(2)}, u32[]{:S(2)}) collective-permute-start(f32[4,2,1024]{2,1,0:T(2,128)S(1)} %get-tuple-element.121), channel_id=1, source_target_pairs={{0,24},{2,26},{4,28},{6,30},{8,16},{10,18},{12,20},{14,22},{16,8},... | collective-permute-start | bytes 98312 | tf_op jit(solution)/shard_map/ppermute | solution.py:302
  105.3 20.6 %collective-permute-start.15 = (bf16[4,32,1024]{2,1,0:T(8,128)(2,1)S(1)}, bf16[4,32,1024]{2,1,0:T(8,128)(2,1)S(1)}, u32[]{:S(2)}, u32[]{:S(2)}) collective-permute-start(bf16[4,32,1024]{2,1,0:T(8,128)(2,1)S(1)} %get-tuple-element.50), channel_id=1, source_target_pairs={{0,8},{2,10},{4,12},{6,14},{8,0},{10,2},{12,4},{14,6},{16,24},{18,... | collective-permute-start | bytes 786440 | tf_op jit(solution)/shard_map/ppermute | solution.py:302
  106.4 23.6 %collective-permute-start.16 = (bf16[4,32,1024]{2,1,0:T(8,128)(2,1)S(1)}, bf16[4,32,1024]{2,1,0:T(8,128)(2,1)S(1)}, u32[]{:S(2)}, u32[]{:S(2)}) collective-permute-start(bf16[4,32,1024]{2,1,0:T(8,128)(2,1)S(1)} %get-tuple-element.51), channel_id=1, source_target_pairs={{0,24},{2,26},{4,28},{6,30},{8,16},{10,18},{12,20},{14,22},{16,8},... | collective-permute-start | bytes 786440 | tf_op jit(solution)/shard_map/ppermute | solution.py:302
  106.4 27.8 %collective-permute-start.20 = (bf16[194,1024]{1,0:T(8,128)(2,1)S(1)}, bf16[194,1024]{1,0:T(8,128)(2,1)S(1)}, u32[]{:S(2)}, u32[]{:S(2)}) collective-permute-start(bf16[194,1024]{1,0:T(8,128)(2,1)S(1)} %pad_maximum_fusion.8), channel_id=1, source_target_pairs={{0,16},{2,18},{4,20},{6,22},{8,24},{10,26},{12,28},{14,30},{16,0},... | collective-permute-start | bytes 1191944 | tf_op jit(solution)/shard_map/ppermute | solution.py:302
  112.2 1.4 collective-permute-start.12
  114.3 3.7 %collective-permute-start.13 = (f32[16,32]{1,0:T(8,128)S(1)}, f32[16,32]{1,0:T(8,128)S(1)}, u32[]{:S(2)}, u32[]{:S(2)}) collective-permute-start(f32[16,32]{1,0:T(8,128)S(1)} %add.148), channel_id=1, source_target_pairs={{0,2},{2,0},{4,6},{6,4},{8,10},{10,8},{12,14},{14,12},{16,18},{18,... | collective-permute-start | bytes 6152 | tf_op jit(solution)/shard_map/ppermute | solution.py:302
  118.0 3.7 %collective-permute-start.14 = (f32[16,32]{1,0:T(8,128)S(1)}, f32[16,32]{1,0:T(8,128)S(1)}, u32[]{:S(2)}, u32[]{:S(2)}) collective-permute-start(f32[16,32]{1,0:T(8,128)S(1)} %add.149), channel_id=1, source_target_pairs={{0,4},{2,6},{4,0},{6,2},{8,12},{10,14},{12,8},{14,10},{16,20},{18,... | collective-permute-start | bytes 6152 | tf_op jit(solution)/shard_map/ppermute | solution.py:302
  130.0 4.2 %collective-permute-start.17 = (f32[16,32]{1,0:T(8,128)S(1)}, f32[16,32]{1,0:T(8,128)S(1)}, u32[]{:S(2)}, u32[]{:S(2)}) collective-permute-start(f32[16,32]{1,0:T(8,128)S(1)} %add.150.own_ref), channel_id=1, source_target_pairs={{0,8},{2,10},{4,12},{6,14},{8,0},{10,2},{12,4},{14,6},{16,24},{18,... | collective-permute-start | bytes 6152 | tf_op jit(solution)/shard_map/ppermute | solution.py:302
  130.0 4.7 %collective-permute-start.18 = (f32[16,32]{1,0:T(8,128)S(1)}, f32[16,32]{1,0:T(8,128)S(1)}, u32[]{:S(2)}, u32[]{:S(2)}) collective-permute-start(f32[16,32]{1,0:T(8,128)S(1)} %add.150.own_ref), channel_id=1, source_target_pairs={{0,16},{2,18},{4,20},{6,22},{8,24},{10,26},{12,28},{14,30},{16,0},... | collective-permute-start | bytes 6152 | tf_op jit(solution)/shard_map/ppermute | solution.py:302
  131.2 5.4 %collective-permute-start.19 = (f32[16,32]{1,0:T(8,128)S(1)}, f32[16,32]{1,0:T(8,128)S(1)}, u32[]{:S(2)}, u32[]{:S(2)}) collective-permute-start(f32[16,32]{1,0:T(8,128)S(1)} %add.150.own_ref), channel_id=1, source_target_pairs={{0,24},{2,26},{4,28},{6,30},{8,16},{10,18},{12,20},{14,22},{16,8},... | collective-permute-start | bytes 6152 | tf_op jit(solution)/shard_map/ppermute | solution.py:302
  136.6 7.5 %collective-permute-start.21 = (bf16[2,66,1024]{2,1,0:T(8,128)(2,1)S(1)}, bf16[2,66,1024]{2,1,0:T(8,128)(2,1)S(1)}, u32[]{:S(2)}, u32[]{:S(2)}) collective-permute-start(bf16[2,66,1024]{2,1,0:T(8,128)(2,1)S(1)} %pad_maximum_fusion.9), channel_id=1, source_target_pairs={{0,8},{2,10},{4,12},{6,14},{8,0},{10,2},{12,4},{14,6},{16,24},{18,... | collective-permute-start | bytes 811016 | tf_op jit(solution)/shard_map/ppermute | solution.py:302
  144.2 107.7 %all-to-all-start.1 = ((bf16[16,128,1024]{2,1,0:T(8,128)(2,1)}), bf16[16,128,1024]{2,1,0:T(8,128)(2,1)}, u32[]{:S(2)}, u32[]{:S(2)}) async-start(bf16[16,128,1024]{2,1,0:T(8,128)(2,1)} %get-tuple-element.74), calls=%async_computation.1 | async-start | bytes 8388608 | tf_op jit(solution)/shard_map/all_to_all | solution.py:297
  154.8 13.0 %collective-permute-start.22 = (bf16[4,32,1024]{2,1,0:T(8,128)(2,1)S(1)}, bf16[4,32,1024]{2,1,0:T(8,128)(2,1)S(1)}, u32[]{:S(2)}, u32[]{:S(2)}) collective-permute-start(bf16[4,32,1024]{2,1,0:T(8,128)(2,1)S(1)} %get-tuple-element.98), channel_id=1, source_target_pairs={{0,2},{2,0},{4,6},{6,4},{8,10},{10,8},{12,14},{14,12},{16,18},{18,... | collective-permute-start | bytes 786440 | tf_op jit(solution)/shard_map/ppermute | solution.py:302
  156.3 25.6 %collective-permute-start.23 = (bf16[4,32,1024]{2,1,0:T(8,128)(2,1)S(1)}, bf16[4,32,1024]{2,1,0:T(8,128)(2,1)S(1)}, u32[]{:S(2)}, u32[]{:S(2)}) collective-permute-start(bf16[4,32,1024]{2,1,0:T(8,128)(2,1)S(1)} %get-tuple-element.97), channel_id=1, source_target_pairs={{0,4},{2,6},{4,0},{6,2},{8,12},{10,14},{12,8},{14,10},{16,20},{18,... | collective-permute-start | bytes 786440 | tf_op jit(solution)/shard_map/ppermute | solution.py:302
  156.9 25.0 %collective-permute-start.24 = (bf16[4,32,1024]{2,1,0:T(8,128)(2,1)S(1)}, bf16[4,32,1024]{2,1,0:T(8,128)(2,1)S(1)}, u32[]{:S(2)}, u32[]{:S(2)}) collective-permute-start(bf16[4,32,1024]{2,1,0:T(8,128)(2,1)S(1)} %get-tuple-element.96), channel_id=1, source_target_pairs={{0,6},{2,4},{4,2},{6,0},{8,14},{10,12},{12,10},{14,8},{16,22},{18,... | collective-permute-start | bytes 786440 | tf_op jit(solution)/shard_map/ppermute | solution.py:302
  158.9 41.2 %collective-permute-start.25 = (bf16[4,66,1024]{2,0,1:T(4,128)(2,1)S(1)}, bf16[4,66,1024]{2,0,1:T(4,128)(2,1)S(1)}, u32[]{:S(2)}, u32[]{:S(2)}) collective-permute-start(bf16[4,66,1024]{2,0,1:T(4,128)(2,1)S(1)} %copy.30), channel_id=1, source_target_pairs={{0,4},{2,6},{4,0},{6,2},{8,12},{10,14},{12,8},{14,10},{16,20},{18,... | collective-permute-start | bytes 1622024 | tf_op jit(solution)/shard_map/ppermute | solution.py:302
  202.3 24.5 %collective-permute-start.29 = (bf16[8,66,1024]{2,0,1:T(8,128)(2,1)}, bf16[8,66,1024]{2,0,1:T(8,128)(2,1)S(1)}, u32[]{:S(2)}, u32[]{:S(2)}) collective-permute-start(bf16[8,66,1024]{2,0,1:T(8,128)(2,1)} %pad_maximum_fusion), channel_id=1, source_target_pairs={{0,2},{2,0},{4,6},{6,4},{8,10},{10,8},{12,14},{14,12},{16,18},{18,... | collective-permute-start | bytes 3244040 | tf_op jit(solution)/shard_map/ppermute | solution.py:302
  209.4 46.3 %collective-permute-start.26 = (bf16[4,32,1024]{2,1,0:T(8,128)(2,1)}, bf16[4,32,1024]{2,1,0:T(8,128)(2,1)S(1)}, u32[]{:S(2)}, u32[]{:S(2)}) collective-permute-start(bf16[4,32,1024]{2,1,0:T(8,128)(2,1)} %get-tuple-element.89), channel_id=1, source_target_pairs={{0,8},{2,10},{4,12},{6,14},{8,0},{10,2},{12,4},{14,6},{16,24},{18,... | collective-permute-start | bytes 786440 | tf_op jit(solution)/shard_map/ppermute | solution.py:302
  217.5 39.6 %collective-permute-start.27 = (bf16[4,32,1024]{2,1,0:T(8,128)(2,1)}, bf16[4,32,1024]{2,1,0:T(8,128)(2,1)S(1)}, u32[]{:S(2)}, u32[]{:S(2)}) collective-permute-start(bf16[4,32,1024]{2,1,0:T(8,128)(2,1)} %get-tuple-element.88), channel_id=1, source_target_pairs={{0,16},{2,18},{4,20},{6,22},{8,24},{10,26},{12,28},{14,30},{16,0},... | collective-permute-start | bytes 786440 | tf_op jit(solution)/shard_map/ppermute | solution.py:302
  217.9 43.5 %collective-permute-start.28 = (bf16[4,32,1024]{2,1,0:T(8,128)(2,1)S(1)}, bf16[4,32,1024]{2,1,0:T(8,128)(2,1)S(1)}, u32[]{:S(2)}, u32[]{:S(2)}) collective-permute-start(bf16[4,32,1024]{2,1,0:T(8,128)(2,1)S(1)} %get-tuple-element.87), channel_id=1, source_target_pairs={{0,24},{2,26},{4,28},{6,30},{8,16},{10,18},{12,20},{14,22},{16,8},... | collective-permute-start | bytes 786440 | tf_op jit(solution)/shard_map/ppermute | solution.py:302
  (18 other events, 106.9 us)

commit v8 on v7

--- a/solution.py
+++ b/solution.py
@@ -368,7 +368,8 @@
         small = jnp.concatenate([third_w.T, b_first, b_second], axis=0)
         slabs = [pick(slabs, plane ^ i, 1) for i in range(planes)]
         joined = jnp.concatenate([slabs[2].reshape(-1, width), small], axis=0)
-        parts, slabs, joined = lax.optimization_barrier((parts, slabs, joined))
+        center = blocked(center_kernel, got_second)
+        parts, slabs, joined, center = lax.optimization_barrier((parts, slabs, joined, center))
         both = jnp.concatenate(by_plane(parts), axis=0)
         joined = across(joined, 2)
         size = joined.shape[0] - small.shape[0]
@@ -388,8 +389,7 @@
         sums = sums + swap(sums, "pair", 1)
         sums = sums + swap(sums, "member", 1)
         sums = sums + swap(sums, "member", 2)
-        center = blocked(center_kernel, got_second)
-        sums, parts[1], parts[3], center = lax.optimization_barrier((sums, parts[1], parts[3], center))
+        sums, parts[1], parts[3] = lax.optimization_barrier((sums, parts[1], parts[3]))
         far = [across(sums, i) for i in range(1, planes)]
         far, held[1], parts = lax.optimization_barrier((far, held[1], parts))
         held.append(swap(jnp.concatenate(held, axis=0), "member", 4))

time: 263 us -> 270 us (1.027)
  starting transfers between devices: 57.1 us -> 60.4 us
  waiting for transfers between devices: 155 us -> 158 us
    all_to_all x2, waiting for transfers between devices: 19.3 us -> 61.5 us  [exchange(): return lax.all_to_all(x, 'member', split_axis=0, concat_axis=0, tiled=True)]
    ppermute x30, waiting for transfers between devices: 136 us -> 96.5 us  [swap(): return lax.ppermute(x, axis, [(i, i ^ bit) for i in range(count)])]
    ppermute x30, starting transfers between devices: 44.7 us -> 47.5 us  [swap(): return lax.ppermute(x, axis, [(i, i ^ bit) for i in range(count)])]
  transfers between devices with their start and end apart: 32 -> 32, of which waited for: 22 -> 20; matrix products, arithmetic and copies ran while one was open for 8% -> 8% of each run, Pallas kernels for 10% -> 9%
where the time goes in v8:
time: 270 us; the launch traced here: 269 us
  waiting for transfers between devices  158 us (59%)
  starting transfers between devices  60.4 us (22%)
  Pallas kernels  26.3 us (10%)
  other arithmetic  12 us (4%)
  local copies, waits for them, and re-layouts  10.9 us (4%)
    ppermute x30, waiting for transfers between devices, swap(): return lax.ppermute(x, axis, [(i, i ^ bit) for i in range(count)])  96.5 us
    all_to_all x2, waiting for transfers between devices, exchange(): return lax.all_to_all(x, 'member', split_axis=0, concat_axis=0, tiled=True)  61.5 us
    ppermute x30, starting transfers between devices, swap(): return lax.ppermute(x, axis, [(i, i ^ bit) for i in range(count)])  47.5 us
    all_to_all x2, starting transfers between devices, exchange(): return lax.all_to_all(x, 'member', split_axis=0, concat_axis=0, tiled=True)  12.9 us
    pallas_call x3, Pallas kernels, blocked(): pl.pallas_call(kernel, grid=(total // rows,), in_specs=[pl.BlockSpec(w.sh...  10.9 us
    pallas_call x1, Pallas kernels, solve(): pl.pallas_call(solve_kernel, in_specs=[vmem] * len(sums) + [anywhere], ou...  6.04 us
  transfers between devices with their start and end apart: 32, of which 20 were waited for; matrix products, arithmetic and copies ran while one was open for 8% of the time, Pallas kernels for 9%

profile of v8, /device:TPU:12, one launch (start us, length us, event | category | flops | bytes accessed | tf_op | source)
XLA Modules:
  0.0 269.0 jit_solution(8727679249046407193)
XLA Ops:
  0.7 7.3 %all-to-all-start = ((bf16[16,128,1024]{2,1,0:T(8,128)(2,1)}), bf16[16,128,1024]{2,1,0:T(8,128)(2,1)}, u32[]{:S(2)}, u32[]{:S(2)}) async-start(bf16[16,128,1024]{2,1,0:T(8,128)(2,1)} %bitcast.153), calls=%async_computation | async-start | bytes 8388608 | tf_op jit(solution)/shard_map/all_to_all | solution.py:297
  12.1 2.2 copy-done
  14.3 4.8 %shard_map.130 = f32[64,512]{1,0:T(8,128)S(1)} custom-call(s32[1]{0:T(128)} %bitcast.1.side_ref, bf16[512,512]{1,0:T(8,128)(2,1)S(1)} %shard_map.128.refs_0_, bf16[512,512]{1,0:T(8,128)(2,1)S(1)} %shard_map.129.refs_1_, bf16[512,512]{1,0:T(8,128)(2,1)S(1)} %collective-permute-done.refs_2_, bf16[512,512]{1,0:T(8,128)(2,1)S(1)} %collective-permute-done.1.refs_3_, ...), custom_call_target="tpu_custom_call" | custom-call | flops 1 | bytes 1 | tf_op jit(solution)/shard_map/pallas_call | solution.py:274
  24.5 1.5 collective-permute-start.9
  29.0 8.9 %collective-permute-start.7 = (f32[4,2,1024]{2,1,0:T(2,128)S(1)}, f32[4,2,1024]{2,1,0:T(2,128)S(1)}, u32[]{:S(2)}, u32[]{:S(2)}) collective-permute-start(f32[4,2,1024]{2,1,0:T(2,128)S(1)} %get-tuple-element.122), channel_id=1, source_target_pairs={{0,16},{2,18},{4,20},{6,22},{8,24},{10,26},{12,28},{14,30},{16,0},... | collective-permute-start | bytes 98312 | tf_op jit(solution)/shard_map/ppermute | solution.py:302
  38.3 5.7 %collective-permute-done.10 = bf16[4,32,1024]{2,1,0:T(8,128)(2,1)S(1)} collective-permute-done((bf16[4,32,1024]{2,1,0:T(8,128)(2,1)S(1)}, bf16[4,32,1024]{2,1,0:T(8,128)(2,1)S(1)}, u32[]{:S(2)}, u32[]{:S(2)}) %collective-permute-start.10) | collective-permute-done | bytes 262176 | tf_op jit(solution)/shard_map/ppermute | solution.py:302
  44.1 17.7 %collective-permute-done.11 = bf16[4,32,1024]{2,1,0:T(8,128)(2,1)S(1)} collective-permute-done((bf16[4,32,1024]{2,1,0:T(8,128)(2,1)S(1)}, bf16[4,32,1024]{2,1,0:T(8,128)(2,1)S(1)}, u32[]{:S(2)}, u32[]{:S(2)}) %collective-permute-start.11) | collective-permute-done | bytes 262176 | tf_op jit(solution)/shard_map/ppermute | solution.py:302
  62.3 41.9 %all-to-all-done.x_ref = bf16[16,128,1024]{2,1,0:T(8,128)(2,1)} async-done(((bf16[16,128,1024]{2,1,0:T(8,128)(2,1)}), bf16[16,128,1024]{2,1,0:T(8,128)(2,1)}, u32[]{:S(2)}, u32[]{:S(2)}) %all-to-all-start) | async-done | bytes 4194336 | tf_op jit(solution)/shard_map/all_to_all | solution.py:297
  104.2 4.2 %shard_map.131.x_ref = bf16[16,128,1024]{2,1,0:T(8,128)(2,1)} custom-call(bf16[16,128,1024]{2,1,0:T(8,128)(2,1)} %all-to-all-done.x_ref), custom_call_target="tpu_custom_call" | custom-call | flops 1 | bytes 1 | tf_op jit(solution)/shard_map/pallas_call | solution.py:71
  108.6 4.3 %collective-permute-start.16 = (bf16[4,32,1024]{2,1,0:T(8,128)(2,1)S(1)}, bf16[4,32,1024]{2,1,0:T(8,128)(2,1)S(1)}, u32[]{:S(2)}, u32[]{:S(2)}) collective-permute-start(bf16[4,32,1024]{2,1,0:T(8,128)(2,1)S(1)} %get-tuple-element.51), channel_id=1, source_target_pairs={{0,24},{2,26},{4,28},{6,30},{8,16},{10,18},{12,20},{14,22},{16,8},... | collective-permute-start | bytes 786440 | tf_op jit(solution)/shard_map/ppermute | solution.py:302
  113.8 1.8 shard_map.132
  117.6 1.9 collective-permute-start.13
  119.5 1.8 collective-permute-done.13
  121.3 3.6 %collective-permute-done.14 = f32[16,32]{1,0:T(8,128)S(1)} collective-permute-done((f32[16,32]{1,0:T(8,128)S(1)}, f32[16,32]{1,0:T(8,128)S(1)}, u32[]{:S(2)}, u32[]{:S(2)}) %collective-permute-start.14) | collective-permute-done | bytes 2080 | tf_op jit(solution)/shard_map/ppermute | solution.py:302
  124.9 9.4 %collective-permute-done.16 = bf16[4,32,1024]{2,1,0:T(8,128)(2,1)S(1)} collective-permute-done((bf16[4,32,1024]{2,1,0:T(8,128)(2,1)S(1)}, bf16[4,32,1024]{2,1,0:T(8,128)(2,1)S(1)}, u32[]{:S(2)}, u32[]{:S(2)}) %collective-permute-start.16) | collective-permute-done | bytes 262176 | tf_op jit(solution)/shard_map/ppermute | solution.py:302
  134.4 2.5 collective-permute-start.18
  137.9 2.1 collective-permute-done.20
  140.8 1.6 collective-permute-start.21
  142.4 6.0 %shard_map.133 = (bf16[16,16]{1,0:T(8,128)(2,1)}, bf16[256,256]{1,0:T(8,128)(2,1)}, bf16[16,128,1024]{2,1,0:T(8,128)(2,1)}) custom-call(f32[16,32]{1,0:T(8,128)} %copy-done.10, f32[16,32]{1,0:T(8,128)} %copy-done.13, f32[16,32]{1,0:T(8,128)} %copy-done.14, f32[16,32]{1,0:T(8,128)} %copy-done.15, bf16[16,128,1024]{2,1,0:T(8,128)(2,1)} %shard_map.131.x_ref), custom_call_target="tpu_custom_call" | custom-call | flops 1 | bytes 1 | tf_op jit(solution)/shard_map/pallas_call | solution.py:152
  148.5 5.5 %all-to-all-start.1 = ((bf16[16,128,1024]{2,1,0:T(8,128)(2,1)}), bf16[16,128,1024]{2,1,0:T(8,128)(2,1)}, u32[]{:S(2)}, u32[]{:S(2)}) async-start(bf16[16,128,1024]{2,1,0:T(8,128)(2,1)} %get-tuple-element.74), calls=%async_computation.1 | async-start | bytes 8388608 | tf_op jit(solution)/shard_map/all_to_all | solution.py:297
  155.4 2.9 %shard_map.134 = bf16[16,32,1024]{2,1,0:T(8,128)(2,1)} custom-call(bf16[256,256]{1,0:T(8,128)(2,1)} %get-tuple-element.61.spread_ref, bf16[16,32,1024]{2,1,0:T(8,128)(2,1)} %bitcast.172), custom_call_target="tpu_custom_call" | custom-call | flops 1 | bytes 1 | tf_op jit(solution)/shard_map/pallas_call | solution.py:71
  165.0 8.4 %collective-permute-done.22 = bf16[4,32,1024]{2,1,0:T(8,128)(2,1)S(1)} collective-permute-done((bf16[4,32,1024]{2,1,0:T(8,128)(2,1)S(1)}, bf16[4,32,1024]{2,1,0:T(8,128)(2,1)S(1)}, u32[]{:S(2)}, u32[]{:S(2)}) %collective-permute-start.22) | collective-permute-done | bytes 262176 | tf_op jit(solution)/shard_map/ppermute | solution.py:302
  173.4 14.2 %collective-permute-done.23 = bf16[4,32,1024]{2,1,0:T(8,128)(2,1)S(1)} collective-permute-done((bf16[4,32,1024]{2,1,0:T(8,128)(2,1)S(1)}, bf16[4,32,1024]{2,1,0:T(8,128)(2,1)S(1)}, u32[]{:S(2)}, u32[]{:S(2)}) %collective-permute-start.23) | collective-permute-done | bytes 262176 | tf_op jit(solution)/shard_map/ppermute | solution.py:302
  188.9 15.8 %collective-permute-done.25 = bf16[4,66,1024]{2,0,1:T(4,128)(2,1)S(1)} collective-permute-done((bf16[4,66,1024]{2,0,1:T(4,128)(2,1)S(1)}, bf16[4,66,1024]{2,0,1:T(4,128)(2,1)S(1)}, u32[]{:S(2)}, u32[]{:S(2)}) %collective-permute-start.25) | collective-permute-done | bytes 540704 | tf_op jit(solution)/shard_map/ppermute | solution.py:302
  204.7 2.2 pad_maximum_fusion
  206.9 3.1 %collective-permute-start.29 = (bf16[8,66,1024]{2,0,1:T(8,128)(2,1)}, bf16[8,66,1024]{2,0,1:T(8,128)(2,1)S(1)}, u32[]{:S(2)}, u32[]{:S(2)}) collective-permute-start(bf16[8,66,1024]{2,0,1:T(8,128)(2,1)} %pad_maximum_fusion), channel_id=1, source_target_pairs={{0,2},{2,0},{4,6},{6,4},{8,10},{10,8},{12,14},{14,12},{16,18},{18,... | collective-permute-start | bytes 3244040 | tf_op jit(solution)/shard_map/ppermute | solution.py:302
  211.6 2.1 dynamic-slice_bitcast_fusion
  213.7 9.1 %collective-permute-start.26 = (bf16[4,32,1024]{2,1,0:T(8,128)(2,1)}, bf16[4,32,1024]{2,1,0:T(8,128)(2,1)S(1)}, u32[]{:S(2)}, u32[]{:S(2)}) collective-permute-start(bf16[4,32,1024]{2,1,0:T(8,128)(2,1)} %get-tuple-element.89), channel_id=1, source_target_pairs={{0,8},{2,10},{4,12},{6,14},{8,0},{10,2},{12,4},{14,6},{16,24},{18,... | collective-permute-start | bytes 786440 | tf_op jit(solution)/shard_map/ppermute | solution.py:302
  224.9 7.0 %collective-permute-done.29 = bf16[8,66,1024]{2,0,1:T(8,128)(2,1)S(1)} collective-permute-done((bf16[8,66,1024]{2,0,1:T(8,128)(2,1)}, bf16[8,66,1024]{2,0,1:T(8,128)(2,1)S(1)}, u32[]{:S(2)}, u32[]{:S(2)}) %collective-permute-start.29) | collective-permute-done | bytes 1081376 | tf_op jit(solution)/shard_map/ppermute | solution.py:302
  237.7 19.5 %all-to-all-done.1.x_ref = bf16[16,128,1024]{2,1,0:T(8,128)(2,1)} async-done(((bf16[16,128,1024]{2,1,0:T(8,128)(2,1)}), bf16[16,128,1024]{2,1,0:T(8,128)(2,1)}, u32[]{:S(2)}, u32[]{:S(2)}) %all-to-all-start.1) | async-done | bytes 4194336 | tf_op jit(solution)/shard_map/all_to_all | solution.py:297
  257.3 3.7 %shard_map.135 = bf16[16,128,1024]{2,1,0:T(8,128)(2,1)} custom-call(bf16[16,128,1024]{2,1,0:T(8,128)(2,1)} %all-to-all-done.1.x_ref), custom_call_target="tpu_custom_call" | custom-call | flops 1 | bytes 1 | tf_op jit(solution)/shard_map/pallas_call | solution.py:71
  262.5 5.3 %collective-permute-done.28.refs_3_ = bf16[4,32,1024]{2,1,0:T(8,128)(2,1)S(1)} collective-permute-done((bf16[4,32,1024]{2,1,0:T(8,128)(2,1)S(1)}, bf16[4,32,1024]{2,1,0:T(8,128)(2,1)S(1)}, u32[]{:S(2)}, u32[]{:S(2)}) %collective-permute-start.28) | collective-permute-done | bytes 262176 | tf_op jit(solution)/shard_map/ppermute | solution.py:302
  (140 shorter events, 39.4 us)
Async XLA Ops:
  0.7 103.6 %all-to-all-start = ((bf16[16,128,1024]{2,1,0:T(8,128)(2,1)}), bf16[16,128,1024]{2,1,0:T(8,128)(2,1)}, u32[]{:S(2)}, u32[]{:S(2)}) async-start(bf16[16,128,1024]{2,1,0:T(8,128)(2,1)} %bitcast.153), calls=%async_computation | async-start | bytes 8388608 | tf_op jit(solution)/shard_map/all_to_all | solution.py:297
  9.0 2.0 collective-permute-start
  10.0 2.1 collective-permute-start.1
  19.1 1.3 collective-permute-start.2
  20.9 5.7 %collective-permute-start.3 = (f32[4,2,1024]{2,1,0:T(2,128)S(1)}, f32[4,2,1024]{2,1,0:T(2,128)S(1)}, u32[]{:S(2)}, u32[]{:S(2)}) collective-permute-start(f32[4,2,1024]{2,1,0:T(2,128)S(1)} %get-tuple-element.130), channel_id=1, source_target_pairs={{0,2},{2,0},{4,6},{6,4},{8,10},{10,8},{12,14},{14,12},{16,18},{18,... | collective-permute-start | bytes 98312 | tf_op jit(solution)/shard_map/ppermute | solution.py:302
  22.4 5.7 %collective-permute-start.4 = (f32[4,2,1024]{2,1,0:T(2,128)S(1)}, f32[4,2,1024]{2,1,0:T(2,128)S(1)}, u32[]{:S(2)}, u32[]{:S(2)}) collective-permute-start(f32[4,2,1024]{2,1,0:T(2,128)S(1)} %get-tuple-element.131), channel_id=1, source_target_pairs={{0,4},{2,6},{4,0},{6,2},{8,12},{10,14},{12,8},{14,10},{16,20},{18,... | collective-permute-start | bytes 98312 | tf_op jit(solution)/shard_map/ppermute | solution.py:302
  22.9 5.2 %collective-permute-start.5 = (f32[4,2,1024]{2,1,0:T(2,128)S(1)}, f32[4,2,1024]{2,1,0:T(2,128)S(1)}, u32[]{:S(2)}, u32[]{:S(2)}) collective-permute-start(f32[4,2,1024]{2,1,0:T(2,128)S(1)} %get-tuple-element.132), channel_id=1, source_target_pairs={{0,6},{2,4},{4,2},{6,0},{8,14},{10,12},{12,10},{14,8},{16,22},{18,... | collective-permute-start | bytes 98312 | tf_op jit(solution)/shard_map/ppermute | solution.py:302
  24.5 13.3 %collective-permute-start.9 = (bf16[4,32,1024]{2,1,0:T(8,128)(2,1)S(1)}, bf16[4,32,1024]{2,1,0:T(8,128)(2,1)S(1)}, u32[]{:S(2)}, u32[]{:S(2)}) collective-permute-start(bf16[4,32,1024]{2,1,0:T(8,128)(2,1)S(1)} %get-tuple-element.113), channel_id=1, source_target_pairs={{0,2},{2,0},{4,6},{6,4},{8,10},{10,8},{12,14},{14,12},{16,18},{18,... | collective-permute-start | bytes 786440 | tf_op jit(solution)/shard_map/ppermute | solution.py:302
  26.0 18.0 %collective-permute-start.10 = (bf16[4,32,1024]{2,1,0:T(8,128)(2,1)S(1)}, bf16[4,32,1024]{2,1,0:T(8,128)(2,1)S(1)}, u32[]{:S(2)}, u32[]{:S(2)}) collective-permute-start(bf16[4,32,1024]{2,1,0:T(8,128)(2,1)S(1)} %get-tuple-element.112), channel_id=1, source_target_pairs={{0,4},{2,6},{4,0},{6,2},{8,12},{10,14},{12,8},{14,10},{16,20},{18,... | collective-permute-start | bytes 786440 | tf_op jit(solution)/shard_map/ppermute | solution.py:302
  26.6 35.2 %collective-permute-start.11 = (bf16[4,32,1024]{2,1,0:T(8,128)(2,1)S(1)}, bf16[4,32,1024]{2,1,0:T(8,128)(2,1)S(1)}, u32[]{:S(2)}, u32[]{:S(2)}) collective-permute-start(bf16[4,32,1024]{2,1,0:T(8,128)(2,1)S(1)} %get-tuple-element.114), channel_id=1, source_target_pairs={{0,6},{2,4},{4,2},{6,0},{8,14},{10,12},{12,10},{14,8},{16,22},{18,... | collective-permute-start | bytes 786440 | tf_op jit(solution)/shard_map/ppermute | solution.py:302
  28.3 80.2 %collective-permute-start.6 = (f32[4,2,1024]{2,1,0:T(2,128)S(1)}, f32[4,2,1024]{2,1,0:T(2,128)S(1)}, u32[]{:S(2)}, u32[]{:S(2)}) collective-permute-start(f32[4,2,1024]{2,1,0:T(2,128)S(1)} %get-tuple-element.123), channel_id=1, source_target_pairs={{0,8},{2,10},{4,12},{6,14},{8,0},{10,2},{12,4},{14,6},{16,24},{18,... | collective-permute-start | bytes 98312 | tf_op jit(solution)/shard_map/ppermute | solution.py:302
  29.0 79.5 %collective-permute-start.7 = (f32[4,2,1024]{2,1,0:T(2,128)S(1)}, f32[4,2,1024]{2,1,0:T(2,128)S(1)}, u32[]{:S(2)}, u32[]{:S(2)}) collective-permute-start(f32[4,2,1024]{2,1,0:T(2,128)S(1)} %get-tuple-element.122), channel_id=1, source_target_pairs={{0,16},{2,18},{4,20},{6,22},{8,24},{10,26},{12,28},{14,30},{16,0},... | collective-permute-start | bytes 98312 | tf_op jit(solution)/shard_map/ppermute | solution.py:302
  37.9 70.6 %collective-permute-start.8 = (f32[4,2,1024]{2,1,0:T(2,128)S(1)}, f32[4,2,1024]{2,1,0:T(2,128)S(1)}, u32[]{:S(2)}, u32[]{:S(2)}) collective-permute-start(f32[4,2,1024]{2,1,0:T(2,128)S(1)} %get-tuple-element.121), channel_id=1, source_target_pairs={{0,24},{2,26},{4,28},{6,30},{8,16},{10,18},{12,20},{14,22},{16,8},... | collective-permute-start | bytes 98312 | tf_op jit(solution)/shard_map/ppermute | solution.py:302
  108.5 16.4 %collective-permute-start.15 = (bf16[4,32,1024]{2,1,0:T(8,128)(2,1)S(1)}, bf16[4,32,1024]{2,1,0:T(8,128)(2,1)S(1)}, u32[]{:S(2)}, u32[]{:S(2)}) collective-permute-start(bf16[4,32,1024]{2,1,0:T(8,128)(2,1)S(1)} %get-tuple-element.50), channel_id=1, source_target_pairs={{0,8},{2,10},{4,12},{6,14},{8,0},{10,2},{12,4},{14,6},{16,24},{18,... | collective-permute-start | bytes 786440 | tf_op jit(solution)/shard_map/ppermute | solution.py:302
  108.6 25.8 %collective-permute-start.16 = (bf16[4,32,1024]{2,1,0:T(8,128)(2,1)S(1)}, bf16[4,32,1024]{2,1,0:T(8,128)(2,1)S(1)}, u32[]{:S(2)}, u32[]{:S(2)}) collective-permute-start(bf16[4,32,1024]{2,1,0:T(8,128)(2,1)S(1)} %get-tuple-element.51), channel_id=1, source_target_pairs={{0,24},{2,26},{4,28},{6,30},{8,16},{10,18},{12,20},{14,22},{16,8},... | collective-permute-start | bytes 786440 | tf_op jit(solution)/shard_map/ppermute | solution.py:302
  112.8 27.2 %collective-permute-start.20 = (bf16[194,1024]{1,0:T(8,128)(2,1)S(1)}, bf16[194,1024]{1,0:T(8,128)(2,1)S(1)}, u32[]{:S(2)}, u32[]{:S(2)}) collective-permute-start(bf16[194,1024]{1,0:T(8,128)(2,1)S(1)} %pad_maximum_fusion.8), channel_id=1, source_target_pairs={{0,16},{2,18},{4,20},{6,22},{8,24},{10,26},{12,28},{14,30},{16,0},... | collective-permute-start | bytes 1191944 | tf_op jit(solution)/shard_map/ppermute | solution.py:302
  115.5 1.4 collective-permute-start.12
  117.6 3.7 %collective-permute-start.13 = (f32[16,32]{1,0:T(8,128)S(1)}, f32[16,32]{1,0:T(8,128)S(1)}, u32[]{:S(2)}, u32[]{:S(2)}) collective-permute-start(f32[16,32]{1,0:T(8,128)S(1)} %add.148), channel_id=1, source_target_pairs={{0,2},{2,0},{4,6},{6,4},{8,10},{10,8},{12,14},{14,12},{16,18},{18,... | collective-permute-start | bytes 6152 | tf_op jit(solution)/shard_map/ppermute | solution.py:302
  121.3 3.7 %collective-permute-start.14 = (f32[16,32]{1,0:T(8,128)S(1)}, f32[16,32]{1,0:T(8,128)S(1)}, u32[]{:S(2)}, u32[]{:S(2)}) collective-permute-start(f32[16,32]{1,0:T(8,128)S(1)} %add.149), channel_id=1, source_target_pairs={{0,4},{2,6},{4,0},{6,2},{8,12},{10,14},{12,8},{14,10},{16,20},{18,... | collective-permute-start | bytes 6152 | tf_op jit(solution)/shard_map/ppermute | solution.py:302
  134.4 5.6 %collective-permute-start.17 = (f32[16,32]{1,0:T(8,128)S(1)}, f32[16,32]{1,0:T(8,128)S(1)}, u32[]{:S(2)}, u32[]{:S(2)}) collective-permute-start(f32[16,32]{1,0:T(8,128)S(1)} %add.150.own_ref), channel_id=1, source_target_pairs={{0,8},{2,10},{4,12},{6,14},{8,0},{10,2},{12,4},{14,6},{16,24},{18,... | collective-permute-start | bytes 6152 | tf_op jit(solution)/shard_map/ppermute | solution.py:302
  134.4 5.7 %collective-permute-start.18 = (f32[16,32]{1,0:T(8,128)S(1)}, f32[16,32]{1,0:T(8,128)S(1)}, u32[]{:S(2)}, u32[]{:S(2)}) collective-permute-start(f32[16,32]{1,0:T(8,128)S(1)} %add.150.own_ref), channel_id=1, source_target_pairs={{0,16},{2,18},{4,20},{6,22},{8,24},{10,26},{12,28},{14,30},{16,0},... | collective-permute-start | bytes 6152 | tf_op jit(solution)/shard_map/ppermute | solution.py:302
  136.9 3.9 %collective-permute-start.19 = (f32[16,32]{1,0:T(8,128)S(1)}, f32[16,32]{1,0:T(8,128)S(1)}, u32[]{:S(2)}, u32[]{:S(2)}) collective-permute-start(f32[16,32]{1,0:T(8,128)S(1)} %add.150.own_ref), channel_id=1, source_target_pairs={{0,24},{2,26},{4,28},{6,30},{8,16},{10,18},{12,20},{14,22},{16,8},... | collective-permute-start | bytes 6152 | tf_op jit(solution)/shard_map/ppermute | solution.py:302
  140.8 7.7 %collective-permute-start.21 = (bf16[2,66,1024]{2,1,0:T(8,128)(2,1)S(1)}, bf16[2,66,1024]{2,1,0:T(8,128)(2,1)S(1)}, u32[]{:S(2)}, u32[]{:S(2)}) collective-permute-start(bf16[2,66,1024]{2,1,0:T(8,128)(2,1)S(1)} %pad_maximum_fusion.9), channel_id=1, source_target_pairs={{0,8},{2,10},{4,12},{6,14},{8,0},{10,2},{12,4},{14,6},{16,24},{18,... | collective-permute-start | bytes 811016 | tf_op jit(solution)/shard_map/ppermute | solution.py:302
  148.5 108.8 %all-to-all-start.1 = ((bf16[16,128,1024]{2,1,0:T(8,128)(2,1)}), bf16[16,128,1024]{2,1,0:T(8,128)(2,1)}, u32[]{:S(2)}, u32[]{:S(2)}) async-start(bf16[16,128,1024]{2,1,0:T(8,128)(2,1)} %get-tuple-element.74), calls=%async_computation.1 | async-start | bytes 8388608 | tf_op jit(solution)/shard_map/all_to_all | solution.py:297
  159.6 13.8 %collective-permute-start.22 = (bf16[4,32,1024]{2,1,0:T(8,128)(2,1)S(1)}, bf16[4,32,1024]{2,1,0:T(8,128)(2,1)S(1)}, u32[]{:S(2)}, u32[]{:S(2)}) collective-permute-start(bf16[4,32,1024]{2,1,0:T(8,128)(2,1)S(1)} %get-tuple-element.98), channel_id=1, source_target_pairs={{0,2},{2,0},{4,6},{6,4},{8,10},{10,8},{12,14},{14,12},{16,18},{18,... | collective-permute-start | bytes 786440 | tf_op jit(solution)/shard_map/ppermute | solution.py:302
  161.1 26.4 %collective-permute-start.23 = (bf16[4,32,1024]{2,1,0:T(8,128)(2,1)S(1)}, bf16[4,32,1024]{2,1,0:T(8,128)(2,1)S(1)}, u32[]{:S(2)}, u32[]{:S(2)}) collective-permute-start(bf16[4,32,1024]{2,1,0:T(8,128)(2,1)S(1)} %get-tuple-element.97), channel_id=1, source_target_pairs={{0,4},{2,6},{4,0},{6,2},{8,12},{10,14},{12,8},{14,10},{16,20},{18,... | collective-permute-start | bytes 786440 | tf_op jit(solution)/shard_map/ppermute | solution.py:302
  161.7 25.8 %collective-permute-start.24 = (bf16[4,32,1024]{2,1,0:T(8,128)(2,1)S(1)}, bf16[4,32,1024]{2,1,0:T(8,128)(2,1)S(1)}, u32[]{:S(2)}, u32[]{:S(2)}) collective-permute-start(bf16[4,32,1024]{2,1,0:T(8,128)(2,1)S(1)} %get-tuple-element.96), channel_id=1, source_target_pairs={{0,6},{2,4},{4,2},{6,0},{8,14},{10,12},{12,10},{14,8},{16,22},{18,... | collective-permute-start | bytes 786440 | tf_op jit(solution)/shard_map/ppermute | solution.py:302
  163.7 41.1 %collective-permute-start.25 = (bf16[4,66,1024]{2,0,1:T(4,128)(2,1)S(1)}, bf16[4,66,1024]{2,0,1:T(4,128)(2,1)S(1)}, u32[]{:S(2)}, u32[]{:S(2)}) collective-permute-start(bf16[4,66,1024]{2,0,1:T(4,128)(2,1)S(1)} %copy.30), channel_id=1, source_target_pairs={{0,4},{2,6},{4,0},{6,2},{8,12},{10,14},{12,8},{14,10},{16,20},{18,... | collective-permute-start | bytes 1622024 | tf_op jit(solution)/shard_map/ppermute | solution.py:302
  206.9 25.0 %collective-permute-start.29 = (bf16[8,66,1024]{2,0,1:T(8,128)(2,1)}, bf16[8,66,1024]{2,0,1:T(8,128)(2,1)S(1)}, u32[]{:S(2)}, u32[]{:S(2)}) collective-permute-start(bf16[8,66,1024]{2,0,1:T(8,128)(2,1)} %pad_maximum_fusion), channel_id=1, source_target_pairs={{0,2},{2,0},{4,6},{6,4},{8,10},{10,8},{12,14},{14,12},{16,18},{18,... | collective-permute-start | bytes 3244040 | tf_op jit(solution)/shard_map/ppermute | solution.py:302
  213.7 47.3 %collective-permute-start.26 = (bf16[4,32,1024]{2,1,0:T(8,128)(2,1)}, bf16[4,32,1024]{2,1,0:T(8,128)(2,1)S(1)}, u32[]{:S(2)}, u32[]{:S(2)}) collective-permute-start(bf16[4,32,1024]{2,1,0:T(8,128)(2,1)} %get-tuple-element.89), channel_id=1, source_target_pairs={{0,8},{2,10},{4,12},{6,14},{8,0},{10,2},{12,4},{14,6},{16,24},{18,... | collective-permute-start | bytes 786440 | tf_op jit(solution)/shard_map/ppermute | solution.py:302
  222.8 39.8 %collective-permute-start.27 = (bf16[4,32,1024]{2,1,0:T(8,128)(2,1)}, bf16[4,32,1024]{2,1,0:T(8,128)(2,1)S(1)}, u32[]{:S(2)}, u32[]{:S(2)}) collective-permute-start(bf16[4,32,1024]{2,1,0:T(8,128)(2,1)} %get-tuple-element.88), channel_id=1, source_target_pairs={{0,16},{2,18},{4,20},{6,22},{8,24},{10,26},{12,28},{14,30},{16,0},... | collective-permute-start | bytes 786440 | tf_op jit(solution)/shard_map/ppermute | solution.py:302
  223.6 44.3 %collective-permute-start.28 = (bf16[4,32,1024]{2,1,0:T(8,128)(2,1)S(1)}, bf16[4,32,1024]{2,1,0:T(8,128)(2,1)S(1)}, u32[]{:S(2)}, u32[]{:S(2)}) collective-permute-start(bf16[4,32,1024]{2,1,0:T(8,128)(2,1)S(1)} %get-tuple-element.87), channel_id=1, source_target_pairs={{0,24},{2,26},{4,28},{6,30},{8,16},{10,18},{12,20},{14,22},{16,8},... | collective-permute-start | bytes 786440 | tf_op jit(solution)/shard_map/ppermute | solution.py:302
  (18 other events, 110.1 us)
